TPU v7x, 32 devices: a whole 2x2x4 slice. The times are simulated.
32 devices in a mesh: grp: 2 (over y), lon: 4 (over x, core), lat: 4 (over z).
Axes of the slice: x: 2, y: 2, z: 4, core: 2. Of those that a mesh axis runs over, the one named last changes fastest.
Arguments:
- state: float32 [128, 720, 256], P(('grp', 'lat'), 'lon'), parts along dimension 0, may hold values from -6 to 6
- norm_gain: float32 [1, 2, 256], replicated, may hold values from 0.25 to 1.75
- disco_kernel: float32 [1, 64, 24, 8], P(None, 'lat'), may hold values from -1.25 to 1.25
- taps: int32 [64, 24], P('lat'), may hold values from 0 to 50
- counts: int32 [64], P('lat'), may hold values from 6 to 24, as said below
- disco_mix: bfloat16 [1, 2048, 256], replicated, may hold values from -0.125 to 0.125
- filter_gain: float32 [1, 256, 256], replicated, may hold values from -0.9 to 0.9
- mlp_in: bfloat16 [1, 256, 512], replicated, may hold values from -0.375 to 0.375
- mlp_out: bfloat16 [1, 512, 256], replicated, may hold values from -0.25 to 0.25
Outputs:
- new_state: float32 [128, 720, 256], P(('grp', 'lat'), 'lon'), parts along dimension 0
There are 2 independent parts, one for each index of `grp`. A program takes and returns all parts, laid end to end along the dimension named above; an argument that names none is the same for every part. Nothing has to cross between parts.
Inputs may be any that keep to these rules, and one draw needn't show every extreme that they name: `taps`: slot s of row i names a tap as (a + 1) * 17 + d + 8, row offset a in -1..1 and longitude offset d in -8..8; only the first counts[i] slots of a row are live. The first and last rows of the grid have 24 live slots; counts grow toward those rows.
All inputs are finite; a program needn't handle non-finite values.
Results may differ from a plain program's by a relative error of at most 0.0042.
Values may be sent and summed in bfloat16 or wider, within the bound.
A program may use at most 384 MiB of HBM per device.

v0:
```python
import math

import jax
import jax.numpy as jnp
from jax import lax
from jax.sharding import PartitionSpec as P

M = 256
L = 256
K = 8
R = 8
S = 24


exact_prec = lax.Precision.HIGHEST


def extended_2(cells, sides, width, closed):
    for axis, dim in sides:
        count = lax.axis_size(axis)
        ends = count if closed else count - 1
        head = lax.slice_in_dim(cells, 0, width, axis=dim)
        tail = lax.slice_in_dim(cells, cells.shape[dim] - width, cells.shape[dim], axis=dim)
        cells = jnp.concatenate(
            [
                lax.ppermute(tail, axis, [(i, (i + 1) % count) for i in range(ends)]),
                cells,
                lax.ppermute(head, axis, [((i + 1) % count, i) for i in range(ends)]),
            ],
            axis=dim,
        )
    return cells


def layer_norm(values, gain):
    center = values - jnp.mean(values, axis=-1, keepdims=True)
    spread = jnp.mean(center * center, axis=-1, keepdims=True)
    return center * lax.rsqrt(spread + 1e-05) * gain


def trig_table(mode_ids, lon_points, lon_total):
    product = mode_ids[:, None] * lon_points[None, :] % lon_total
    angles = product.astype(jnp.float32) * (2.0 * math.pi / lon_total)
    return (jnp.cos(angles), jnp.sin(angles))


def quad_weights(lat_count):
    row_ids = jnp.arange(lat_count).astype(jnp.float32)
    colatitude = math.pi * (row_ids + 0.5) / lat_count
    return math.pi * jnp.sin(colatitude) / lat_count


def legendre_table(mode_ids, lat_count, degrees):
    row_ids = jnp.arange(lat_count).astype(jnp.float32)
    colatitude = math.pi * (row_ids + 0.5) / lat_count
    cosine = jnp.cos(colatitude)[None, :]
    sine_val = jnp.sin(colatitude)[None, :]
    orders = mode_ids.astype(jnp.float32)[:, None]
    factor_ids = jnp.arange(1, degrees + 1).astype(jnp.float32)[None, :]
    log_terms = jnp.where(
        factor_ids <= orders, 0.5 * jnp.log((2.0 * factor_ids - 1.0) / (2.0 * factor_ids)), 0.0
    )
    log_start = 0.5 * jnp.log((2.0 * orders + 1.0) / (4.0 * math.pi)) + jnp.sum(
        log_terms, axis=1, keepdims=True
    )
    diagonal = jnp.exp(log_start + orders * jnp.log(sine_val))

    def advance(carry, degree):
        latest, earlier = carry
        deg_sq = degree * degree
        ord_sq = orders * orders
        upper_coef = jnp.sqrt((4.0 * deg_sq - 1.0) / jnp.maximum(deg_sq - ord_sq, 1.0))
        previous = degree - 1.0
        lower_coef = jnp.sqrt(
            jnp.maximum(previous * previous - ord_sq, 0.0)
            / jnp.maximum(4.0 * previous * previous - 1.0, 1.0)
        )
        recurred = upper_coef * (cosine * latest - lower_coef * earlier)
        second_row = cosine * jnp.sqrt(2.0 * orders + 3.0) * latest
        current = jnp.where(
            degree < orders,
            0.0,
            jnp.where(
                degree == orders, diagonal, jnp.where(degree == orders + 1.0, second_row, recurred)
            ),
        )
        return ((current, latest), current)

    blank_rows = jnp.zeros_like(diagonal)
    closing, values = lax.scan(
        advance, (blank_rows, blank_rows), jnp.arange(degrees).astype(jnp.float32), unroll=16
    )
    return jnp.transpose(values, (1, 0, 2))


def local(state, norm_gain, disco_kernel, taps, counts, disco_mix, filter_gain, mlp_in, mlp_out):
    lat_rows, lon_cols, channels = state.shape
    lon_parts = lax.axis_size("lon")
    lat_parts = lax.axis_size("lat")
    lon_total = lon_cols * lon_parts
    lat_total = lat_rows * lat_parts
    lon_pos = lax.axis_index("lon")
    lat_pos = lax.axis_index("lat")
    lon_points = lon_pos * lon_cols + jnp.arange(lon_cols, dtype=jnp.int32)
    modes_lon = M // lon_parts
    modes_own = M // (lon_parts * lat_parts)
    tap_span = 2 * R + 1
    tap_count = 3 * tap_span
    live_slots = jnp.arange(S, dtype=jnp.int32)[None, :] < counts[:, None]
    matches = (
        taps[:, :, None] == jnp.arange(tap_count, dtype=jnp.int32)[None, None, :]
    ) & live_slots[:, :, None]
    onehot = jnp.where(matches, 1.0, 0.0).astype(jnp.float32)
    own_modes = lon_pos * modes_lon + lat_pos * modes_own + jnp.arange(modes_own, dtype=jnp.int32)
    legendre = legendre_table(own_modes, lat_total, L)
    weighted = legendre * quad_weights(lat_total)[None, None, :]
    normed = layer_norm(state, norm_gain[0, 0]).astype(jnp.bfloat16)
    lat_ext = extended_2(normed, (("lat", 0),), 1, False)
    extended = extended_2(lat_ext, (("lon", 1),), R, True)
    kernel = jnp.einsum("ist,isk->itk", onehot, disco_kernel[0], precision=exact_prec)
    accum = jnp.zeros((lat_rows, lon_cols, K, channels), jnp.float32)
    for tap_id in range(tap_count):
        lat_off = tap_id // tap_span
        lon_off = tap_id % tap_span
        shifted = extended[lat_off : lat_off + lat_rows, lon_off : lon_off + lon_cols]
        accum = accum + kernel[:, tap_id, :][:, None, :, None] * shifted[:, :, None, :].astype(
            jnp.float32
        )
    conv_all = accum.astype(jnp.bfloat16)
    disco_out = jnp.dot(
        conv_all.reshape(lat_rows * lon_cols, K * channels),
        disco_mix[0],
        preferred_element_type=jnp.float32,
    ).reshape(lat_rows, lon_cols, channels)
    mode_ids = jnp.arange(modes_lon * lax.axis_size("lon"), dtype=jnp.int32)
    cosine, sine_val = trig_table(mode_ids, lon_points, lon_total)
    as_float = normed.astype(jnp.float32)
    real_part = jnp.einsum("mp,ipc->mic", cosine / lon_total, as_float, precision=exact_prec)
    imag_part = jnp.einsum("mp,ipc->mic", -sine_val / lon_total, as_float, precision=exact_prec)
    spectrum = lax.psum_scatter(
        jnp.stack([real_part, imag_part], axis=2).astype(jnp.bfloat16),
        "lon",
        scatter_dimension=0,
        tiled=True,
    ).astype(jnp.float32)
    owned = lax.all_to_all(
        spectrum.astype(jnp.bfloat16), "lat", split_axis=0, concat_axis=1, tiled=True
    ).astype(spectrum.dtype)
    coefficient = jnp.einsum("mlj,mjrc->mlrc", weighted, owned, precision=exact_prec)
    scaled = coefficient * filter_gain[0][None, :, None, :]
    filtered = jnp.einsum("mlj,mlrc->mjrc", legendre, scaled, precision=exact_prec).astype(
        jnp.bfloat16
    )
    returned = lax.all_to_all(filtered, "lat", split_axis=1, concat_axis=0, tiled=True)
    shard_piece = lax.all_gather(returned, "lon", axis=0, tiled=True)
    mode_ids = jnp.arange(shard_piece.shape[0], dtype=jnp.int32)
    cosine, sine_val = trig_table(mode_ids, lon_points, lon_total)
    factor = jnp.where(mode_ids == 0, 1.0, 2.0).astype(jnp.float32)[:, None]
    as_float = shard_piece.astype(jnp.float32)
    cos_term = jnp.einsum("mp,mic->ipc", factor * cosine, as_float[:, :, 0], precision=exact_prec)
    sin_term = jnp.einsum("mp,mic->ipc", factor * sine_val, as_float[:, :, 1], precision=exact_prec)
    spectral_out = cos_term - sin_term
    state = state + disco_out + spectral_out
    normed_two = layer_norm(state, norm_gain[0, 1]).astype(jnp.bfloat16)
    hidden = jax.nn.gelu(jnp.dot(normed_two, mlp_in[0], preferred_element_type=jnp.float32)).astype(
        jnp.bfloat16
    )
    state = state + jnp.dot(hidden, mlp_out[0], preferred_element_type=jnp.float32)
    return state


def solution(mesh):
    in_specs = (
        P(("grp", "lat"), "lon", None),
        P(),
        P(None, "lat", None, None),
        P("lat", None),
        P("lat"),
        P(),
        P(),
        P(),
        P(),
    )
    out_specs = P(("grp", "lat"), "lon", None)
    return jax.shard_map(local, mesh=mesh, in_specs=in_specs, out_specs=out_specs, check_vma=False)
```

profile of v0, /device:TPU:19, one launch (start us, length us, event | category | flops | bytes accessed | tf_op | source)
XLA Modules:
  0.0 1314.4 jit_solution(10612231311055935089)
XLA Ops:
  9.1 2.7 multiply_reduce_fusion.1
  12.5 3.6 fusion.178
  17.4 3.2 collective-permute-start
  23.3 2.7 convert_bitcast_fusion
  26.1 2.7 convert_bitcast_fusion.1
  31.5 864.8 %while.21 = (s32[]{:T(128)}, f32[16,64]{1,0:T(8,128)S(1)}, f32[16,64]{1,0:T(8,128)S(1)}, f32[16,16,16,64]{3,2,1,0:T(8,128)}, f32[16,16]{1,0:T(8,128)S(1)}, /*ind...) while((s32[]{:T(128)}, f32[16,64]{1,0:T(8,128)S(1)}, ...), condition=%wide.region_4.5_spmd.clone.clone.clone.clone, body=%wide.region_3.4_spmd.clone.clone.clone.clone.sunk | while | flops 187810 | bytes 796712 | solution.py:90
  944.1 3.4 copy.1017
  952.4 3.8 fusion.84
  956.7 4.1 maximum_maximum_fusion
  962.3 10.1 slice_convert_fusion.38
  972.3 2.8 copy.1020
  975.1 5.4 all-to-all-start
  980.5 34.7 %slice_convert_fusion.47 = (f32[16,180,256]{2,0,1:T(8,128)}, f32[16,180,256]{2,0,1:T(8,128)}, f32[16,180,256]{2,0,1:T(8,128)}, f32[16,180,256]{2,0,1:T(8,128)}, ...) fusion(bf16[18,188,256]{2,0,1:T(8,128)(2,1)} %copy-done.1), kind=kLoop, calls=%fused_computation.262 | loop fusion | flops 14008320 | bytes 84049920 | tf_op jit(solution)/shard_map/convert_element_type | solution.py:126
  1016.6 5.1 fusion.87
  1021.7 5.4 fusion.80
  1029.2 4.5 all-to-all-start.1
  1033.7 18.1 %slice_convert_fusion.39 = (f32[16,180,256]{2,0,1:T(8,128)}, f32[16,180,256]{2,0,1:T(8,128)}, f32[16,180,256]{2,0,1:T(8,128)}, f32[16,180,256]{2,0,1:T(8,128)}, ...) fusion(bf16[18,188,256]{2,0,1:T(8,128)(2,1)S(1)} %get-tuple-ele, ...), kind=kLoop, calls=%fused_computation.252 | loop fusion | flops 14008320 | bytes 84049920 | tf_op jit(solution)/shard_map/convert_element_type | solution.py:126
  1052.0 3.9 all-to-all-done.1
  1058.6 201.4 %add_convert_fusion = bf16[16,180,8,256]{3,2,0,1:T(8,128)(2,1)} fusion(f32[16,180,256]{2,0,1:T(8,128)} %get-tuple-element.569, f32[16,8]{1,0:T(8,128)S(1)} %bitcast.546, f32[16,180,256]{2,0,1:T(8,128)} %get-tuple-element.570, f32[16,8]{1,0:T(8,128)S(1)} %bitcast.545, f32[16,180,256]{2,0,1:T(8,128)} %get-tuple-element.571, f32[16,8]{1,0:T(8,128)S(1)} %bitcast.582, ...), kind=kLoop, calls=%fused_computation.178 | loop fusion | flops 601620480 | bytes 162227712 | tf_op jit(solution)/shard_map/convert_element_type | solution.py:129
  1260.0 19.0 %convert_element_type.382 = bf16[16,180,2048]{2,0,1:T(8,128)(2,1)} reshape(bf16[16,180,8,256]{3,2,0,1:T(8,128)(2,1)} %add_convert_fusion) | data formatting | bytes 23592960 | tf_op jit(solution)/shard_map/convert_element_type | solution.py:129
  1279.1 3.9 fusion.75
  1285.3 10.8 fusion.185
  1296.3 2.7 multiply_reduce_fusion
  1304.4 2.7 fusion.76
  (1176 shorter events, 452.7 us)
Async XLA Ops:
  6.5 1278.7 %copy-start = (bf16[1,2048,256]{2,1,0:T(8,128)(2,1)S(1)}, bf16[1,2048,256]{2,1,0:T(8,128)(2,1)}, u32[]{:S(2)}) copy-start(bf16[1,2048,256]{2,1,0:T(8,128)(2,1)} %param.16) | copy-start | bytes 3145732
  6.5 965.8 %reduce-scatter.2.cloned.1.call-start = ((), (), s32[]{:S(2)}) async-start(), calls=%async_computation.3 | async-start | bytes 5242880 | tf_op jit(solution)/shard_map/reduce_scatter | solution.py:140
  16.2 936.2 %copy-start.2 = (bf16[16,180,256]{2,0,1:T(8,128)(2,1)}, bf16[16,180,256]{2,0,1:T(8,128)(2,1)S(1)}, u32[]{:S(2)}) copy-start(bf16[16,180,256]{2,0,1:T(8,128)(2,1)S(1)} %get-tuple-element.447) | copy-start | bytes 4423684
  17.4 931.4 %collective-permute-start = (bf16[1,180,256]{2,1,0:T(8,128)(2,1)}, bf16[1,180,256]{2,1,0:T(8,128)(2,1)}, u32[]{:S(2)}, u32[]{:S(2)}) collective-permute-start(bf16[1,180,256]{2,1,0:T(8,128)(2,1)} %copy.911), channel_id=1, source_target_pairs={{0,1},{1,2},{2,3},{4,5},{5,6},{6,7},{8,9},{9,10},{10,11},{12,13},{... | collective-permute-start | bytes 276488 | tf_op jit(solution)/shard_map/ppermute | solution.py:26
  21.2 928.6 %collective-permute-start.1 = (bf16[1,180,256]{2,1,0:T(8,128)(2,1)}, bf16[1,180,256]{2,1,0:T(8,128)(2,1)}, u32[]{:S(2)}, u32[]{:S(2)}) collective-permute-start(bf16[1,180,256]{2,1,0:T(8,128)(2,1)} %copy.912), channel_id=1, source_target_pairs={{1,0},{2,1},{3,2},{5,4},{6,5},{7,6},{9,8},{10,9},{11,10},{13,12},{... | collective-permute-start | bytes 276488 | tf_op jit(solution)/shard_map/ppermute | solution.py:28
  31.5 864.8 %copy-start.41 = (s32[16]{0:T(128)S(1)}, s32[16]{0:T(128)}, u32[]{:S(2)}) copy-start(s32[16]{0:T(128)} %param.15) | copy-start | bytes 196
  31.5 864.9 %copy-start.43 = (f32[1,16,24,8]{2,3,1,0:T(8,128)S(1)}, f32[1,16,24,8]{2,3,1,0:T(8,128)}, u32[]{:S(2)}) copy-start(f32[1,16,24,8]{2,3,1,0:T(8,128)} %param.13) | copy-start | bytes 36868
  31.5 864.9 %copy-start.44 = (s32[16,24]{1,0:T(8,128)S(1)}, s32[16,24]{1,0:T(8,128)}, u32[]{:S(2)}) copy-start(s32[16,24]{1,0:T(8,128)} %param.14) | copy-start | bytes 4612
  951.0 5.3 collective-permute-start.2
  952.4 4.3 collective-permute-start.3
  975.1 40.1 %all-to-all-start = ((bf16[64,16,2,256]{3,1,2,0:T(8,128)(2,1)}), bf16[64,16,2,256]{3,1,2,0:T(8,128)(2,1)}, u32[]{:S(2)}, u32[]{:S(2)}) async-start(bf16[64,16,2,256]{3,1,2,0:T(8,128)(2,1)} %copy.1020), calls=%async_computation.1 | async-start | bytes 2097152 | tf_op jit(solution)/shard_map/all_to_all | solution.py:146
  1029.2 26.8 %all-to-all-start.1 = ((bf16[16,64,2,256]{3,2,0,1:T(2,128)(2,1)}), bf16[16,64,2,256]{3,2,0,1:T(2,128)(2,1)}, u32[]{:S(2)}, u32[]{:S(2)}) async-start(bf16[16,64,2,256]{3,2,0,1:T(2,128)(2,1)} %copy.1022), calls=%async_computation.2 | async-start | bytes 2097152 | tf_op jit(solution)/shard_map/all_to_all | solution.py:154
  1033.7 245.4 %all-gather.2.cloned.1.call-start = ((), (), s32[]{:S(2)}) async-start(), calls=%async_computation.4 | async-start | bytes 5242880 | tf_op jit(solution)/shard_map/all_gather | solution.py:155
  1051.8 6.6 copy-start.9
  1051.8 6.6 copy-start.10
  1051.8 6.6 copy-start.11
  1051.8 6.6 copy-start.12
  1051.8 6.6 copy-start.13
  1051.8 6.6 copy-start.14
  1051.8 6.6 copy-start.15
  1051.8 6.6 copy-start.16
  1051.8 6.6 copy-start.17
  1260.0 19.1 %copy-start.37 = (s32[180]{0:T(256)S(1)}, s32[180]{0:T(256)}, u32[]{:S(2)}) copy-start(s32[180]{0:T(256)} %copy-done.36) | copy-start | bytes 2164
  1260.0 19.1 %copy-start.38 = (f32[256]{0:T(256)S(1)}, f32[256]{0:T(256)}, u32[]{:S(2)}) copy-start(f32[256]{0:T(256)} %compare_select_fusion) | copy-start | bytes 3076
  (29 other events, 155.9 us)
Sparse Core Ops, SparseCore 0:
  31.3 45.8 reduce-scatter.1
  1058.5 36.7 all-gather.1
where the time goes:
time: 1340 us; the launch traced here: 1310 us
  other arithmetic  642 us (48%)
  loops' own time  490 us (37%)
  local copies, waits for them, and re-layouts  107 us (8%)
  matrix products  38.6 us (3%)
  starting transfers between devices  16.6 us (1%)
  between operations  14.8 us (1%)
    another operation x1, loops' own time, legendre_table(): lax.scan(advance, (blank_rows, blank_rows), jnp.arange(degrees).astype(jn...  490 us
    convert_element_type x1, other arithmetic, local(): conv_all = accum.astype(jnp.bfloat16)  201 us
    lt x128, other arithmetic, advance(): degree < orders  162 us
    eq x128, other arithmetic, advance(): degree == orders  81.8 us
    eq x128, other arithmetic, advance(): degree == orders + 1.0  81.2 us
    convert_element_type x5, other arithmetic, local(): shifted[:, :, None, :].astype(jnp.float32)  70.3 us
    mul x51, local copies, waits for them, and re-layouts, local(): kernel[:, tap_id, :][:, None, :, None]  44.5 us
  transfers between devices with their start and end apart: 8, of which 2 were waited for; matrix products, arithmetic and copies ran while one was open for 55% of the time, Pallas kernels for 0%

commit v1 on v0

v1 whole, which is shorter than its diff:
```python
import functools
import math

import jax
import jax.numpy as jnp
from jax import lax
from jax.experimental import pallas as pl
from jax.experimental.pallas import tpu as pltpu
from jax.sharding import PartitionSpec as P

M = 256
L = 256
K = 8
R = 8
S = 24
WIDTH = 64
REACH = WIDTH + 2 * R
LANES = 256

exact_prec = lax.Precision.HIGHEST


def halo(cells, axis, dim, width, closed):
    count = lax.axis_size(axis)
    ends = count if closed else count - 1
    head = lax.slice_in_dim(cells, 0, width, axis=dim)
    tail = lax.slice_in_dim(cells, cells.shape[dim] - width, cells.shape[dim], axis=dim)
    before = lax.ppermute(tail, axis, [(i, (i + 1) % count) for i in range(ends)])
    after = lax.ppermute(head, axis, [((i + 1) % count, i) for i in range(ends)])
    return before, after


def layer_norm(values, gain):
    center = values - jnp.mean(values, axis=-1, keepdims=True)
    spread = jnp.mean(center * center, axis=-1, keepdims=True)
    return center * lax.rsqrt(spread + 1e-05) * gain


def trig_table(mode_ids, lon_points, lon_total):
    product = mode_ids * lon_points % lon_total
    angles = product.astype(jnp.float32) * (2.0 * math.pi / lon_total)
    return (jnp.cos(angles), jnp.sin(angles))


def colatitudes(lat_count):
    row_ids = jnp.arange(lat_count).astype(jnp.float32)
    return math.pi * (row_ids + 0.5) / lat_count


def legendre_kernel(orders_ref, cosine_ref, diagonal_ref, out_ref):
    orders = orders_ref[...]
    cosine = cosine_ref[...]
    diagonal = diagonal_ref[...]
    ord_sq = orders * orders
    second_coef = cosine * jnp.sqrt(2.0 * orders + 3.0)

    def advance(step, carry):
        latest, earlier = carry
        degree = step.astype(jnp.float32)
        deg_sq = degree * degree
        upper_coef = jnp.sqrt((4.0 * deg_sq - 1.0) / jnp.maximum(deg_sq - ord_sq, 1.0))
        previous = degree - 1.0
        lower_coef = jnp.sqrt(
            jnp.maximum(previous * previous - ord_sq, 0.0)
            / jnp.maximum(4.0 * previous * previous - 1.0, 1.0)
        )
        recurred = upper_coef * (cosine * latest - lower_coef * earlier)
        current = jnp.where(
            degree < orders,
            0.0,
            jnp.where(
                degree == orders,
                diagonal,
                jnp.where(degree == orders + 1.0, second_coef * latest, recurred),
            ),
        )
        out_ref[step] = current
        return current, latest

    blank = diagonal * 0.0
    lax.fori_loop(0, out_ref.shape[0], advance, (blank, blank), unroll=8)


def legendre_table(mode_ids, lat_count, degrees):
    colatitude = colatitudes(lat_count)
    cosine = jnp.cos(colatitude)[None, :]
    sine_val = jnp.sin(colatitude)[None, :]
    orders = mode_ids.astype(jnp.float32)[:, None]
    factor_ids = jnp.arange(1, degrees + 1).astype(jnp.float32)[None, :]
    log_terms = jnp.where(
        factor_ids <= orders, 0.5 * jnp.log((2.0 * factor_ids - 1.0) / (2.0 * factor_ids)), 0.0
    )
    log_start = 0.5 * jnp.log((2.0 * orders + 1.0) / (4.0 * math.pi)) + jnp.sum(
        log_terms, axis=1, keepdims=True
    )
    diagonal = jnp.exp(log_start + orders * jnp.log(sine_val))
    shape = diagonal.shape
    return pl.pallas_call(
        legendre_kernel,
        out_shape=jax.ShapeDtypeStruct((degrees,) + shape, jnp.float32),
        compiler_params=pltpu.CompilerParams(vmem_limit_bytes=48 * 2**20),
        cost_estimate=pl.CostEstimate(
            flops=40 * degrees * 1024, bytes_accessed=4 * degrees * 2048, transcendentals=0
        ),
        name="legendre",
    )(jnp.broadcast_to(orders, shape), jnp.broadcast_to(cosine, shape), diagonal)


def disco_body(above_ref, here_ref, below_ref, base_ref, mix_ref, state_ref, out_ref, band_ref):
    cols = state_ref.shape[1]
    channels = state_ref.shape[2]
    for k in range(K):
        row = jnp.broadcast_to(base_ref[0, k : k + 1, :], (WIDTH, LANES))
        band = pltpu.roll(row, 0, 1, stride=1, stride_axis=0)
        band_ref[k * WIDTH : (k + 1) * WIDTH, :] = band.astype(jnp.bfloat16)
    band = band_ref[:, : 3 * REACH]
    pieces = []
    for start in range(0, cols, WIDTH):
        window = jnp.concatenate(
            [ref[0, start : start + REACH, :] for ref in (above_ref, here_ref, below_ref)], axis=0
        )
        conv = jnp.dot(band, window, preferred_element_type=jnp.float32).astype(jnp.bfloat16)
        pieces.append(
            jnp.concatenate([conv[k * WIDTH : (k + 1) * WIDTH] for k in range(K)], axis=1)
        )
    mixed = jnp.dot(
        jnp.concatenate(pieces, axis=0), mix_ref[...], preferred_element_type=jnp.float32
    )
    out_ref[0] = state_ref[0] + mixed[:cols]


def disco_update(extended, base, mix, state):
    rows, cols, channels = state.shape
    width = extended.shape[1]

    def ext_spec(offset):
        return pl.BlockSpec((1, width, channels), lambda i: (i + offset, 0, 0))

    cell = pl.BlockSpec((1, cols, channels), lambda i: (i, 0, 0))
    return pl.pallas_call(
        disco_body,
        grid=(rows,),
        in_specs=[
            ext_spec(0),
            ext_spec(1),
            ext_spec(2),
            pl.BlockSpec((1, K, LANES), lambda i: (i, 0, 0)),
            pl.BlockSpec(mix.shape, lambda i: (0, 0)),
            cell,
        ],
        out_specs=cell,
        out_shape=jax.ShapeDtypeStruct(state.shape, jnp.float32),
        scratch_shapes=[pltpu.VMEM((K * WIDTH, LANES), jnp.bfloat16)],
        compiler_params=pltpu.CompilerParams(vmem_limit_bytes=48 * 2**20),
        cost_estimate=pl.CostEstimate(
            flops=2 * rows * cols * K * channels * 512, bytes_accessed=12 * 2**20, transcendentals=0
        ),
        name="disco",
    )(extended, extended, extended, base, mix, state)


def mlp_body(state_ref, spectral_ref, gain_ref, in_ref, out_mat_ref, out_ref):
    state = state_ref[0] + spectral_ref[0].astype(jnp.float32)
    normed = layer_norm(state, gain_ref[...]).astype(jnp.bfloat16)
    hidden = jax.nn.gelu(jnp.dot(normed, in_ref[...], preferred_element_type=jnp.float32))
    out_ref[0] = state + jnp.dot(
        hidden.astype(jnp.bfloat16), out_mat_ref[...], preferred_element_type=jnp.float32
    )


def mlp_update(state, spectral, gain, mat_in, mat_out):
    rows, cols, channels = state.shape
    cell = pl.BlockSpec((1, cols, channels), lambda i: (i, 0, 0))
    return pl.pallas_call(
        mlp_body,
        grid=(rows,),
        in_specs=[
            cell,
            cell,
            pl.BlockSpec(gain.shape, lambda i: (0, 0)),
            pl.BlockSpec(mat_in.shape, lambda i: (0, 0)),
            pl.BlockSpec(mat_out.shape, lambda i: (0, 0)),
        ],
        out_specs=cell,
        out_shape=jax.ShapeDtypeStruct(state.shape, jnp.float32),
        compiler_params=pltpu.CompilerParams(vmem_limit_bytes=48 * 2**20),
        name="mlp",
    )(state, spectral, gain, mat_in, mat_out)


def local(state, norm_gain, disco_kernel, taps, counts, disco_mix, filter_gain, mlp_in, mlp_out):
    lat_rows, lon_cols, channels = state.shape
    lon_parts = lax.axis_size("lon")
    lat_parts = lax.axis_size("lat")
    parts = lon_parts * lat_parts
    lon_total = lon_cols * lon_parts
    lat_total = lat_rows * lat_parts
    rank = lax.axis_index("lat") * lon_parts + lax.axis_index("lon")
    modes_own = M // parts
    tap_span = 2 * R + 1

    normed = layer_norm(state, norm_gain[0, 0]).astype(jnp.bfloat16)
    whole_rows = lax.all_to_all(normed, "lon", split_axis=0, concat_axis=1, tiled=True)

    slot_ids = jnp.arange(2 * M, dtype=jnp.int32)
    imaginary = slot_ids // modes_own % 2 == 1
    slot_modes = slot_ids // (2 * modes_own) * modes_own + slot_ids % modes_own
    points = jnp.arange(lon_total, dtype=jnp.int32)
    cosine, sine_val = trig_table(slot_modes[:, None], points[None, :], lon_total)
    analysis = (jnp.where(imaginary[:, None], -sine_val, cosine) / lon_total).astype(jnp.bfloat16)
    factor = jnp.where(slot_modes == 0, 1.0, 2.0).astype(jnp.float32)
    cosine, sine_val = trig_table(slot_modes[None, :], points[:, None], lon_total)
    synthesis = (jnp.where(imaginary[None, :], -sine_val, cosine) * factor[None, :]).astype(
        jnp.bfloat16
    )

    own_modes = rank * modes_own + jnp.arange(modes_own, dtype=jnp.int32)
    legendre = legendre_table(own_modes, lat_total, L)
    weights = math.pi * jnp.sin(colatitudes(lat_total)) / lat_total
    weighted = (legendre * weights[None, None, :]).astype(jnp.bfloat16)
    legendre = legendre.astype(jnp.bfloat16)

    live = jnp.arange(S, dtype=jnp.int32)[None, :] < counts[:, None]
    lanes = taps // tap_span * REACH + taps % tap_span
    matches = (lanes[:, :, None] == jnp.arange(LANES, dtype=jnp.int32)) & live[:, :, None]
    base = jnp.einsum(
        "isq,isk->ikq", matches.astype(jnp.float32), disco_kernel[0], precision=exact_prec
    )

    above, below = halo(normed, "lat", 0, 1, False)
    extended = jnp.concatenate([above, normed, below], axis=0)
    west, east = halo(extended, "lon", 1, R, True)
    blocks = -(-lon_cols // WIDTH)
    spare = blocks * WIDTH - lon_cols
    extended = jnp.concatenate(
        [west, extended, east, jnp.zeros((lat_rows + 2, spare, channels), jnp.bfloat16)], axis=1
    )
    partial = disco_update(extended, base, disco_mix[0], state)

    spectrum = jnp.einsum(
        "mp,ipc->imc", analysis, whole_rows, preferred_element_type=jnp.float32
    ).astype(jnp.bfloat16)
    owned = lax.all_to_all(spectrum, ("lat", "lon"), split_axis=1, concat_axis=0, tiled=True)
    owned = owned.reshape(lat_total, 2, modes_own, channels)
    coefficient = jnp.einsum(
        "lmj,jrmc->mlrc", weighted, owned, preferred_element_type=jnp.float32
    )
    scaled = (coefficient * filter_gain[0][None, :, None, :]).astype(jnp.bfloat16)
    filtered = jnp.einsum(
        "lmj,mlrc->mjrc", legendre, scaled, preferred_element_type=jnp.float32
    ).astype(jnp.bfloat16)
    filtered = jnp.transpose(filtered, (1, 2, 0, 3)).reshape(
        lat_total, 2 * modes_own, channels
    )
    returned = lax.all_to_all(filtered, ("lat", "lon"), split_axis=0, concat_axis=1, tiled=True)
    spectral = jnp.einsum(
        "pm,imc->ipc", synthesis, returned, preferred_element_type=jnp.float32
    ).astype(jnp.bfloat16)
    spectral = lax.all_to_all(spectral, "lon", split_axis=1, concat_axis=0, tiled=True)
    return mlp_update(partial, spectral, norm_gain[0, 1:2], mlp_in[0], mlp_out[0])


def solution(mesh):
    in_specs = (
        P(("grp", "lat"), "lon", None),
        P(),
        P(None, "lat", None, None),
        P("lat", None),
        P("lat"),
        P(),
        P(),
        P(),
        P(),
    )
    out_specs = P(("grp", "lat"), "lon", None)
    return jax.shard_map(local, mesh=mesh, in_specs=in_specs, out_specs=out_specs, check_vma=False)
```

time: 1340 us -> 166 us (0.12); the launches traced: 1310 us -> 164 us
  other arithmetic: 642 us -> 10.5 us
  loops' own time: 490 us -> 0 us
  local copies, waits for them, and re-layouts: 107 us -> 13.6 us
  waiting for transfers between devices: 4.4 us -> 57 us
  Pallas kernels: 0 us -> 32.1 us
  matrix products: 38.6 us -> 20.9 us
  between operations: 14.8 us -> 0.25 us
    another operation x1 -> x0, loops' own time: 490 us -> none  [legendre_table(): lax.scan(advance, (blank_rows, blank_rows), jnp.arange(degrees).astype(jn...]
    convert_element_type x8 -> x2, other arithmetic: 274 us -> 3.06 us  [the longest x1 2.78 us: local(): normed = layer_norm(state, norm_gain[0, 0]).astype(jnp.bfloat16)]
    eq x256 -> x1, other arithmetic: 163 us -> 0.01 us  [local(): imaginary = slot_ids // modes_own % 2 == 1]
    lt x129 -> x1, other arithmetic: 162 us -> 0.07 us  [local(): live = jnp.arange(S, dtype=jnp.int32)[None, :] < counts[:, None]]
    mul x51 -> x0, local copies, waits for them, and re-layouts: 44.5 us -> none  [local(): kernel[:, tap_id, :][:, None, :, None]]
    all_to_all x2 -> x4, waiting for transfers between devices: 3.89 us -> 36.8 us  [the longest x1 19.3 us: local(): lax.all_to_all(spectrum, ('lat', 'lon'), split_axis=1, concat_axis=0, til...]
    pallas_call x0 -> x3, Pallas kernels: none -> 32.1 us  [the longest x1 16.6 us: disco_update(): pl.pallas_call(disco_body, grid=(rows,), in_specs=[ext_spec(0), ext_spec(...]
    while x240 -> x0, other arithmetic: 20.5 us -> none
  transfers between devices with their start and end apart: 8 -> 8, of which waited for: 2 -> 3; matrix products, arithmetic and copies ran while one was open for 55% -> 7% of each run, Pallas kernels for 0% -> 12%
where the time goes in v1:
time: 166 us; the launch traced here: 164 us
  waiting for transfers between devices  57 us (34%)
  Pallas kernels  32.1 us (19%)
  starting transfers between devices  29.8 us (18%)
  matrix products  20.9 us (13%)
  local copies, waits for them, and re-layouts  13.6 us (8%)
  other arithmetic  10.5 us (6%)
    ppermute x2, waiting for transfers between devices, halo(): lax.ppermute(tail, axis, [(i, (i + 1) % count) for i in range(ends)])  20.2 us
    all_to_all x1, waiting for transfers between devices, local(): lax.all_to_all(spectrum, ('lat', 'lon'), split_axis=1, concat_axis=0, til...  19.3 us
    all_to_all x1, waiting for transfers between devices, local(): lax.all_to_all(normed, 'lon', split_axis=0, concat_axis=1, tiled=True)  17.5 us
    pallas_call x1, Pallas kernels, disco_update(): pl.pallas_call(disco_body, grid=(rows,), in_specs=[ext_spec(0), ext_spec(...  16.6 us
    pallas_call x1, Pallas kernels, mlp_update(): pl.pallas_call(mlp_body, grid=(rows,), in_specs=[cell, cell, pl.BlockSpec...  12.7 us
    dot_general x1, matrix products, local(): jnp.einsum('mp,ipc->imc', analysis, whole_rows, preferred_element_type=jn...  8.28 us
    dot_general x1, matrix products, local(): jnp.einsum('pm,imc->ipc', synthesis, returned, preferred_element_type=jnp...  7.6 us
    all_to_all x1, starting transfers between devices, local(): lax.all_to_all(filtered, ('lat', 'lon'), split_axis=0, concat_axis=1, til...  7.06 us
  transfers between devices with their start and end apart: 8, of which 3 were waited for; matrix products, arithmetic and copies ran while one was open for 7% of the time, Pallas kernels for 12%

profile of v1, /device:TPU:19, one launch (start us, length us, event | category | flops | bytes accessed | tf_op | source)
XLA Modules:
  0.0 164.2 jit_solution(16343725034212973835)
XLA Ops:
  0.0 2.4 %reduce_sum.27 = f32[16,180]{0,1:T(8,128)S(1)} reduce(f32[16,180,256]{2,0,1:T(8,128)} %param.9, f32[]{:T(128)} %constant.127.clone.1), dimensions={2}, to_apply=%region_0.0 | reduce | flops 734400 | bytes 2960644 | tf_op jit(solution)/shard_map/reduce_sum | solution.py:34
  2.8 3.7 %fusion.72 = (f32[16,180,256]{2,1,0:T(8,128)}, f32[16,180]{1,0:T(8,128)S(1)}) fusion(f32[16,180,256]{2,0,1:T(8,128)S(1)} %copy-done.5, f32[16,180]{1,0:T(8,128)S(1)} %broadcast_multiply_fusion), kind=kLoop, calls=%fused_computation.113 | loop fusion | flops 2208960 | bytes 5921280 | tf_op args[0]
  6.4 2.8 %multiply_convert_fusion.2 = bf16[16,180,256]{2,1,0:T(8,128)(2,1)} fusion(f32[256]{0:T(256)S(1)} %bitcast.60, f32[16,180]{1,0:T(8,128)S(1)} %add_rsqrt_fusion, f32[16,180]{1,0:T(8,128)S(1)} %broadcast_multiply_fusion, f32[16,180,256]{2,0,1:T(8,128)S(1)} %copy-done.5), kind=kLoop, calls=%fused_computation.4 | loop fusion | flops 2949120 | bytes 4447744 | tf_op jit(solution)/shard_map/convert_element_type | solution.py:202
  9.2 4.4 %all-to-all-start = ((bf16[16,180,256]{2,1,0:T(8,128)(2,1)}), bf16[16,180,256]{2,1,0:T(8,128)(2,1)S(1)}, u32[]{:S(2)}, u32[]{:S(2)}) async-start(bf16[16,180,256]{2,1,0:T(8,128)(2,1)} %multiply_convert_fusion.2), calls=%async_computation | async-start | bytes 3014656 | tf_op jit(solution)/shard_map/all_to_all | solution.py:203
  13.6 17.5 %all-to-all-done = bf16[16,180,256]{2,1,0:T(8,128)(2,1)S(1)} async-done(((bf16[16,180,256]{2,1,0:T(8,128)(2,1)}), bf16[16,180,256]{2,1,0:T(8,128)(2,1)S(1)}, u32[]{:S(2)}, u32[]{:S(2)}) %all-to-all-start) | async-done | bytes 1474592 | tf_op jit(solution)/shard_map/all_to_all | solution.py:203
  31.5 8.3 %fusion.16 = bf16[4,512,256]{1,2,0:T(8,128)(2,1)S(1)} fusion(bf16[4,720,256]{2,1,0:T(8,128)(2,1)S(1)} %all_to_all.53, s32[512]{0:T(512)S(1)} %fusion.56, pred[512]{0:T(512)(128)(4,1)S(1)} %fusion.53), kind=kOutput, calls=%fused_computation.29 | convolution fusion | flops 760291328 | bytes 2525696 | tf_op jit(solution)/shard_map/mp,ipc->imc/dot_general | solution.py:240
  39.8 1.4 copy.84
  41.2 6.6 %all-to-all-start.1 = ((bf16[4,512,256]{2,0,1:T(4,128)(2,1)}), bf16[4,512,256]{2,0,1:T(4,128)(2,1)S(1)}, u32[]{:S(2)}, u32[]{:S(2)}) async-start(bf16[4,512,256]{2,0,1:T(4,128)(2,1)} %copy.84), calls=%async_computation.1 | async-start | bytes 2097152 | tf_op jit(solution)/shard_map/all_to_all | solution.py:243
  48.3 2.7 %legendre.1 = f32[256,16,64]{2,1,0:T(8,128)S(1)} custom-call(f32[16,64]{1,0:T(8,128)S(1)} %broadcast_in_dim.43.orders_ref, f32[16,64]{1,0:T(8,128)S(1)} %broadcast_in_dim.44.cosine_ref, f32[16,64]{1,0:T(8,128)S(1)} %add_exponential_fusion.diagonal_ref), custom_call_target="tpu_custom_call" | custom-call | flops 10485760 | bytes 2097152 | tf_op jit(solution)/shard_map/legendre/pallas_call | solution.py:98
  51.4 19.3 %all-to-all-done.1 = bf16[4,512,256]{2,0,1:T(4,128)(2,1)S(1)} async-done(((bf16[4,512,256]{2,0,1:T(4,128)(2,1)}), bf16[4,512,256]{2,0,1:T(4,128)(2,1)S(1)}, u32[]{:S(2)}, u32[]{:S(2)}) %all-to-all-start.1) | async-done | bytes 1048608 | tf_op jit(solution)/shard_map/all_to_all | solution.py:243
  71.8 4.6 %fusion.17 = bf16[64,2,16,256]{3,0,1,2:T(8,128)(2,1)} fusion(f32[256,256]{1,0:T(8,128)S(1)} %bitcast.61, bf16[256,16,64,1]{2,1,0,3:T(8,128)(2,1)S(1)} %get-tuple-element.8, bf16[256,16,64,1]{2,1,0,3:T(8,128)(2,1)S(1)} %get-tuple-element.7, bf16[64,2,16,256]{3,2,1,0:T(8,128)(2,1)S(1)} %bitcast.58), kind=kOutput, calls=%fused_computation.30 | convolution fusion | flops 541589504 | bytes 3407872 | tf_op jit(solution)/shard_map/lmj,mlrc->mjrc/dot_general | solution.py:249
  76.4 2.8 %copy.90 = bf16[64,2,16,256]{3,2,1,0:T(8,128)(2,1)} copy(bf16[64,2,16,256]{3,0,1,2:T(8,128)(2,1)} %fusion.17) | data formatting | bytes 2097152 | tf_op jit(solution)/shard_map/convert_element_type | solution.py:251
  79.2 7.1 %all-to-all-start.2 = ((bf16[64,32,256]{2,1,0:T(8,128)(2,1)}), bf16[64,32,256]{2,1,0:T(8,128)(2,1)S(1)}, u32[]{:S(2)}, u32[]{:S(2)}) async-start(bf16[64,32,256]{2,1,0:T(8,128)(2,1)} %bitcast.56), calls=%async_computation.2 | async-start | bytes 2097152 | tf_op jit(solution)/shard_map/all_to_all | solution.py:255
  86.3 3.1 %collective-permute-start = (bf16[1,180,256]{2,1,0:T(8,128)(2,1)S(1)}, bf16[1,180,256]{2,1,0:T(8,128)(2,1)S(1)}, u32[]{:S(2)}, u32[]{:S(2)}) collective-permute-start(bf16[1,180,256]{2,1,0:T(8,128)(2,1)S(1)} %get-tuple-element.11), channel_id=1, source_target_pairs={{0,1},{1,2},{2,3},{4,5},{5,6},{6,7},{8,9},{9,10},{10,11},{12,13},{... | collective-permute-start | bytes 276488 | tf_op jit(solution)/shard_map/ppermute | solution.py:28
  89.4 2.4 %collective-permute-start.1 = (bf16[1,180,256]{2,1,0:T(8,128)(2,1)S(1)}, bf16[1,180,256]{2,1,0:T(8,128)(2,1)S(1)}, u32[]{:S(2)}, u32[]{:S(2)}) collective-permute-start(bf16[1,180,256]{2,1,0:T(8,128)(2,1)S(1)} %get-tuple-element.12), channel_id=1, source_target_pairs={{1,0},{2,1},{3,2},{5,4},{6,5},{7,6},{9,8},{10,9},{11,10},{13,12},{... | collective-permute-start | bytes 276488 | tf_op jit(solution)/shard_map/ppermute | solution.py:29
  91.9 20.2 %collective-permute-done = bf16[1,180,256]{2,1,0:T(8,128)(2,1)S(1)} collective-permute-done((bf16[1,180,256]{2,1,0:T(8,128)(2,1)S(1)}, bf16[1,180,256]{2,1,0:T(8,128)(2,1)S(1)}, u32[]{:S(2)}, u32[]{:S(2)}) %collective-permute-start) | collective-permute-done | bytes 92192 | tf_op jit(solution)/shard_map/ppermute | solution.py:28
  112.1 1.1 collective-permute-start.2
  113.3 7.6 %fusion.15 = bf16[4,720,256]{2,1,0:T(8,128)(2,1)S(1)} fusion(bf16[4,512,256]{2,1,0:T(8,128)(2,1)S(1)} %bitcast.59, f32[512]{0:T(512)S(1)} %compare_select_fusion, s32[512]{0:T(512)S(1)} %fusion.56, pred[512]{0:T(512)(128)(4,1)S(1)} %fusion.53), kind=kOutput, calls=%fused_computation.28 | convolution fusion | flops 760504320 | bytes 2527744 | tf_op jit(solution)/shard_map/pm,imc->ipc/dot_general | solution.py:256
  120.9 1.9 %copy.92 = bf16[4,720,256]{2,0,1:T(4,128)(2,1)} copy(bf16[4,720,256]{2,1,0:T(8,128)(2,1)S(1)} %fusion.15) | data formatting | bytes 2949120 | tf_op jit(solution)/shard_map/convert_element_type | solution.py:258
  122.7 5.3 %all-to-all-start.3 = ((bf16[4,720,256]{2,0,1:T(4,128)(2,1)}), bf16[4,720,256]{2,0,1:T(4,128)(2,1)S(1)}, u32[]{:S(2)}, u32[]{:S(2)}) async-start(bf16[4,720,256]{2,0,1:T(4,128)(2,1)} %copy.92), calls=%async_computation.3 | async-start | bytes 2949120 | tf_op jit(solution)/shard_map/all_to_all | solution.py:259
  129.7 16.6 %disco.1.state_ref = f32[16,180,256]{2,1,0:T(8,128)S(1)} custom-call(bf16[18,208,256]{2,1,0:T(8,128)(2,1)S(1)} %maximum_maximum_fusion.above_ref.here_ref.below_ref, bf16[18,208,256]{2,1,0:T(8,128)(2,1)S(1)} %maximum_maximum_fusion.above_ref.here_ref.below_ref, bf16[18,208,256]{2,1,0:T(8,128)(2,1)S(1)} %maximum_maximum_fusion.above_ref.here_ref.below_ref, ...), custom_call_target="tpu_custom_call" | custom-call | flops 6039797760 | bytes 12582912 | tf_op jit(solution)/shard_map/disco/pallas_call | solution.py:140
  146.3 1.6 copy-done.1
  149.0 12.7 %mlp.1 = f32[16,180,256]{2,1,0:T(8,128)S(1)} custom-call(f32[16,180,256]{2,1,0:T(8,128)} %copy-done.1, bf16[16,180,256]{2,1,0:T(8,128)(2,1)S(1)} %bitcast.48, f32[1,256]{1,0:T(1,128)S(1)} %get-tuple-element.13.gain_ref, bf16[256,512]{1,0:T(8,128)(2,1)S(1)} %bitcast.49, bf16[512,256]{1,0:T(8,128)(2,1)S(1)} %bitcast.50), custom_call_target="tpu_custom_call" | custom-call | tf_op jit(solution)/shard_map/mlp/pallas_call | solution.py:174
  161.7 2.5 %copy.95 = f32[16,180,256]{2,0,1:T(8,128)} copy(f32[16,180,256]{2,1,0:T(8,128)S(1)} %mlp.1) | data formatting | bytes 5898240 | tf_op jit(solution)/shard_map/mlp/pallas_call | solution.py:174
  (60 shorter events, 5.5 us)
Async XLA Ops:
  0.0 128.0 %copy-start = (f32[1,16,24,8]{2,3,1,0:T(8,128)S(1)}, f32[1,16,24,8]{2,3,1,0:T(8,128)}, u32[]{:S(2)}) copy-start(f32[1,16,24,8]{2,3,1,0:T(8,128)} %param.11) | copy-start | bytes 36868
  0.0 2.8 %copy-start.5 = (f32[16,180,256]{2,0,1:T(8,128)S(1)}, f32[16,180,256]{2,0,1:T(8,128)}, u32[]{:S(2)}) copy-start(f32[16,180,256]{2,0,1:T(8,128)} %param.9) | copy-start | bytes 8847364
  2.8 3.7 %copy-start.8 = (f32[1,2,256]{2,1,0:T(2,128)S(1)}, f32[1,2,256]{2,1,0:T(2,128)}, u32[]{:S(2)}) copy-start(f32[1,2,256]{2,1,0:T(2,128)} %param.10) | copy-start | bytes 6148
  9.2 21.8 %all-to-all-start = ((bf16[16,180,256]{2,1,0:T(8,128)(2,1)}), bf16[16,180,256]{2,1,0:T(8,128)(2,1)S(1)}, u32[]{:S(2)}, u32[]{:S(2)}) async-start(bf16[16,180,256]{2,1,0:T(8,128)(2,1)} %multiply_convert_fusion.2), calls=%async_computation | async-start | bytes 3014656 | tf_op jit(solution)/shard_map/all_to_all | solution.py:203
  41.2 29.5 %all-to-all-start.1 = ((bf16[4,512,256]{2,0,1:T(4,128)(2,1)}), bf16[4,512,256]{2,0,1:T(4,128)(2,1)S(1)}, u32[]{:S(2)}, u32[]{:S(2)}) async-start(bf16[4,512,256]{2,0,1:T(4,128)(2,1)} %copy.84), calls=%async_computation.1 | async-start | bytes 2097152 | tf_op jit(solution)/shard_map/all_to_all | solution.py:243
  70.8 1.0 copy-start.10
  79.2 7.1 %copy-start.6 = (bf16[16,180,256]{2,1,0:T(8,128)(2,1)S(1)}, bf16[16,180,256]{2,1,0:T(8,128)(2,1)}, u32[]{:S(2)}) copy-start(bf16[16,180,256]{2,1,0:T(8,128)(2,1)} %multiply_convert_fusion.2) | copy-start | bytes 4423684
  79.2 12.6 %copy-start.9 = (s32[16]{0:T(128)S(1)}, s32[16]{0:T(128)}, u32[]{:S(2)}) copy-start(s32[16]{0:T(128)} %param.13) | copy-start | bytes 196
  79.2 12.7 %copy-start.7 = (s32[16,24]{1,0:T(8,128)S(1)}, s32[16,24]{1,0:T(8,128)}, u32[]{:S(2)}) copy-start(s32[16,24]{1,0:T(8,128)} %param.12) | copy-start | bytes 4612
  79.2 34.0 %all-to-all-start.2 = ((bf16[64,32,256]{2,1,0:T(8,128)(2,1)}), bf16[64,32,256]{2,1,0:T(8,128)(2,1)S(1)}, u32[]{:S(2)}, u32[]{:S(2)}) async-start(bf16[64,32,256]{2,1,0:T(8,128)(2,1)} %bitcast.56), calls=%async_computation.2 | async-start | bytes 2097152 | tf_op jit(solution)/shard_map/all_to_all | solution.py:255
  86.3 25.8 %collective-permute-start = (bf16[1,180,256]{2,1,0:T(8,128)(2,1)S(1)}, bf16[1,180,256]{2,1,0:T(8,128)(2,1)S(1)}, u32[]{:S(2)}, u32[]{:S(2)}) collective-permute-start(bf16[1,180,256]{2,1,0:T(8,128)(2,1)S(1)} %get-tuple-element.11), channel_id=1, source_target_pairs={{0,1},{1,2},{2,3},{4,5},{5,6},{6,7},{8,9},{9,10},{10,11},{12,13},{... | collective-permute-start | bytes 276488 | tf_op jit(solution)/shard_map/ppermute | solution.py:28
  89.4 22.7 %collective-permute-start.1 = (bf16[1,180,256]{2,1,0:T(8,128)(2,1)S(1)}, bf16[1,180,256]{2,1,0:T(8,128)(2,1)S(1)}, u32[]{:S(2)}, u32[]{:S(2)}) collective-permute-start(bf16[1,180,256]{2,1,0:T(8,128)(2,1)S(1)} %get-tuple-element.12), channel_id=1, source_target_pairs={{1,0},{2,1},{3,2},{5,4},{6,5},{7,6},{9,8},{10,9},{11,10},{13,12},{... | collective-permute-start | bytes 276488 | tf_op jit(solution)/shard_map/ppermute | solution.py:29
  112.1 16.4 %collective-permute-start.2 = (bf16[18,8,256]{2,1,0:T(8,128)(2,1)S(1)}, bf16[18,8,256]{2,1,0:T(8,128)(2,1)S(1)}, u32[]{:S(2)}, u32[]{:S(2)}) collective-permute-start(bf16[18,8,256]{2,1,0:T(8,128)(2,1)S(1)} %get-tuple-element.9), channel_id=1, source_target_pairs={{0,4},{4,8},{8,12},{12,0},{1,5},{5,9},{9,13},{13,1},{2,6},{6,10},{... | collective-permute-start | bytes 221192 | tf_op jit(solution)/shard_map/ppermute | solution.py:28
  113.2 15.3 %collective-permute-start.3 = (bf16[18,8,256]{2,1,0:T(8,128)(2,1)S(1)}, bf16[18,8,256]{2,1,0:T(8,128)(2,1)S(1)}, u32[]{:S(2)}, u32[]{:S(2)}) collective-permute-start(bf16[18,8,256]{2,1,0:T(8,128)(2,1)S(1)} %get-tuple-element.10), channel_id=1, source_target_pairs={{4,0},{8,4},{12,8},{0,12},{5,1},{9,5},{13,9},{1,13},{6,2},{10,6},{... | collective-permute-start | bytes 221192 | tf_op jit(solution)/shard_map/ppermute | solution.py:29
  122.7 25.2 %all-to-all-start.3 = ((bf16[4,720,256]{2,0,1:T(4,128)(2,1)}), bf16[4,720,256]{2,0,1:T(4,128)(2,1)S(1)}, u32[]{:S(2)}, u32[]{:S(2)}) async-start(bf16[4,720,256]{2,0,1:T(4,128)(2,1)} %copy.92), calls=%async_computation.3 | async-start | bytes 2949120 | tf_op jit(solution)/shard_map/all_to_all | solution.py:259
  128.5 1.2 copy-start.4
  146.3 1.6 copy-start.1
  147.9 0.9 copy-start.2
  147.9 1.0 copy-start.3

commit v2 on v1

--- a/solution.py
+++ b/solution.py
@@ -16,6 +16,8 @@
 WIDTH = 64
 REACH = WIDTH + 2 * R
 LANES = 256
+STEP = 30
+CUTS = 2
 
 exact_prec = lax.Precision.HIGHEST
 
@@ -106,9 +108,8 @@
     )(jnp.broadcast_to(orders, shape), jnp.broadcast_to(cosine, shape), diagonal)
 
 
-def disco_body(above_ref, here_ref, below_ref, base_ref, mix_ref, state_ref, out_ref, band_ref):
-    cols = state_ref.shape[1]
-    channels = state_ref.shape[2]
+def disco_body(above_ref, here_ref, below_ref, base_ref, mix_ref, out_ref, band_ref):
+    cols = out_ref.shape[1]
     for k in range(K):
         row = jnp.broadcast_to(base_ref[0, k : k + 1, :], (WIDTH, LANES))
         band = pltpu.roll(row, 0, 1, stride=1, stride_axis=0)
@@ -126,12 +127,12 @@
     mixed = jnp.dot(
         jnp.concatenate(pieces, axis=0), mix_ref[...], preferred_element_type=jnp.float32
     )
-    out_ref[0] = state_ref[0] + mixed[:cols]
-
-
-def disco_update(extended, base, mix, state):
-    rows, cols, channels = state.shape
-    width = extended.shape[1]
+    out_ref[0] = mixed[:cols]
+
+
+def disco_update(extended, base, mix, cols):
+    rows = base.shape[0]
+    width, channels = extended.shape[1:]
 
     def ext_spec(offset):
         return pl.BlockSpec((1, width, channels), lambda i: (i + offset, 0, 0))
@@ -146,46 +147,47 @@
             ext_spec(2),
             pl.BlockSpec((1, K, LANES), lambda i: (i, 0, 0)),
             pl.BlockSpec(mix.shape, lambda i: (0, 0)),
-            cell,
         ],
         out_specs=cell,
-        out_shape=jax.ShapeDtypeStruct(state.shape, jnp.float32),
+        out_shape=jax.ShapeDtypeStruct((rows, cols, channels), jnp.float32),
         scratch_shapes=[pltpu.VMEM((K * WIDTH, LANES), jnp.bfloat16)],
         compiler_params=pltpu.CompilerParams(vmem_limit_bytes=48 * 2**20),
         cost_estimate=pl.CostEstimate(
             flops=2 * rows * cols * K * channels * 512, bytes_accessed=12 * 2**20, transcendentals=0
         ),
         name="disco",
-    )(extended, extended, extended, base, mix, state)
-
-
-def mlp_body(state_ref, spectral_ref, gain_ref, in_ref, out_mat_ref, out_ref):
-    state = state_ref[0] + spectral_ref[0].astype(jnp.float32)
+    )(extended, extended, extended, base, mix)
+
+
+def mlp_body(state_ref, disco_ref, *refs):
+    *spectral_refs, gain_ref, in_ref, out_mat_ref, out_ref = refs
+    cells = state_ref.shape[0] * state_ref.shape[1]
+    channels = state_ref.shape[2]
+    spectral = jnp.concatenate([ref[...].astype(jnp.float32) for ref in spectral_refs], axis=2)
+    state = (state_ref[...] + disco_ref[...] + spectral).reshape(cells, channels)
     normed = layer_norm(state, gain_ref[...]).astype(jnp.bfloat16)
     hidden = jax.nn.gelu(jnp.dot(normed, in_ref[...], preferred_element_type=jnp.float32))
-    out_ref[0] = state + jnp.dot(
+    state = state + jnp.dot(
         hidden.astype(jnp.bfloat16), out_mat_ref[...], preferred_element_type=jnp.float32
     )
-
-
-def mlp_update(state, spectral, gain, mat_in, mat_out):
-    rows, cols, channels = state.shape
-    cell = pl.BlockSpec((1, cols, channels), lambda i: (i, 0, 0))
+    out_ref[...] = state.reshape(out_ref.shape)
+
+
+def mlp_update(state, disco, spectral, gain, mat_in, mat_out):
+    cols, rows, channels = state.shape
+    step = max(size for size in range(1, STEP + 1) if cols % size == 0)
+    cell = pl.BlockSpec((step, rows, channels), lambda i: (i, 0, 0))
     return pl.pallas_call(
         mlp_body,
-        grid=(rows,),
-        in_specs=[
-            cell,
-            cell,
-            pl.BlockSpec(gain.shape, lambda i: (0, 0)),
-            pl.BlockSpec(mat_in.shape, lambda i: (0, 0)),
-            pl.BlockSpec(mat_out.shape, lambda i: (0, 0)),
-        ],
+        grid=(cols // step,),
+        in_specs=[cell, cell]
+        + [pl.BlockSpec((step, rows, part.shape[2]), lambda i: (i, 0, 0)) for part in spectral]
+        + [pl.BlockSpec(mat.shape, lambda i: (0, 0)) for mat in (gain, mat_in, mat_out)],
         out_specs=cell,
         out_shape=jax.ShapeDtypeStruct(state.shape, jnp.float32),
         compiler_params=pltpu.CompilerParams(vmem_limit_bytes=48 * 2**20),
         name="mlp",
-    )(state, spectral, gain, mat_in, mat_out)
+    )(state, disco, *spectral, gain, mat_in, mat_out)
 
 
 def local(state, norm_gain, disco_kernel, taps, counts, disco_mix, filter_gain, mlp_in, mlp_out):
@@ -200,7 +202,13 @@
     tap_span = 2 * R + 1
 
     normed = layer_norm(state, norm_gain[0, 0]).astype(jnp.bfloat16)
-    whole_rows = lax.all_to_all(normed, "lon", split_axis=0, concat_axis=1, tiled=True)
+    cut = channels // CUTS
+    whole_rows = [
+        lax.all_to_all(
+            normed[:, :, n * cut : (n + 1) * cut], "lon", split_axis=0, concat_axis=1, tiled=True
+        )
+        for n in range(CUTS)
+    ]
 
     slot_ids = jnp.arange(2 * M, dtype=jnp.int32)
     imaginary = slot_ids // modes_own % 2 == 1
@@ -235,29 +243,36 @@
     extended = jnp.concatenate(
         [west, extended, east, jnp.zeros((lat_rows + 2, spare, channels), jnp.bfloat16)], axis=1
     )
-    partial = disco_update(extended, base, disco_mix[0], state)
-
-    spectrum = jnp.einsum(
-        "mp,ipc->imc", analysis, whole_rows, preferred_element_type=jnp.float32
-    ).astype(jnp.bfloat16)
-    owned = lax.all_to_all(spectrum, ("lat", "lon"), split_axis=1, concat_axis=0, tiled=True)
-    owned = owned.reshape(lat_total, 2, modes_own, channels)
-    coefficient = jnp.einsum(
-        "lmj,jrmc->mlrc", weighted, owned, preferred_element_type=jnp.float32
-    )
-    scaled = (coefficient * filter_gain[0][None, :, None, :]).astype(jnp.bfloat16)
-    filtered = jnp.einsum(
-        "lmj,mlrc->mjrc", legendre, scaled, preferred_element_type=jnp.float32
-    ).astype(jnp.bfloat16)
-    filtered = jnp.transpose(filtered, (1, 2, 0, 3)).reshape(
-        lat_total, 2 * modes_own, channels
-    )
-    returned = lax.all_to_all(filtered, ("lat", "lon"), split_axis=0, concat_axis=1, tiled=True)
-    spectral = jnp.einsum(
-        "pm,imc->ipc", synthesis, returned, preferred_element_type=jnp.float32
-    ).astype(jnp.bfloat16)
-    spectral = lax.all_to_all(spectral, "lon", split_axis=1, concat_axis=0, tiled=True)
-    return mlp_update(partial, spectral, norm_gain[0, 1:2], mlp_in[0], mlp_out[0])
+    disco = jnp.transpose(disco_update(extended, base, disco_mix[0], lon_cols), (1, 0, 2))
+
+    spectral = []
+    for n in range(CUTS):
+        gain = filter_gain[0, :, n * cut : (n + 1) * cut]
+        spectrum = jnp.einsum(
+            "mp,ipc->imc", analysis, whole_rows[n], preferred_element_type=jnp.float32
+        ).astype(jnp.bfloat16)
+        owned = lax.all_to_all(spectrum, ("lat", "lon"), split_axis=1, concat_axis=0, tiled=True)
+        owned = owned.reshape(lat_total, 2, modes_own, cut)
+        coefficient = jnp.einsum(
+            "lmj,jrmc->mlrc", weighted, owned, preferred_element_type=jnp.float32
+        )
+        scaled = (coefficient * gain[None, :, None, :]).astype(jnp.bfloat16)
+        filtered = jnp.einsum(
+            "lmj,mlrc->mjrc", legendre, scaled, preferred_element_type=jnp.float32
+        ).astype(jnp.bfloat16)
+        filtered = jnp.transpose(filtered, (1, 2, 0, 3)).reshape(lat_total, 2 * modes_own, cut)
+        returned = lax.all_to_all(
+            filtered, ("lat", "lon"), split_axis=0, concat_axis=1, tiled=True
+        )
+        restored = jnp.einsum(
+            "pm,imc->ipc", synthesis, returned, preferred_element_type=jnp.float32
+        ).astype(jnp.bfloat16)
+        restored = lax.all_to_all(restored, "lon", split_axis=1, concat_axis=0, tiled=True)
+        spectral.append(jnp.transpose(restored, (1, 0, 2)))
+    result = mlp_update(
+        jnp.transpose(state, (1, 0, 2)), disco, spectral, norm_gain[0, 1:2], mlp_in[0], mlp_out[0]
+    )
+    return jnp.transpose(result, (1, 0, 2))
 
 
 def solution(mesh):

time: 166 us -> 193 us (1.16)
  waiting for transfers between devices: 57 us -> 10.8 us
  local copies, waits for them, and re-layouts: 13.6 us -> 45.9 us
  starting transfers between devices: 29.8 us -> 53.4 us
  matrix products: 20.9 us -> 37.9 us
  Pallas kernels: 32.1 us -> 25.8 us
  other arithmetic: 10.5 us -> 15.9 us
    ppermute x2, waiting for transfers between devices: 20.2 us -> 0.01 us  [halo(): lax.ppermute(tail, axis, [(i, (i + 1) % count) for i in range(ends)])]
    all_to_all x1 -> x2, waiting for transfers between devices: 19.3 us -> 0.01 us  [local(): lax.all_to_all(spectrum, ('lat', 'lon'), split_axis=1, concat_axis=0, til...]
    all_to_all x2 -> x4, starting transfers between devices: 9.68 us -> 22.1 us  [the longest x2 11.1 us: local(): lax.all_to_all(normed[:, :, n * cut:(n + 1) * cut], 'lon', split_axis=0,...]
    all_to_all x3 -> x8, local copies, waits for them, and re-layouts: 0.61 us -> 12.4 us  [the longest x4 8.19 us: local(): lax.all_to_all(normed[:, :, n * cut:(n + 1) * cut], 'lon', split_axis=0,...]
    dot_general x1 -> x2, matrix products: 8.28 us -> 16.9 us  [local(): jnp.einsum('mp,ipc->imc', analysis, whole_rows[n], preferred_element_type...]
    all_to_all x2 -> x4, waiting for transfers between devices: 17.5 us -> 9.49 us  [the longest x2 9.49 us: local(): lax.all_to_all(normed[:, :, n * cut:(n + 1) * cut], 'lon', split_axis=0,...]
    convert_element_type x2 -> x6, local copies, waits for them, and re-layouts: 3.3 us -> 11.1 us  [the longest x2 3.2 us: local(): spectrum = jnp.einsum('mp,ipc->imc', analysis, whole_rows[n], preferred_e...]
    dot_general x1 -> x2, matrix products: 7.6 us -> 14.2 us  [local(): jnp.einsum('pm,imc->ipc', synthesis, returned, preferred_element_type=jnp...]
  transfers between devices with their start and end apart: 8 -> 12, of which waited for: 3 -> 2; matrix products, arithmetic and copies ran while one was open for 7% -> 42% of each run, Pallas kernels for 12% -> 10%
where the time goes in v2:
time: 193 us; the launch traced here: 190 us
  starting transfers between devices  53.4 us (28%)
  local copies, waits for them, and re-layouts  45.9 us (24%)
  matrix products  37.9 us (20%)
  Pallas kernels  25.8 us (13%)
  other arithmetic  15.9 us (8%)
  waiting for transfers between devices  10.8 us (6%)
    dot_general x2, matrix products, local(): jnp.einsum('mp,ipc->imc', analysis, whole_rows[n], preferred_element_type...  16.9 us
    pallas_call x1, Pallas kernels, disco_update(): pl.pallas_call(disco_body, grid=(rows,), in_specs=[ext_spec(0), ext_spec(...  15.4 us
    dot_general x2, matrix products, local(): jnp.einsum('pm,imc->ipc', synthesis, returned, preferred_element_type=jnp...  14.2 us
    all_to_all x2, starting transfers between devices, local(): lax.all_to_all(filtered, ('lat', 'lon'), split_axis=0, concat_axis=1, til...  13.2 us
    all_to_all x2, starting transfers between devices, local(): lax.all_to_all(spectrum, ('lat', 'lon'), split_axis=1, concat_axis=0, til...  12.1 us
    all_to_all x2, starting transfers between devices, local(): lax.all_to_all(normed[:, :, n * cut:(n + 1) * cut], 'lon', split_axis=0,...  11.1 us
    all_to_all x2, starting transfers between devices, local(): lax.all_to_all(restored, 'lon', split_axis=1, concat_axis=0, tiled=True)  11 us
    all_to_all x2, waiting for transfers between devices, local(): lax.all_to_all(normed[:, :, n * cut:(n + 1) * cut], 'lon', split_axis=0,...  9.49 us
  transfers between devices with their start and end apart: 12, of which 2 were waited for; matrix products, arithmetic and copies ran while one was open for 42% of the time, Pallas kernels for 10%

profile of v2, /device:TPU:19, one launch (start us, length us, event | category | flops | bytes accessed | tf_op | source)
XLA Modules:
  0.0 190.0 jit_solution(9659644062171157146)
XLA Ops:
  3.5 2.5 %multiply_reduce_fusion = f32[16,180]{1,0:T(8,128)S(1)} fusion(f32[16,180,256]{2,0,1:T(8,128)S(1)} %copy-done.1, f32[16,180]{1,0:T(8,128)S(1)} %broadcast_multiply_fusion), kind=kLoop, calls=%fused_computation.4 | loop fusion | flops 2208960 | bytes 2972160 | tf_op jit(solution)/shard_map/reduce_sum | solution.py:37
  9.6 5.0 %all-to-all-start = ((bf16[16,180,128]{2,1,0:T(8,128)(2,1)}), bf16[16,180,128]{2,1,0:T(8,128)(2,1)}, u32[]{:S(2)}, u32[]{:S(2)}) async-start(bf16[16,180,128]{2,1,0:T(8,128)(2,1)} %get-tuple-element.10), calls=%async_computation | async-start | bytes 1507328 | tf_op jit(solution)/shard_map/all_to_all | solution.py:207
  14.6 9.5 %all-to-all-done = bf16[16,180,128]{2,1,0:T(8,128)(2,1)} async-done(((bf16[16,180,128]{2,1,0:T(8,128)(2,1)}), bf16[16,180,128]{2,1,0:T(8,128)(2,1)}, u32[]{:S(2)}, u32[]{:S(2)}) %all-to-all-start) | async-done | bytes 737312 | tf_op jit(solution)/shard_map/all_to_all | solution.py:207
  24.1 6.1 %all-to-all-start.4 = ((bf16[16,180,128]{2,1,0:T(8,128)(2,1)}), bf16[16,180,128]{2,1,0:T(8,128)(2,1)}, u32[]{:S(2)}, u32[]{:S(2)}) async-start(bf16[16,180,128]{2,1,0:T(8,128)(2,1)} %get-tuple-element.9), calls=%async_computation.4 | async-start | bytes 1507328 | tf_op jit(solution)/shard_map/all_to_all | solution.py:207
  35.5 8.1 %fusion.18 = bf16[4,512,128]{1,2,0:T(8,128)(2,1)S(1)} fusion(bf16[4,720,128]{2,1,0:T(8,128)(2,1)} %all_to_all.103, s32[512]{0:T(512)S(1)} %fusion.57, pred[512]{0:T(512)(128)(4,1)S(1)} %fusion.54), kind=kOutput, calls=%fused_computation.36 | convolution fusion | flops 382541824 | bytes 1264128 | tf_op jit(solution)/shard_map/mp,ipc->imc/dot_general | solution.py:251
  44.6 6.1 %all-to-all-start.1 = ((bf16[4,512,128]{2,0,1:T(4,128)(2,1)}), bf16[4,512,128]{2,0,1:T(4,128)(2,1)S(1)}, u32[]{:S(2)}, u32[]{:S(2)}) async-start(bf16[4,512,128]{2,0,1:T(4,128)(2,1)} %copy.125), calls=%async_computation.1 | async-start | bytes 1048576 | tf_op jit(solution)/shard_map/all_to_all | solution.py:254
  56.5 8.8 %fusion.19 = bf16[4,512,128]{1,2,0:T(8,128)(2,1)} fusion(bf16[4,720,128]{2,1,0:T(8,128)(2,1)} %all_to_all.118, s32[512]{0:T(512)} %copy-done.13, pred[512]{0:T(512)(128)(4,1)} %copy-done.16), kind=kOutput, calls=%fused_computation.37 | convolution fusion | flops 382541824 | bytes 1264128 | tf_op jit(solution)/shard_map/mp,ipc->imc/dot_general | solution.py:251
  68.2 6.0 %all-to-all-start.5 = ((bf16[4,512,128]{2,0,1:T(4,128)(2,1)}), bf16[4,512,128]{2,0,1:T(4,128)(2,1)S(1)}, u32[]{:S(2)}, u32[]{:S(2)}) async-start(bf16[4,512,128]{2,0,1:T(4,128)(2,1)} %copy.137), calls=%async_computation.5 | async-start | bytes 1048576 | tf_op jit(solution)/shard_map/all_to_all | solution.py:254
  74.3 2.7 %legendre.1 = f32[256,16,64]{2,1,0:T(8,128)S(1)} custom-call(f32[16,64]{1,0:T(8,128)S(1)} %broadcast_in_dim.47.orders_ref, f32[16,64]{1,0:T(8,128)S(1)} %broadcast_in_dim.48.cosine_ref, f32[16,64]{1,0:T(8,128)S(1)} %add_exponential_fusion.diagonal_ref), custom_call_target="tpu_custom_call" | custom-call | flops 10485760 | bytes 2097152 | tf_op jit(solution)/shard_map/legendre/pallas_call | solution.py:100
  78.7 2.8 %copy.148 = bf16[256,16,64,1]{0,2,3,1:T(8,128)(2,1)} copy(bf16[256,16,64,1]{2,1,0,3:T(8,128)(2,1)} %get-tuple-element.5) | data formatting | bytes 1048576 | tf_op jit(solution)/shard_map/convert_element_type | solution.py:228
  81.5 2.8 %copy.149 = bf16[256,16,64,1]{0,2,3,1:T(8,128)(2,1)} copy(bf16[256,16,64,1]{2,1,0,3:T(8,128)(2,1)} %get-tuple-element.6) | data formatting | bytes 1048576 | tf_op jit(solution)/shard_map/convert_element_type | solution.py:229
  87.9 3.3 %fusion.16 = bf16[64,2,16,128]{3,0,1,2:T(8,128)(2,1)} fusion(bf16[256,16,64,1]{0,2,3,1:T(8,128)(2,1)} %copy.149, bf16[256,16,64,1]{0,2,3,1:T(8,128)(2,1)} %copy.148, f32[256,128]{1,0:T(8,128)} %get-tuple-element.14, bf16[64,2,16,128]{3,2,1,0:T(8,128)(2,1)} %bitcast.112), kind=kOutput, calls=%fused_computation.34 | convolution fusion | flops 270794752 | bytes 2228224 | tf_op jit(solution)/shard_map/lmj,mlrc->mjrc/dot_general | solution.py:260
  94.2 6.0 %all-to-all-start.2 = ((bf16[64,32,128]{2,1,0:T(8,128)(2,1)}), bf16[64,32,128]{2,1,0:T(8,128)(2,1)S(1)}, u32[]{:S(2)}, u32[]{:S(2)}) async-start(bf16[64,32,128]{2,1,0:T(8,128)(2,1)} %bitcast.107), calls=%async_computation.2 | async-start | bytes 1048576 | tf_op jit(solution)/shard_map/all_to_all | solution.py:264
  101.8 3.1 %collective-permute-start = (bf16[1,180,256]{2,1,0:T(8,128)(2,1)}, bf16[1,180,256]{2,1,0:T(8,128)(2,1)}, u32[]{:S(2)}, u32[]{:S(2)}) collective-permute-start(bf16[1,180,256]{2,1,0:T(8,128)(2,1)} %get-tuple-element.11), channel_id=1, source_target_pairs={{0,1},{1,2},{2,3},{4,5},{5,6},{6,7},{8,9},{9,10},{10,11},{12,13},{... | collective-permute-start | bytes 276488 | tf_op jit(solution)/shard_map/ppermute | solution.py:30
  109.1 3.3 %fusion.17 = bf16[64,2,16,128]{3,0,1,2:T(8,128)(2,1)} fusion(bf16[256,16,64,1]{0,2,3,1:T(8,128)(2,1)} %copy.149, bf16[256,16,64,1]{0,2,3,1:T(8,128)(2,1)} %copy.148, f32[256,128]{1,0:T(8,128)} %get-tuple-element.13, bf16[64,2,16,128]{3,2,1,0:T(8,128)(2,1)} %bitcast.110), kind=kOutput, calls=%fused_computation.35 | convolution fusion | flops 270794752 | bytes 2228224 | tf_op jit(solution)/shard_map/lmj,mlrc->mjrc/dot_general | solution.py:260
  114.6 7.2 %all-to-all-start.6 = ((bf16[64,32,128]{2,1,0:T(8,128)(2,1)}), bf16[64,32,128]{2,1,0:T(8,128)(2,1)}, u32[]{:S(2)}, u32[]{:S(2)}) async-start(bf16[64,32,128]{2,1,0:T(8,128)(2,1)} %bitcast.106), calls=%async_computation.6 | async-start | bytes 1048576 | tf_op jit(solution)/shard_map/all_to_all | solution.py:264
  124.1 7.1 %fusion.14 = bf16[4,720,128]{2,1,0:T(8,128)(2,1)S(1)} fusion(bf16[4,512,128]{2,1,0:T(8,128)(2,1)S(1)} %bitcast.113, f32[512]{0:T(512)S(1)} %compare_select_fusion, s32[512]{0:T(512)S(1)} %copy-done.14, pred[512]{0:T(512)(128)(4,1)S(1)} %copy-done.17), kind=kOutput, calls=%fused_computation.32 | convolution fusion | flops 382648320 | bytes 1266176 | tf_op jit(solution)/shard_map/pm,imc->ipc/dot_general | solution.py:267
  133.7 6.8 %all-to-all-start.3 = ((bf16[4,720,128]{2,0,1:T(4,128)(2,1)}), bf16[4,720,128]{2,0,1:T(4,128)(2,1)}, u32[]{:S(2)}, u32[]{:S(2)}) async-start(bf16[4,720,128]{2,0,1:T(4,128)(2,1)} %copy.133), calls=%async_computation.3 | async-start | bytes 1474560 | tf_op jit(solution)/shard_map/all_to_all | solution.py:270
  140.5 3.5 %maximum_maximum_fusion.above_ref.here_ref.below_ref = bf16[18,208,256]{2,1,0:T(8,128)(2,1)} fusion(bf16[18,8,256]{2,1,0:T(8,128)(2,1)S(1)} %collective-permute-done.3, bf16[1,180,256]{2,1,0:T(8,128)(2,1)} %collective-permute-done.1, bf16[16,180,256]{2,1,0:T(8,128)(2,1)} %copy-done.7, bf16[1,180,256]{2,1,0:T(8,128)(2,1)} %collective-permute-done, ...), kind=kLoop, calls=%fused_computation.9 | loop fusion | flops 11501568 | bytes 3723680 | tf_op jit(solution)/shard_map/concatenate | solution.py:243
  145.1 7.1 %fusion.15 = bf16[4,720,128]{2,1,0:T(8,128)(2,1)S(1)} fusion(bf16[4,512,128]{2,1,0:T(8,128)(2,1)S(1)} %bitcast.111, f32[512]{0:T(512)S(1)} %compare_select_fusion, s32[512]{0:T(512)S(1)} %copy-done.14, pred[512]{0:T(512)(128)(4,1)S(1)} %copy-done.17), kind=kOutput, calls=%fused_computation.33 | convolution fusion | flops 382648320 | bytes 1266176 | tf_op jit(solution)/shard_map/pm,imc->ipc/dot_general | solution.py:267
  153.3 4.2 %all-to-all-start.7 = ((bf16[4,720,128]{2,0,1:T(4,128)(2,1)}), bf16[4,720,128]{2,0,1:T(4,128)(2,1)}, u32[]{:S(2)}, u32[]{:S(2)}) async-start(bf16[4,720,128]{2,0,1:T(4,128)(2,1)} %copy.145), calls=%async_computation.7 | async-start | bytes 1474560 | tf_op jit(solution)/shard_map/all_to_all | solution.py:270
  160.3 15.4 %disco.1 = f32[16,180,256]{2,1,0:T(8,128)S(1)} custom-call(bf16[18,208,256]{2,1,0:T(8,128)(2,1)S(1)} %copy-done.3, bf16[18,208,256]{2,1,0:T(8,128)(2,1)S(1)} %copy-done.3, bf16[18,208,256]{2,1,0:T(8,128)(2,1)S(1)} %copy-done.3, f32[16,8,256]{2,1,0:T(8,128)S(1)} %convolution_bitcast_fusion.base_ref, bf16[2048,256]{1,0:T(8,128)(2,1)S(1)} %bitcast.99), custom_call_target="tpu_custom_call" | custom-call | flops 6039797760 | bytes 12582912 | tf_op jit(solution)/shard_map/disco/pallas_call | solution.py:141
  175.7 2.5 %copy.178 = f32[16,180,256]{2,0,1:T(8,128)} copy(f32[16,180,256]{2,1,0:T(8,128)S(1)} %disco.1) | data formatting | bytes 5898240 | tf_op jit(solution)/shard_map/disco/pallas_call | solution.py:141
  182.4 7.6 %mlp.1 = f32[180,16,256]{2,1,0:T(8,128)} custom-call(f32[180,16,256]{2,1,0:T(8,128)S(1)} %bitcast.94, f32[180,16,256]{2,1,0:T(8,128)} %bitcast.100, bf16[180,16,128]{2,1,0:T(8,128)(2,1)S(1)} %bitcast.95, bf16[180,16,128]{2,1,0:T(8,128)(2,1)S(1)} %bitcast.96, f32[1,256]{1,0:T(1,128)S(1)} %get-tuple-element.15.refs_2_, bf16[256,512]{1,0:T(8,128)(2,1)S(1)} %bitcast.97, ...), custom_call_target="tpu_custom_call" | custom-call | tf_op jit(solution)/shard_map/mlp/pallas_call | solution.py:180
  (100 shorter events, 52.4 us)
Async XLA Ops:
  0.0 122.0 %copy-start = (f32[1,16,24,8]{2,3,1,0:T(8,128)S(1)}, f32[1,16,24,8]{2,3,1,0:T(8,128)}, u32[]{:S(2)}) copy-start(f32[1,16,24,8]{2,3,1,0:T(8,128)} %param.11) | copy-start | bytes 36868
  0.8 2.7 %copy-start.1 = (f32[16,180,256]{2,0,1:T(8,128)S(1)}, f32[16,180,256]{2,0,1:T(8,128)}, u32[]{:S(2)}) copy-start(f32[16,180,256]{2,0,1:T(8,128)} %param.9) | copy-start | bytes 8847364
  9.6 14.5 %all-to-all-start = ((bf16[16,180,128]{2,1,0:T(8,128)(2,1)}), bf16[16,180,128]{2,1,0:T(8,128)(2,1)}, u32[]{:S(2)}, u32[]{:S(2)}) async-start(bf16[16,180,128]{2,1,0:T(8,128)(2,1)} %get-tuple-element.10), calls=%async_computation | async-start | bytes 1507328 | tf_op jit(solution)/shard_map/all_to_all | solution.py:207
  14.6 20.9 %copy-start.16 = (pred[512]{0:T(512)(128)(4,1)}, pred[512]{0:T(512)(128)(4,1)S(1)}, u32[]{:S(2)}) copy-start(pred[512]{0:T(512)(128)(4,1)S(1)} %fusion.54) | copy-start | bytes 1540
  24.1 20.5 %all-to-all-start.4 = ((bf16[16,180,128]{2,1,0:T(8,128)(2,1)}), bf16[16,180,128]{2,1,0:T(8,128)(2,1)}, u32[]{:S(2)}, u32[]{:S(2)}) async-start(bf16[16,180,128]{2,1,0:T(8,128)(2,1)} %get-tuple-element.9), calls=%async_computation.4 | async-start | bytes 1507328 | tf_op jit(solution)/shard_map/all_to_all | solution.py:207
  31.4 4.1 %copy-start.13 = (s32[512]{0:T(512)}, s32[512]{0:T(512)S(1)}, u32[]{:S(2)}) copy-start(s32[512]{0:T(512)S(1)} %fusion.57) | copy-start | bytes 6148
  44.6 22.8 %all-to-all-start.1 = ((bf16[4,512,128]{2,0,1:T(4,128)(2,1)}), bf16[4,512,128]{2,0,1:T(4,128)(2,1)S(1)}, u32[]{:S(2)}, u32[]{:S(2)}) async-start(bf16[4,512,128]{2,0,1:T(4,128)(2,1)} %copy.125), calls=%async_computation.1 | async-start | bytes 1048576 | tf_op jit(solution)/shard_map/all_to_all | solution.py:254
  68.2 25.2 %all-to-all-start.5 = ((bf16[4,512,128]{2,0,1:T(4,128)(2,1)}), bf16[4,512,128]{2,0,1:T(4,128)(2,1)S(1)}, u32[]{:S(2)}, u32[]{:S(2)}) async-start(bf16[4,512,128]{2,0,1:T(4,128)(2,1)} %copy.137), calls=%async_computation.5 | async-start | bytes 1048576 | tf_op jit(solution)/shard_map/all_to_all | solution.py:254
  94.2 20.4 %all-to-all-start.2 = ((bf16[64,32,128]{2,1,0:T(8,128)(2,1)}), bf16[64,32,128]{2,1,0:T(8,128)(2,1)S(1)}, u32[]{:S(2)}, u32[]{:S(2)}) async-start(bf16[64,32,128]{2,1,0:T(8,128)(2,1)} %bitcast.107), calls=%async_computation.2 | async-start | bytes 1048576 | tf_op jit(solution)/shard_map/all_to_all | solution.py:264
  101.8 20.6 %collective-permute-start = (bf16[1,180,256]{2,1,0:T(8,128)(2,1)}, bf16[1,180,256]{2,1,0:T(8,128)(2,1)}, u32[]{:S(2)}, u32[]{:S(2)}) collective-permute-start(bf16[1,180,256]{2,1,0:T(8,128)(2,1)} %get-tuple-element.11), channel_id=1, source_target_pairs={{0,1},{1,2},{2,3},{4,5},{5,6},{6,7},{8,9},{9,10},{10,11},{12,13},{... | collective-permute-start | bytes 276488 | tf_op jit(solution)/shard_map/ppermute | solution.py:30
  104.9 17.5 %collective-permute-start.1 = (bf16[1,180,256]{2,1,0:T(8,128)(2,1)}, bf16[1,180,256]{2,1,0:T(8,128)(2,1)}, u32[]{:S(2)}, u32[]{:S(2)}) collective-permute-start(bf16[1,180,256]{2,1,0:T(8,128)(2,1)} %get-tuple-element.12), channel_id=1, source_target_pairs={{1,0},{2,1},{3,2},{5,4},{6,5},{7,6},{9,8},{10,9},{11,10},{13,12},{... | collective-permute-start | bytes 276488 | tf_op jit(solution)/shard_map/ppermute | solution.py:31
  112.4 9.4 %copy-start.15 = (s32[16]{0:T(128)S(1)}, s32[16]{0:T(128)}, u32[]{:S(2)}) copy-start(s32[16]{0:T(128)} %param.13) | copy-start | bytes 196
  112.4 9.6 %copy-start.12 = (s32[16,24]{1,0:T(8,128)S(1)}, s32[16,24]{1,0:T(8,128)}, u32[]{:S(2)}) copy-start(s32[16,24]{1,0:T(8,128)} %param.12) | copy-start | bytes 4612
  114.6 7.4 %copy-start.8 = (bf16[64,32,128]{2,1,0:T(8,128)(2,1)}, bf16[64,32,128]{2,1,0:T(8,128)(2,1)S(1)}, u32[]{:S(2)}) copy-start(bf16[64,32,128]{2,1,0:T(8,128)(2,1)S(1)} %all-to-all-done.2) | copy-start | bytes 1572868
  114.6 19.1 %all-to-all-start.6 = ((bf16[64,32,128]{2,1,0:T(8,128)(2,1)}), bf16[64,32,128]{2,1,0:T(8,128)(2,1)}, u32[]{:S(2)}, u32[]{:S(2)}) async-start(bf16[64,32,128]{2,1,0:T(8,128)(2,1)} %bitcast.106), calls=%async_computation.6 | async-start | bytes 1048576 | tf_op jit(solution)/shard_map/all_to_all | solution.py:264
  122.0 2.1 %copy-start.9 = (bf16[64,32,128]{2,1,0:T(8,128)(2,1)S(1)}, bf16[64,32,128]{2,1,0:T(8,128)(2,1)}, u32[]{:S(2)}) copy-start(bf16[64,32,128]{2,1,0:T(8,128)(2,1)} %copy-done.8) | copy-start | bytes 1572868
  122.4 1.8 copy-start.14
  122.4 1.8 copy-start.17
  123.4 17.1 %collective-permute-start.2 = (bf16[18,8,256]{2,1,0:T(8,128)(2,1)S(1)}, bf16[18,8,256]{2,1,0:T(8,128)(2,1)S(1)}, u32[]{:S(2)}, u32[]{:S(2)}) collective-permute-start(bf16[18,8,256]{2,1,0:T(8,128)(2,1)S(1)} %get-tuple-element.7), channel_id=1, source_target_pairs={{0,4},{4,8},{8,12},{12,0},{1,5},{5,9},{9,13},{13,1},{2,6},{6,10},{... | collective-permute-start | bytes 221192 | tf_op jit(solution)/shard_map/ppermute | solution.py:30
  124.0 16.5 %collective-permute-start.3 = (bf16[18,8,256]{2,1,0:T(8,128)(2,1)S(1)}, bf16[18,8,256]{2,1,0:T(8,128)(2,1)S(1)}, u32[]{:S(2)}, u32[]{:S(2)}) collective-permute-start(bf16[18,8,256]{2,1,0:T(8,128)(2,1)S(1)} %get-tuple-element.8), channel_id=1, source_target_pairs={{4,0},{8,4},{12,8},{0,12},{5,1},{9,5},{13,9},{1,13},{6,2},{10,6},{... | collective-permute-start | bytes 221192 | tf_op jit(solution)/shard_map/ppermute | solution.py:31
  133.7 19.6 %all-to-all-start.3 = ((bf16[4,720,128]{2,0,1:T(4,128)(2,1)}), bf16[4,720,128]{2,0,1:T(4,128)(2,1)}, u32[]{:S(2)}, u32[]{:S(2)}) async-start(bf16[4,720,128]{2,0,1:T(4,128)(2,1)} %copy.133), calls=%async_computation.3 | async-start | bytes 1474560 | tf_op jit(solution)/shard_map/all_to_all | solution.py:270
  153.3 27.4 %all-to-all-start.7 = ((bf16[4,720,128]{2,0,1:T(4,128)(2,1)}), bf16[4,720,128]{2,0,1:T(4,128)(2,1)}, u32[]{:S(2)}, u32[]{:S(2)}) async-start(bf16[4,720,128]{2,0,1:T(4,128)(2,1)} %copy.145), calls=%async_computation.7 | async-start | bytes 1474560 | tf_op jit(solution)/shard_map/all_to_all | solution.py:270
  180.7 1.7 copy-start.4
  180.7 1.7 copy-start.5
  (6 other events, 7.7 us)

commit v3 on v2

--- a/solution.py
+++ b/solution.py
@@ -1,4 +1,3 @@
-import functools
 import math
 
 import jax
@@ -17,7 +16,7 @@
 REACH = WIDTH + 2 * R
 LANES = 256
 STEP = 30
-CUTS = 2
+CUTS = 1
 
 exact_prec = lax.Precision.HIGHEST
 
@@ -36,12 +35,6 @@
     center = values - jnp.mean(values, axis=-1, keepdims=True)
     spread = jnp.mean(center * center, axis=-1, keepdims=True)
     return center * lax.rsqrt(spread + 1e-05) * gain
-
-
-def trig_table(mode_ids, lon_points, lon_total):
-    product = mode_ids * lon_points % lon_total
-    angles = product.astype(jnp.float32) * (2.0 * math.pi / lon_total)
-    return (jnp.cos(angles), jnp.sin(angles))
 
 
 def colatitudes(lat_count):
@@ -202,6 +195,11 @@
     tap_span = 2 * R + 1
 
     normed = layer_norm(state, norm_gain[0, 0]).astype(jnp.bfloat16)
+    slot_ids = jnp.arange(2 * M, dtype=jnp.int32)
+    imaginary = slot_ids // modes_own % 2 == 1
+    slot_modes = slot_ids // (2 * modes_own) * modes_own + slot_ids % modes_own
+    points = jnp.arange(lon_total, dtype=jnp.int32)
+    normed, slot_modes = lax.optimization_barrier((normed, slot_modes))
     cut = channels // CUTS
     whole_rows = [
         lax.all_to_all(
@@ -209,24 +207,17 @@
         )
         for n in range(CUTS)
     ]
-
-    slot_ids = jnp.arange(2 * M, dtype=jnp.int32)
-    imaginary = slot_ids // modes_own % 2 == 1
-    slot_modes = slot_ids // (2 * modes_own) * modes_own + slot_ids % modes_own
-    points = jnp.arange(lon_total, dtype=jnp.int32)
-    cosine, sine_val = trig_table(slot_modes[:, None], points[None, :], lon_total)
-    analysis = (jnp.where(imaginary[:, None], -sine_val, cosine) / lon_total).astype(jnp.bfloat16)
-    factor = jnp.where(slot_modes == 0, 1.0, 2.0).astype(jnp.float32)
-    cosine, sine_val = trig_table(slot_modes[None, :], points[:, None], lon_total)
-    synthesis = (jnp.where(imaginary[None, :], -sine_val, cosine) * factor[None, :]).astype(
-        jnp.bfloat16
-    )
+    quarter = jnp.where(imaginary, lon_total // 4, 0)
+    steps = (slot_modes[:, None] * points[None, :] + quarter[:, None]) % lon_total
+    waves = jnp.cos(steps.astype(jnp.float32) * (2.0 * math.pi / lon_total)).astype(jnp.bfloat16)
+    waves = lax.optimization_barrier(waves)
 
     own_modes = rank * modes_own + jnp.arange(modes_own, dtype=jnp.int32)
+    factor = jnp.where(own_modes == 0, 1.0, 2.0).astype(jnp.float32)
     legendre = legendre_table(own_modes, lat_total, L)
-    weights = math.pi * jnp.sin(colatitudes(lat_total)) / lat_total
+    weights = math.pi * jnp.sin(colatitudes(lat_total)) / (lat_total * lon_total)
     weighted = (legendre * weights[None, None, :]).astype(jnp.bfloat16)
-    legendre = legendre.astype(jnp.bfloat16)
+    legendre = (legendre * factor[None, :, None]).astype(jnp.bfloat16)
 
     live = jnp.arange(S, dtype=jnp.int32)[None, :] < counts[:, None]
     lanes = taps // tap_span * REACH + taps % tap_span
@@ -249,7 +240,7 @@
     for n in range(CUTS):
         gain = filter_gain[0, :, n * cut : (n + 1) * cut]
         spectrum = jnp.einsum(
-            "mp,ipc->imc", analysis, whole_rows[n], preferred_element_type=jnp.float32
+            "mp,ipc->imc", waves, whole_rows[n], preferred_element_type=jnp.float32
         ).astype(jnp.bfloat16)
         owned = lax.all_to_all(spectrum, ("lat", "lon"), split_axis=1, concat_axis=0, tiled=True)
         owned = owned.reshape(lat_total, 2, modes_own, cut)
@@ -265,7 +256,7 @@
             filtered, ("lat", "lon"), split_axis=0, concat_axis=1, tiled=True
         )
         restored = jnp.einsum(
-            "pm,imc->ipc", synthesis, returned, preferred_element_type=jnp.float32
+            "mp,imc->ipc", waves, returned, preferred_element_type=jnp.float32
         ).astype(jnp.bfloat16)
         restored = lax.all_to_all(restored, "lon", split_axis=1, concat_axis=0, tiled=True)
         spectral.append(jnp.transpose(restored, (1, 0, 2)))

time: 193 us -> 188 us (0.974)
  waiting for transfers between devices: 10.8 us -> 64.9 us
  matrix products: 37.9 us -> 11.3 us
  starting transfers between devices: 53.4 us -> 30.1 us
  local copies, waits for them, and re-layouts: 45.9 us -> 34.5 us
  other arithmetic: 15.9 us -> 18.7 us
    ppermute x2, waiting for transfers between devices: 0.01 us -> 34.9 us  [halo(): lax.ppermute(tail, axis, [(i, (i + 1) % count) for i in range(ends)])]
    dot_general x4 -> x2, matrix products: 31 us -> 4.47 us  [the longest x1 3.54 us: local(): jnp.einsum('mp,ipc->imc', waves, whole_rows[n], preferred_element_type=jn...]
    all_to_all x2 -> x1, waiting for transfers between devices: 0.01 us -> 17.9 us  [local(): lax.all_to_all(spectrum, ('lat', 'lon'), split_axis=1, concat_axis=0, til...]
    convert_element_type x6 -> x2, local copies, waits for them, and re-layouts: 11.1 us -> 4.29 us  [the longest x1 2.38 us: local(): spectrum = jnp.einsum('mp,ipc->imc', waves, whole_rows[n], preferred_elem...]
    convert_element_type x1 -> x2, other arithmetic: 1.59 us -> 8.24 us  [the longest x1 6.56 us: local(): jnp.cos(steps.astype(jnp.float32) * (2.0 * math.pi / lon_total))]
    all_to_all x2 -> x1, starting transfers between devices: 13.2 us -> 7.03 us  [local(): lax.all_to_all(filtered, ('lat', 'lon'), split_axis=0, concat_axis=1, til...]
    all_to_all x2 -> x1, starting transfers between devices: 11.1 us -> 5.14 us  [local(): lax.all_to_all(normed[:, :, n * cut:(n + 1) * cut], 'lon', split_axis=0,...]
    all_to_all x2 -> x1, starting transfers between devices: 11 us -> 5.31 us  [local(): lax.all_to_all(restored, 'lon', split_axis=1, concat_axis=0, tiled=True)]
  transfers between devices with their start and end apart: 12 -> 8, of which waited for: 2 -> 5; matrix products, arithmetic and copies ran while one was open for 42% -> 11% of each run, Pallas kernels for 10% -> 10%
where the time goes in v3:
time: 188 us; the launch traced here: 185 us
  waiting for transfers between devices  64.9 us (35%)
  local copies, waits for them, and re-layouts  34.5 us (18%)
  starting transfers between devices  30.1 us (16%)
  Pallas kernels  25.8 us (14%)
  other arithmetic  18.7 us (10%)
  matrix products  11.3 us (6%)
    ppermute x2, waiting for transfers between devices, halo(): lax.ppermute(tail, axis, [(i, (i + 1) % count) for i in range(ends)])  34.9 us
    all_to_all x1, waiting for transfers between devices, local(): lax.all_to_all(spectrum, ('lat', 'lon'), split_axis=1, concat_axis=0, til...  17.9 us
    pallas_call x1, Pallas kernels, disco_update(): pl.pallas_call(disco_body, grid=(rows,), in_specs=[ext_spec(0), ext_spec(...  15.5 us
    all_to_all x1, waiting for transfers between devices, local(): lax.all_to_all(normed[:, :, n * cut:(n + 1) * cut], 'lon', split_axis=0,...  11 us
    pallas_call x1, Pallas kernels, mlp_update(): pl.pallas_call(mlp_body, grid=(cols // step,), in_specs=[cell, cell] + [p...  7.59 us
    all_to_all x3, local copies, waits for them, and re-layouts, local(): lax.all_to_all(restored, 'lon', split_axis=1, concat_axis=0, tiled=True)  7.47 us
    all_to_all x1, starting transfers between devices, local(): lax.all_to_all(filtered, ('lat', 'lon'), split_axis=0, concat_axis=1, til...  7.03 us
    all_to_all x1, starting transfers between devices, local(): lax.all_to_all(spectrum, ('lat', 'lon'), split_axis=1, concat_axis=0, til...  6.58 us
  transfers between devices with their start and end apart: 8, of which 5 were waited for; matrix products, arithmetic and copies ran while one was open for 11% of the time, Pallas kernels for 10%

profile of v3, /device:TPU:19, one launch (start us, length us, event | category | flops | bytes accessed | tf_op | source)
XLA Modules:
  0.0 185.5 jit_solution(6062738025600751083)
XLA Ops:
  0.0 2.4 %reduce_sum.27 = f32[16,180]{0,1:T(8,128)S(1)} reduce(f32[16,180,256]{2,0,1:T(8,128)} %param.9, f32[]{:T(128)} %constant.110.clone.1), dimensions={2}, to_apply=%region_0.0 | reduce | flops 734400 | bytes 2960644 | tf_op jit(solution)/shard_map/reduce_sum | solution.py:35
  2.8 2.4 %multiply_reduce_fusion = f32[16,180]{1,0:T(8,128)S(1)} fusion(f32[16,180,256]{2,0,1:T(8,128)S(1)} %copy-done.1, f32[16,180]{1,0:T(8,128)S(1)} %broadcast_multiply_fusion), kind=kLoop, calls=%fused_computation.6 | loop fusion | flops 2208960 | bytes 2972160 | tf_op jit(solution)/shard_map/reduce_sum | solution.py:36
  5.2 2.8 %multiply_convert_fusion.2 = bf16[16,180,256]{2,1,0:T(8,128)(2,1)} fusion(f32[16,180,256]{2,0,1:T(8,128)S(1)} %copy-done.1, f32[256]{0:T(256)S(1)} %bitcast.66, f32[16,180]{1,0:T(8,128)S(1)} %add_rsqrt_fusion, f32[16,180]{1,0:T(8,128)S(1)} %broadcast_multiply_fusion), kind=kLoop, calls=%fused_computation.5 | loop fusion | flops 2949120 | bytes 4447744 | tf_op jit(solution)/shard_map/convert_element_type | solution.py:197
  8.0 5.1 %all-to-all-start = ((bf16[16,180,256]{2,1,0:T(8,128)(2,1)}), bf16[16,180,256]{2,1,0:T(8,128)(2,1)}, u32[]{:S(2)}, u32[]{:S(2)}) async-start(bf16[16,180,256]{2,1,0:T(8,128)(2,1)} %multiply_convert_fusion.2), calls=%async_computation | async-start | bytes 3014656 | tf_op jit(solution)/shard_map/all_to_all | solution.py:205
  13.2 6.6 %fusion.8 = bf16[512,720]{0,1:T(8,128)(2,1)} fusion(s32[512]{0:T(512)S(1)} %fusion.44, s32[512]{0:T(512)S(1)} %fusion.37), kind=kLoop, calls=%fused_computation.20 | loop fusion | flops 4055040 | bytes 741376 | tf_op jit(solution)/shard_map/convert_element_type | solution.py:212
  19.7 11.0 %all-to-all-done = bf16[16,180,256]{2,1,0:T(8,128)(2,1)} async-done(((bf16[16,180,256]{2,1,0:T(8,128)(2,1)}), bf16[16,180,256]{2,1,0:T(8,128)(2,1)}, u32[]{:S(2)}, u32[]{:S(2)}) %all-to-all-start) | async-done | bytes 1474592 | tf_op jit(solution)/shard_map/all_to_all | solution.py:205
  30.7 2.6 %copy.116 = bf16[4,4,180,256]{3,2,0,1:T(8,128)(2,1)} copy(bf16[4,4,180,256]{3,2,1,0:T(8,128)(2,1)} %bitcast.8) | data formatting | bytes 2949120 | tf_op jit(solution)/shard_map/all_to_all | solution.py:205
  33.3 3.3 %all_to_all.53 = bf16[4,720,256]{2,1,0:T(8,128)(2,1)} reshape(bf16[4,4,180,256]{3,2,1,0:T(8,128)(2,1)} %bitcast.60) | data formatting | bytes 2949120 | tf_op jit(solution)/shard_map/all_to_all | solution.py:205
  36.6 3.5 %fusion.13 = bf16[4,512,256]{1,2,0:T(8,128)(2,1)} fusion(bf16[4,720,256]{2,1,0:T(8,128)(2,1)} %all_to_all.53, bf16[512,720]{0,1:T(8,128)(2,1)} %fusion.8), kind=kOutput, calls=%fused_computation.26 | convolution fusion | flops 755499008 | bytes 3260416 | tf_op jit(solution)/shard_map/mp,ipc->imc/dot_general | solution.py:242
  42.5 6.6 %all-to-all-start.1 = ((bf16[4,512,256]{2,0,1:T(4,128)(2,1)}), bf16[4,512,256]{2,0,1:T(4,128)(2,1)}, u32[]{:S(2)}, u32[]{:S(2)}) async-start(bf16[4,512,256]{2,0,1:T(4,128)(2,1)} %copy.80), calls=%async_computation.1 | async-start | bytes 2097152 | tf_op jit(solution)/shard_map/all_to_all | solution.py:245
  49.6 2.7 %legendre.1 = f32[256,16,64]{2,1,0:T(8,128)S(1)} custom-call(f32[16,64]{1,0:T(8,128)S(1)} %broadcast_in_dim.29.orders_ref, f32[16,64]{1,0:T(8,128)S(1)} %broadcast_in_dim.30.cosine_ref, f32[16,64]{1,0:T(8,128)S(1)} %add_exponential_fusion.diagonal_ref), custom_call_target="tpu_custom_call" | custom-call | flops 10485760 | bytes 2097152 | tf_op jit(solution)/shard_map/legendre/pallas_call | solution.py:93
  54.1 17.9 %all-to-all-done.1 = bf16[4,512,256]{2,0,1:T(4,128)(2,1)} async-done(((bf16[4,512,256]{2,0,1:T(4,128)(2,1)}), bf16[4,512,256]{2,0,1:T(4,128)(2,1)}, u32[]{:S(2)}, u32[]{:S(2)}) %all-to-all-start.1) | async-done | bytes 1048608 | tf_op jit(solution)/shard_map/all_to_all | solution.py:245
  74.4 6.5 %fusion.14 = bf16[64,2,16,256]{3,0,1,2:T(8,128)(2,1)} fusion(f32[256,256]{1,0:T(8,128)S(1)} %bitcast.67, bf16[256,16,64,1]{2,1,0,3:T(8,128)(2,1)} %get-tuple-element.10, bf16[256,16,64,1]{2,1,0,3:T(8,128)(2,1)} %get-tuple-element.9, bf16[64,2,16,256]{3,2,1,0:T(8,128)(2,1)} %bitcast.64), kind=kOutput, calls=%fused_computation.27 | convolution fusion | flops 541589504 | bytes 3407872 | tf_op jit(solution)/shard_map/lmj,mlrc->mjrc/dot_general | solution.py:251
  80.9 2.8 %copy.86 = bf16[64,2,16,256]{3,2,1,0:T(8,128)(2,1)} copy(bf16[64,2,16,256]{3,0,1,2:T(8,128)(2,1)} %fusion.14) | data formatting | bytes 2097152 | tf_op jit(solution)/shard_map/convert_element_type | solution.py:253
  83.8 7.0 %all-to-all-start.2 = ((bf16[64,32,256]{2,1,0:T(8,128)(2,1)}), bf16[64,32,256]{2,1,0:T(8,128)(2,1)}, u32[]{:S(2)}, u32[]{:S(2)}) async-start(bf16[64,32,256]{2,1,0:T(8,128)(2,1)} %bitcast.62), calls=%async_computation.2 | async-start | bytes 2097152 | tf_op jit(solution)/shard_map/all_to_all | solution.py:255
  91.8 3.1 %collective-permute-start = (bf16[1,180,256]{2,1,0:T(8,128)(2,1)S(1)}, bf16[1,180,256]{2,1,0:T(8,128)(2,1)S(1)}, u32[]{:S(2)}, u32[]{:S(2)}) collective-permute-start(bf16[1,180,256]{2,1,0:T(8,128)(2,1)S(1)} %get-tuple-element.14), channel_id=1, source_target_pairs={{0,1},{1,2},{2,3},{4,5},{5,6},{6,7},{8,9},{9,10},{10,11},{12,13},{... | collective-permute-start | bytes 276488 | tf_op jit(solution)/shard_map/ppermute | solution.py:29
  97.4 19.3 %collective-permute-done = bf16[1,180,256]{2,1,0:T(8,128)(2,1)S(1)} collective-permute-done((bf16[1,180,256]{2,1,0:T(8,128)(2,1)S(1)}, bf16[1,180,256]{2,1,0:T(8,128)(2,1)S(1)}, u32[]{:S(2)}, u32[]{:S(2)}) %collective-permute-start) | collective-permute-done | bytes 92192 | tf_op jit(solution)/shard_map/ppermute | solution.py:29
  117.3 2.6 %constant_dynamic-update-slice_fusion.1 = bf16[18,180,256]{2,1,0:T(8,128)(2,1)} fusion(bf16[18,180,256]{2,1,0:T(8,128)(2,1)} %constant_dynamic-update-slice_fusion.2, bf16[16,180,256]{2,1,0:T(8,128)(2,1)} %multiply_convert_fusion.2), kind=kLoop, calls=%fused_computation.48 | loop fusion | bytes 3014656
  124.8 5.3 %all-to-all-start.3 = ((bf16[4,720,256]{2,0,1:T(4,128)(2,1)}), bf16[4,720,256]{2,0,1:T(4,128)(2,1)}, u32[]{:S(2)}, u32[]{:S(2)}) async-start(bf16[4,720,256]{2,0,1:T(4,128)(2,1)} %copy.88), calls=%async_computation.3 | async-start | bytes 2949120 | tf_op jit(solution)/shard_map/all_to_all | solution.py:261
  132.1 15.6 %collective-permute-done.2 = bf16[18,8,256]{2,1,0:T(8,128)(2,1)S(1)} collective-permute-done((bf16[18,8,256]{2,1,0:T(8,128)(2,1)S(1)}, bf16[18,8,256]{2,1,0:T(8,128)(2,1)S(1)}, u32[]{:S(2)}, u32[]{:S(2)}) %collective-permute-start.2) | collective-permute-done | bytes 73760 | tf_op jit(solution)/shard_map/ppermute | solution.py:29
  151.1 15.5 %disco.1 = f32[16,180,256]{2,1,0:T(8,128)S(1)} custom-call(bf16[18,208,256]{2,1,0:T(8,128)(2,1)S(1)} %maximum_maximum_fusion.above_ref.here_ref.below_ref, bf16[18,208,256]{2,1,0:T(8,128)(2,1)S(1)} %maximum_maximum_fusion.above_ref.here_ref.below_ref, bf16[18,208,256]{2,1,0:T(8,128)(2,1)S(1)} %maximum_maximum_fusion.above_ref.here_ref.below_ref, ...), custom_call_target="tpu_custom_call" | custom-call | flops 6039797760 | bytes 12582912 | tf_op jit(solution)/shard_map/disco/pallas_call | solution.py:134
  166.5 2.5 %copy.114 = f32[16,180,256]{2,0,1:T(8,128)} copy(f32[16,180,256]{2,1,0:T(8,128)S(1)} %disco.1) | data formatting | bytes 5898240 | tf_op jit(solution)/shard_map/disco/pallas_call | solution.py:134
  172.8 3.7 %all_to_all.64 = bf16[16,180,256]{2,0,1:T(8,128)(2,1)} reshape(bf16[4,4,180,256]{3,1,0,2:T(4,128)(2,1)} %copy.90) | data formatting | bytes 2949120 | tf_op jit(solution)/shard_map/all_to_all | solution.py:261
  177.9 7.6 %mlp.1 = f32[180,16,256]{2,1,0:T(8,128)} custom-call(f32[180,16,256]{2,1,0:T(8,128)S(1)} %bitcast.54, f32[180,16,256]{2,1,0:T(8,128)} %bitcast.59, bf16[180,16,256]{2,1,0:T(8,128)(2,1)S(1)} %bitcast.55, f32[1,256]{1,0:T(1,128)S(1)} %get-tuple-element.15.refs_1_, bf16[256,512]{1,0:T(8,128)(2,1)S(1)} %bitcast.56, bf16[512,256]{1,0:T(8,128)(2,1)S(1)} %bitcast.57), custom_call_target="tpu_custom_call" | custom-call | tf_op jit(solution)/shard_map/mlp/pallas_call | solution.py:173
  (65 shorter events, 26.8 us)
Async XLA Ops:
  0.0 131.7 %copy-start = (f32[1,16,24,8]{2,3,1,0:T(8,128)S(1)}, f32[1,16,24,8]{2,3,1,0:T(8,128)}, u32[]{:S(2)}) copy-start(f32[1,16,24,8]{2,3,1,0:T(8,128)} %param.11) | copy-start | bytes 36868
  0.0 2.8 %copy-start.1 = (f32[16,180,256]{2,0,1:T(8,128)S(1)}, f32[16,180,256]{2,0,1:T(8,128)}, u32[]{:S(2)}) copy-start(f32[16,180,256]{2,0,1:T(8,128)} %param.9) | copy-start | bytes 8847364
  2.5 2.7 %copy-start.8 = (f32[1,2,256]{2,1,0:T(2,128)S(1)}, f32[1,2,256]{2,1,0:T(2,128)}, u32[]{:S(2)}) copy-start(f32[1,2,256]{2,1,0:T(2,128)} %param.10) | copy-start | bytes 6148
  8.0 22.7 %all-to-all-start = ((bf16[16,180,256]{2,1,0:T(8,128)(2,1)}), bf16[16,180,256]{2,1,0:T(8,128)(2,1)}, u32[]{:S(2)}, u32[]{:S(2)}) async-start(bf16[16,180,256]{2,1,0:T(8,128)(2,1)} %multiply_convert_fusion.2), calls=%async_computation | async-start | bytes 3014656 | tf_op jit(solution)/shard_map/all_to_all | solution.py:205
  42.5 29.5 %all-to-all-start.1 = ((bf16[4,512,256]{2,0,1:T(4,128)(2,1)}), bf16[4,512,256]{2,0,1:T(4,128)(2,1)}, u32[]{:S(2)}, u32[]{:S(2)}) async-start(bf16[4,512,256]{2,0,1:T(4,128)(2,1)} %copy.80), calls=%async_computation.1 | async-start | bytes 2097152 | tf_op jit(solution)/shard_map/all_to_all | solution.py:245
  54.1 20.4 %copy-start.10 = (f32[1,256,256]{2,1,0:T(8,128)S(1)}, f32[1,256,256]{2,1,0:T(8,128)}, u32[]{:S(2)}) copy-start(f32[1,256,256]{2,1,0:T(8,128)} %param.15) | copy-start | bytes 786436
  80.9 16.3 %copy-start.7 = (s32[16,24]{1,0:T(8,128)S(1)}, s32[16,24]{1,0:T(8,128)}, u32[]{:S(2)}) copy-start(s32[16,24]{1,0:T(8,128)} %param.12) | copy-start | bytes 4612
  80.9 16.3 %copy-start.9 = (s32[16]{0:T(128)S(1)}, s32[16]{0:T(128)}, u32[]{:S(2)}) copy-start(s32[16]{0:T(128)} %param.13) | copy-start | bytes 196
  83.8 36.8 %all-to-all-start.2 = ((bf16[64,32,256]{2,1,0:T(8,128)(2,1)}), bf16[64,32,256]{2,1,0:T(8,128)(2,1)}, u32[]{:S(2)}, u32[]{:S(2)}) async-start(bf16[64,32,256]{2,1,0:T(8,128)(2,1)} %bitcast.62), calls=%async_computation.2 | async-start | bytes 2097152 | tf_op jit(solution)/shard_map/all_to_all | solution.py:255
  91.8 24.9 %collective-permute-start = (bf16[1,180,256]{2,1,0:T(8,128)(2,1)S(1)}, bf16[1,180,256]{2,1,0:T(8,128)(2,1)S(1)}, u32[]{:S(2)}, u32[]{:S(2)}) collective-permute-start(bf16[1,180,256]{2,1,0:T(8,128)(2,1)S(1)} %get-tuple-element.14), channel_id=1, source_target_pairs={{0,1},{1,2},{2,3},{4,5},{5,6},{6,7},{8,9},{9,10},{10,11},{12,13},{... | collective-permute-start | bytes 276488 | tf_op jit(solution)/shard_map/ppermute | solution.py:29
  94.9 25.0 %collective-permute-start.1 = (bf16[1,180,256]{2,1,0:T(8,128)(2,1)S(1)}, bf16[1,180,256]{2,1,0:T(8,128)(2,1)S(1)}, u32[]{:S(2)}, u32[]{:S(2)}) collective-permute-start(bf16[1,180,256]{2,1,0:T(8,128)(2,1)S(1)} %get-tuple-element.13), channel_id=1, source_target_pairs={{1,0},{2,1},{3,2},{5,4},{6,5},{7,6},{9,8},{10,9},{11,10},{13,12},{... | collective-permute-start | bytes 276488 | tf_op jit(solution)/shard_map/ppermute | solution.py:30
  120.5 1.4 copy-start.6
  124.8 44.2 %all-to-all-start.3 = ((bf16[4,720,256]{2,0,1:T(4,128)(2,1)}), bf16[4,720,256]{2,0,1:T(4,128)(2,1)}, u32[]{:S(2)}, u32[]{:S(2)}) async-start(bf16[4,720,256]{2,0,1:T(4,128)(2,1)} %copy.88), calls=%async_computation.3 | async-start | bytes 2949120 | tf_op jit(solution)/shard_map/all_to_all | solution.py:261
  131.1 16.6 %collective-permute-start.2 = (bf16[18,8,256]{2,1,0:T(8,128)(2,1)S(1)}, bf16[18,8,256]{2,1,0:T(8,128)(2,1)S(1)}, u32[]{:S(2)}, u32[]{:S(2)}) collective-permute-start(bf16[18,8,256]{2,1,0:T(8,128)(2,1)S(1)} %get-tuple-element.11), channel_id=1, source_target_pairs={{0,4},{4,8},{8,12},{12,0},{1,5},{5,9},{9,13},{13,1},{2,6},{6,10},{... | collective-permute-start | bytes 221192 | tf_op jit(solution)/shard_map/ppermute | solution.py:29
  131.2 17.6 %collective-permute-start.3 = (bf16[18,8,256]{2,1,0:T(8,128)(2,1)S(1)}, bf16[18,8,256]{2,1,0:T(8,128)(2,1)S(1)}, u32[]{:S(2)}, u32[]{:S(2)}) collective-permute-start(bf16[18,8,256]{2,1,0:T(8,128)(2,1)S(1)} %get-tuple-element.12), channel_id=1, source_target_pairs={{4,0},{8,4},{12,8},{0,12},{5,1},{9,5},{13,9},{1,13},{6,2},{10,6},{... | collective-permute-start | bytes 221192 | tf_op jit(solution)/shard_map/ppermute | solution.py:30
  132.0 19.0 %copy-start.5 = (bf16[1,2048,256]{2,1,0:T(8,128)(2,1)S(1)}, bf16[1,2048,256]{2,1,0:T(8,128)(2,1)}, u32[]{:S(2)}) copy-start(bf16[1,2048,256]{2,1,0:T(8,128)(2,1)} %param.14) | copy-start | bytes 3145732
  172.8 3.7 %copy-start.3 = (bf16[1,256,512]{2,1,0:T(8,128)(2,1)S(1)}, bf16[1,256,512]{2,1,0:T(8,128)(2,1)}, u32[]{:S(2)}) copy-start(bf16[1,256,512]{2,1,0:T(8,128)(2,1)} %param.16) | copy-start | bytes 786436
  172.8 3.7 %copy-start.4 = (bf16[1,512,256]{2,1,0:T(8,128)(2,1)S(1)}, bf16[1,512,256]{2,1,0:T(8,128)(2,1)}, u32[]{:S(2)}) copy-start(bf16[1,512,256]{2,1,0:T(8,128)(2,1)} %param.17) | copy-start | bytes 786436
  176.5 1.4 copy-start.2

commit v4 on v3

--- a/solution.py
+++ b/solution.py
@@ -16,7 +16,6 @@
 REACH = WIDTH + 2 * R
 LANES = 256
 STEP = 30
-CUTS = 1
 
 exact_prec = lax.Precision.HIGHEST
 
@@ -152,6 +151,25 @@
     )(extended, extended, extended, base, mix)
 
 
+def norm_body(state_ref, gain_ref, out_ref):
+    out_ref[...] = layer_norm(state_ref[...], gain_ref[...][None]).astype(jnp.bfloat16)
+
+
+def norm_update(state, gain):
+    cols, rows, channels = state.shape
+    step = max(size for size in range(1, STEP + 1) if cols % size == 0)
+    cell = pl.BlockSpec((step, rows, channels), lambda i: (i, 0, 0))
+    return pl.pallas_call(
+        norm_body,
+        grid=(cols // step,),
+        in_specs=[cell, pl.BlockSpec(gain.shape, lambda i: (0, 0))],
+        out_specs=cell,
+        out_shape=jax.ShapeDtypeStruct(state.shape, jnp.bfloat16),
+        compiler_params=pltpu.CompilerParams(vmem_limit_bytes=48 * 2**20),
+        name="norm",
+    )(state, gain)
+
+
 def mlp_body(state_ref, disco_ref, *refs):
     *spectral_refs, gain_ref, in_ref, out_mat_ref, out_ref = refs
     cells = state_ref.shape[0] * state_ref.shape[1]
@@ -194,19 +212,21 @@
     modes_own = M // parts
     tap_span = 2 * R + 1
 
-    normed = layer_norm(state, norm_gain[0, 0]).astype(jnp.bfloat16)
+    share = lat_rows // lon_parts
+    turned = jnp.transpose(state, (1, 0, 2))
+    normed = norm_update(turned, norm_gain[0, 0:1])
+
     slot_ids = jnp.arange(2 * M, dtype=jnp.int32)
     imaginary = slot_ids // modes_own % 2 == 1
     slot_modes = slot_ids // (2 * modes_own) * modes_own + slot_ids % modes_own
     points = jnp.arange(lon_total, dtype=jnp.int32)
     normed, slot_modes = lax.optimization_barrier((normed, slot_modes))
-    cut = channels // CUTS
-    whole_rows = [
-        lax.all_to_all(
-            normed[:, :, n * cut : (n + 1) * cut], "lon", split_axis=0, concat_axis=1, tiled=True
-        )
-        for n in range(CUTS)
-    ]
+    sent = jnp.transpose(normed.reshape(lon_cols, lon_parts, share, channels), (1, 0, 2, 3))
+    whole_rows = lax.all_to_all(sent, "lon", split_axis=0, concat_axis=0, tiled=True)
+    whole_rows = whole_rows.reshape(lon_total, share, channels)
+    normed = jnp.transpose(normed, (1, 0, 2))
+    above, below = halo(normed, "lat", 0, 1, False)
+    whole_rows, above, below = lax.optimization_barrier((whole_rows, above, below))
     quarter = jnp.where(imaginary, lon_total // 4, 0)
     steps = (slot_modes[:, None] * points[None, :] + quarter[:, None]) % lon_total
     waves = jnp.cos(steps.astype(jnp.float32) * (2.0 * math.pi / lon_total)).astype(jnp.bfloat16)
@@ -226,43 +246,38 @@
         "isq,isk->ikq", matches.astype(jnp.float32), disco_kernel[0], precision=exact_prec
     )
 
-    above, below = halo(normed, "lat", 0, 1, False)
     extended = jnp.concatenate([above, normed, below], axis=0)
     west, east = halo(extended, "lon", 1, R, True)
     blocks = -(-lon_cols // WIDTH)
     spare = blocks * WIDTH - lon_cols
+
+    spectrum = jnp.einsum(
+        "mp,pic->mic", waves, whole_rows, preferred_element_type=jnp.float32
+    ).astype(jnp.bfloat16)
+    owned = lax.all_to_all(spectrum, ("lat", "lon"), split_axis=0, concat_axis=0, tiled=True)
+    owned, west, east = lax.optimization_barrier((owned, west, east))
     extended = jnp.concatenate(
         [west, extended, east, jnp.zeros((lat_rows + 2, spare, channels), jnp.bfloat16)], axis=1
     )
     disco = jnp.transpose(disco_update(extended, base, disco_mix[0], lon_cols), (1, 0, 2))
-
-    spectral = []
-    for n in range(CUTS):
-        gain = filter_gain[0, :, n * cut : (n + 1) * cut]
-        spectrum = jnp.einsum(
-            "mp,ipc->imc", waves, whole_rows[n], preferred_element_type=jnp.float32
-        ).astype(jnp.bfloat16)
-        owned = lax.all_to_all(spectrum, ("lat", "lon"), split_axis=1, concat_axis=0, tiled=True)
-        owned = owned.reshape(lat_total, 2, modes_own, cut)
-        coefficient = jnp.einsum(
-            "lmj,jrmc->mlrc", weighted, owned, preferred_element_type=jnp.float32
-        )
-        scaled = (coefficient * gain[None, :, None, :]).astype(jnp.bfloat16)
-        filtered = jnp.einsum(
-            "lmj,mlrc->mjrc", legendre, scaled, preferred_element_type=jnp.float32
-        ).astype(jnp.bfloat16)
-        filtered = jnp.transpose(filtered, (1, 2, 0, 3)).reshape(lat_total, 2 * modes_own, cut)
-        returned = lax.all_to_all(
-            filtered, ("lat", "lon"), split_axis=0, concat_axis=1, tiled=True
-        )
-        restored = jnp.einsum(
-            "mp,imc->ipc", waves, returned, preferred_element_type=jnp.float32
-        ).astype(jnp.bfloat16)
-        restored = lax.all_to_all(restored, "lon", split_axis=1, concat_axis=0, tiled=True)
-        spectral.append(jnp.transpose(restored, (1, 0, 2)))
-    result = mlp_update(
-        jnp.transpose(state, (1, 0, 2)), disco, spectral, norm_gain[0, 1:2], mlp_in[0], mlp_out[0]
-    )
+    owned = owned.reshape(parts, 2, modes_own, share, channels)
+    owned = jnp.transpose(owned, (2, 0, 3, 1, 4)).reshape(modes_own, lat_total, 2, channels)
+    coefficient = jnp.einsum(
+        "lmj,mjrc->mlrc", weighted, owned, preferred_element_type=jnp.float32
+    )
+    scaled = (coefficient * filter_gain[0][None, :, None, :]).astype(jnp.bfloat16)
+    filtered = jnp.einsum(
+        "lmj,mlrc->mjrc", legendre, scaled, preferred_element_type=jnp.float32
+    ).astype(jnp.bfloat16)
+    filtered = jnp.transpose(filtered, (1, 2, 0, 3)).reshape(lat_total, 2 * modes_own, channels)
+    returned = lax.all_to_all(filtered, ("lat", "lon"), split_axis=0, concat_axis=1, tiled=True)
+    restored = jnp.einsum(
+        "mp,imc->pic", waves, returned, preferred_element_type=jnp.float32
+    ).astype(jnp.bfloat16)
+    restored = restored.reshape(lon_parts, lon_cols, share, channels)
+    spectral = lax.all_to_all(restored, "lon", split_axis=0, concat_axis=0, tiled=True)
+    spectral = jnp.transpose(spectral, (1, 0, 2, 3)).reshape(lon_cols, lat_rows, channels)
+    result = mlp_update(turned, disco, [spectral], norm_gain[0, 1:2], mlp_in[0], mlp_out[0])
     return jnp.transpose(result, (1, 0, 2))
 
 

time: 188 us -> 148 us (0.79)
  waiting for transfers between devices: 64.9 us -> 44.8 us
  local copies, waits for them, and re-layouts: 34.5 us -> 24.9 us
  other arithmetic: 18.7 us -> 9.64 us
    ppermute x2, waiting for transfers between devices: 34.9 us -> 0.21 us  [halo(): lax.ppermute(tail, axis, [(i, (i + 1) % count) for i in range(ends)])]
    all_to_all x1, waiting for transfers between devices: 0.01 us -> 22.7 us  [local(): lax.all_to_all(filtered, ('lat', 'lon'), split_axis=0, concat_axis=1, til...]
    all_to_all x7 -> x0, local copies, waits for them, and re-layouts: 15.8 us -> none  [the longest x3 7.47 us: local(): lax.all_to_all(restored, 'lon', split_axis=1, concat_axis=0, tiled=True)]
    all_to_all x3, waiting for transfers between devices: 28.9 us -> 18.8 us  [the longest x1 14 us: local(): lax.all_to_all(spectrum, ('lat', 'lon'), split_axis=0, concat_axis=0, til...]
    reshape x0 -> x5, local copies, waits for them, and re-layouts: none -> 9.26 us  [the longest x1 3.76 us: local(): jnp.transpose(spectral, (1, 0, 2, 3)).reshape(lon_cols, lat_rows, channels)]
    reduce_sum x2 -> x0, other arithmetic: 4.84 us -> none  [the longest x1 2.44 us: layer_norm(): center = values - jnp.mean(values, axis=-1, keepdims=True)]
    convert_element_type x1 -> x0, other arithmetic: 2.83 us -> none  [local(): normed = layer_norm(state, norm_gain[0, 0]).astype(jnp.bfloat16)]
    transpose x0 -> x2, local copies, waits for them, and re-layouts: none -> 2.68 us  [the longest x1 1.62 us: local(): jnp.transpose(spectral, (1, 0, 2, 3)).reshape(lon_cols, lat_rows, channels)]
  transfers between devices with their start and end apart: 8 -> 8, of which waited for: 5 -> 5; matrix products, arithmetic and copies ran while one was open for 11% -> 10% of each run, Pallas kernels for 10% -> 12%
where the time goes in v4:
time: 148 us; the launch traced here: 147 us
  waiting for transfers between devices  44.8 us (30%)
  starting transfers between devices  30.9 us (21%)
  Pallas kernels  27.1 us (18%)
  local copies, waits for them, and re-layouts  24.9 us (17%)
  other arithmetic  9.64 us (7%)
  matrix products  9.47 us (6%)
    all_to_all x1, waiting for transfers between devices, local(): lax.all_to_all(filtered, ('lat', 'lon'), split_axis=0, concat_axis=1, til...  22.7 us
    pallas_call x1, Pallas kernels, disco_update(): pl.pallas_call(disco_body, grid=(rows,), in_specs=[ext_spec(0), ext_spec(...  15.4 us
    all_to_all x1, waiting for transfers between devices, local(): lax.all_to_all(spectrum, ('lat', 'lon'), split_axis=0, concat_axis=0, til...  14 us
    pallas_call x1, Pallas kernels, mlp_update(): pl.pallas_call(mlp_body, grid=(cols // step,), in_specs=[cell, cell] + [p...  7.54 us
    all_to_all x1, starting transfers between devices, local(): lax.all_to_all(filtered, ('lat', 'lon'), split_axis=0, concat_axis=1, til...  6.93 us
    convert_element_type x1, other arithmetic, local(): jnp.cos(steps.astype(jnp.float32) * (2.0 * math.pi / lon_total))  6.61 us
    all_to_all x1, starting transfers between devices, local(): lax.all_to_all(spectrum, ('lat', 'lon'), split_axis=0, concat_axis=0, til...  6.58 us
    all_to_all x1, starting transfers between devices, local(): lax.all_to_all(restored, 'lon', split_axis=0, concat_axis=0, tiled=True)  6.39 us
  transfers between devices with their start and end apart: 8, of which 5 were waited for; matrix products, arithmetic and copies ran while one was open for 10% of the time, Pallas kernels for 12%

profile of v4, /device:TPU:19, one launch (start us, length us, event | category | flops | bytes accessed | tf_op | source)
XLA Modules:
  0.0 147.0 jit_solution(5431621249845766510)
XLA Ops:
  0.8 1.8 %copy-done.1 = f32[16,180,256]{2,0,1:T(8,128)S(1)} copy-done((f32[16,180,256]{2,0,1:T(8,128)S(1)}, f32[16,180,256]{2,0,1:T(8,128)}, u32[]{:S(2)}) %copy-start.1) | copy-done | bytes 2949144
  6.1 5.1 %all-to-all-start = ((bf16[4,180,4,256]{3,2,1,0:T(4,128)(2,1)}), bf16[4,180,4,256]{3,2,1,0:T(4,128)(2,1)}, u32[]{:S(2)}, u32[]{:S(2)}) async-start(bf16[4,180,4,256]{3,2,1,0:T(4,128)(2,1)} %bitcast.48), calls=%async_computation | async-start | bytes 2949120 | tf_op jit(solution)/shard_map/all_to_all | solution.py:225
  11.7 3.2 %collective-permute-start = (bf16[1,180,256]{2,1,0:T(8,128)(2,1)S(1)}, bf16[1,180,256]{2,1,0:T(8,128)(2,1)S(1)}, u32[]{:S(2)}, u32[]{:S(2)}) collective-permute-start(bf16[1,180,256]{2,1,0:T(8,128)(2,1)S(1)} %get-tuple-element.26), channel_id=1, source_target_pairs={{0,1},{1,2},{2,3},{4,5},{5,6},{6,7},{8,9},{9,10},{10,11},{12,13},{... | collective-permute-start | bytes 276488 | tf_op jit(solution)/shard_map/ppermute | solution.py:28
  14.9 2.1 %collective-permute-start.1 = (bf16[1,180,256]{2,1,0:T(8,128)(2,1)S(1)}, bf16[1,180,256]{2,1,0:T(8,128)(2,1)S(1)}, u32[]{:S(2)}, u32[]{:S(2)}) collective-permute-start(bf16[1,180,256]{2,1,0:T(8,128)(2,1)S(1)} %get-tuple-element.25), channel_id=1, source_target_pairs={{1,0},{2,1},{3,2},{5,4},{6,5},{7,6},{9,8},{10,9},{11,10},{13,12},{... | collective-permute-start | bytes 276488 | tf_op jit(solution)/shard_map/ppermute | solution.py:29
  17.0 6.6 %fusion.8 = bf16[512,720]{0,1:T(8,128)(2,1)} fusion(s32[512]{0:T(512)S(1)} %fusion.42, s32[512]{0:T(512)S(1)} %fusion.35), kind=kLoop, calls=%fused_computation.16 | loop fusion | flops 4055040 | bytes 741376 | tf_op jit(solution)/shard_map/convert_element_type | solution.py:232
  23.6 4.8 %all-to-all-done = bf16[4,180,4,256]{3,2,1,0:T(4,128)(2,1)} async-done(((bf16[4,180,4,256]{3,2,1,0:T(4,128)(2,1)}), bf16[4,180,4,256]{3,2,1,0:T(4,128)(2,1)}, u32[]{:S(2)}, u32[]{:S(2)}) %all-to-all-start) | async-done | bytes 1474592 | tf_op jit(solution)/shard_map/all_to_all | solution.py:225
  28.4 1.6 %copy.81 = bf16[720,4,256]{2,0,1:T(8,128)(2,1)S(1)} copy(bf16[720,4,256]{2,1,0:T(4,128)(2,1)} %bitcast.4) | data formatting | bytes 2949120 | tf_op jit(solution)/shard_map/reshape | solution.py:226
  31.1 1.8 %copy.66 = bf16[512,4,256]{2,1,0:T(4,128)(2,1)} copy(bf16[512,4,256]{2,0,1:T(8,128)(2,1)S(1)} %convolution_convert_fusion.1) | data formatting | bytes 2097152 | tf_op jit(solution)/shard_map/convert_element_type | solution.py:256
  32.9 6.6 %all-to-all-start.1 = ((bf16[512,4,256]{2,1,0:T(4,128)(2,1)}), bf16[512,4,256]{2,1,0:T(4,128)(2,1)S(1)}, u32[]{:S(2)}, u32[]{:S(2)}) async-start(bf16[512,4,256]{2,1,0:T(4,128)(2,1)} %copy.66), calls=%async_computation.1 | async-start | bytes 2097152 | tf_op jit(solution)/shard_map/all_to_all | solution.py:257
  39.9 2.7 %legendre.1 = f32[256,16,64]{2,1,0:T(8,128)S(1)} custom-call(f32[16,64]{1,0:T(8,128)S(1)} %broadcast_in_dim.30.orders_ref, f32[16,64]{1,0:T(8,128)S(1)} %broadcast_in_dim.31.cosine_ref, f32[16,64]{1,0:T(8,128)S(1)} %add_exponential_fusion.diagonal_ref), custom_call_target="tpu_custom_call" | custom-call | flops 10485760 | bytes 2097152 | tf_op jit(solution)/shard_map/legendre/pallas_call | solution.py:92
  43.3 1.7 %fusion.13 = (bf16[256,16,64,1]{2,1,0,3:T(8,128)(2,1)}, bf16[256,16,64,1]{2,1,0,3:T(8,128)(2,1)}) fusion(f32[256,16,64]{2,1,0:T(8,128)S(1)} %legendre.1, f32[16]{0:T(128)S(1)} %get-tuple-element.29, f32[64]{0:T(128)S(1)} %broadcast_multiply_fusion), kind=kLoop, calls=%fused_computation.24 | loop fusion | flops 1048576 | bytes 2097472 | tf_op jit(solution)/shard_map/convert_element_type | solution.py:240
  45.3 3.1 %collective-permute-done.3 = bf16[18,8,256]{2,1,0:T(8,128)(2,1)S(1)} collective-permute-done((bf16[18,8,256]{2,1,0:T(8,128)(2,1)S(1)}, bf16[18,8,256]{2,1,0:T(8,128)(2,1)S(1)}, u32[]{:S(2)}, u32[]{:S(2)}) %collective-permute-start.3) | collective-permute-done | bytes 73760 | tf_op jit(solution)/shard_map/ppermute | solution.py:29
  48.3 14.0 %all-to-all-done.1 = bf16[512,4,256]{2,1,0:T(4,128)(2,1)S(1)} async-done(((bf16[512,4,256]{2,1,0:T(4,128)(2,1)}), bf16[512,4,256]{2,1,0:T(4,128)(2,1)S(1)}, u32[]{:S(2)}, u32[]{:S(2)}) %all-to-all-start.1) | async-done | bytes 1048608 | tf_op jit(solution)/shard_map/all_to_all | solution.py:257
  64.1 6.1 %fusion.12 = bf16[64,2,16,256]{3,0,1,2:T(8,128)(2,1)} fusion(f32[256,256]{1,0:T(8,128)S(1)} %bitcast.65, bf16[256,16,64,1]{2,1,0,3:T(8,128)(2,1)} %get-tuple-element.22, bf16[256,16,64,1]{2,1,0,3:T(8,128)(2,1)S(1)} %copy-done.7, bf16[16,64,2,256]{3,0,2,1:T(8,128)(2,1)} %bitcast.63), kind=kOutput, calls=%fused_computation.22 | convolution fusion | flops 541589504 | bytes 3407872 | tf_op jit(solution)/shard_map/lmj,mlrc->mjrc/dot_general | solution.py:269
  70.2 2.9 %copy.75 = bf16[64,2,16,256]{3,2,1,0:T(8,128)(2,1)} copy(bf16[64,2,16,256]{3,0,1,2:T(8,128)(2,1)} %fusion.12) | data formatting | bytes 2097152 | tf_op jit(solution)/shard_map/convert_element_type | solution.py:271
  73.0 6.9 %all-to-all-start.2 = ((bf16[64,32,256]{2,1,0:T(8,128)(2,1)}), bf16[64,32,256]{2,1,0:T(8,128)(2,1)S(1)}, u32[]{:S(2)}, u32[]{:S(2)}) async-start(bf16[64,32,256]{2,1,0:T(8,128)(2,1)} %bitcast.61), calls=%async_computation.2 | async-start | bytes 2097152 | tf_op jit(solution)/shard_map/all_to_all | solution.py:273
  80.1 22.7 %all-to-all-done.2 = bf16[64,32,256]{2,1,0:T(8,128)(2,1)S(1)} async-done(((bf16[64,32,256]{2,1,0:T(8,128)(2,1)}), bf16[64,32,256]{2,1,0:T(8,128)(2,1)S(1)}, u32[]{:S(2)}, u32[]{:S(2)}) %all-to-all-start.2) | async-done | bytes 1048608 | tf_op jit(solution)/shard_map/all_to_all | solution.py:273
  102.9 2.0 %convolution_convert_fusion = bf16[720,4,256]{2,0,1:T(8,128)(2,1)S(1)} fusion(bf16[4,512,256]{2,1,0:T(8,128)(2,1)S(1)} %bitcast.64, bf16[512,720]{0,1:T(8,128)(2,1)} %fusion.8), kind=kOutput, calls=%fused_computation.9 | convolution fusion | flops 755712000 | bytes 3260416 | tf_op jit(solution)/shard_map/mp,imc->pic/dot_general | solution.py:274
  105.0 1.9 %copy.86 = bf16[720,4,256]{2,1,0:T(4,128)(2,1)} copy(bf16[720,4,256]{2,0,1:T(8,128)(2,1)S(1)} %convolution_convert_fusion) | data formatting | bytes 2949120 | tf_op jit(solution)/shard_map/reshape | solution.py:277
  106.8 6.4 %all-to-all-start.3 = ((bf16[4,180,4,256]{3,2,1,0:T(4,128)(2,1)}), bf16[4,180,4,256]{3,2,1,0:T(4,128)(2,1)S(1)}, u32[]{:S(2)}, u32[]{:S(2)}) async-start(bf16[4,180,4,256]{3,2,1,0:T(4,128)(2,1)} %bitcast.59), calls=%async_computation.3 | async-start | bytes 2949120 | tf_op jit(solution)/shard_map/all_to_all | solution.py:278
  114.8 15.4 %disco.1 = f32[16,180,256]{2,1,0:T(8,128)S(1)} custom-call(bf16[18,208,256]{2,1,0:T(8,128)(2,1)S(1)} %maximum_maximum_fusion.above_ref.here_ref.below_ref, bf16[18,208,256]{2,1,0:T(8,128)(2,1)S(1)} %maximum_maximum_fusion.above_ref.here_ref.below_ref, bf16[18,208,256]{2,1,0:T(8,128)(2,1)S(1)} %maximum_maximum_fusion.above_ref.here_ref.below_ref, ...), custom_call_target="tpu_custom_call" | custom-call | flops 6039797760 | bytes 12582912 | tf_op jit(solution)/shard_map/disco/pallas_call | solution.py:133
  130.2 2.5 %copy.98 = f32[16,180,256]{2,0,1:T(8,128)} copy(f32[16,180,256]{2,1,0:T(8,128)S(1)} %disco.1) | data formatting | bytes 5898240 | tf_op jit(solution)/shard_map/disco/pallas_call | solution.py:133
  134.3 3.8 %reshape.141.refs_0_ = bf16[180,16,256]{2,1,0:T(8,128)(2,1)} reshape(bf16[180,4,4,256]{3,2,1,0:T(4,128)(2,1)} %copy.78) | data formatting | bytes 2949120 | tf_op jit(solution)/shard_map/reshape | solution.py:279
  139.4 7.5 %mlp.1 = f32[180,16,256]{2,1,0:T(8,128)} custom-call(f32[180,16,256]{2,1,0:T(8,128)S(1)} %bitcast.50, f32[180,16,256]{2,1,0:T(8,128)} %bitcast.57, bf16[180,16,256]{2,1,0:T(8,128)(2,1)S(1)} %copy-done.3, f32[1,256]{1,0:T(1,128)S(1)} %get-tuple-element.27.refs_1_, bf16[256,512]{1,0:T(8,128)(2,1)S(1)} %bitcast.51, bf16[512,256]{1,0:T(8,128)(2,1)S(1)} %bitcast.52), custom_call_target="tpu_custom_call" | custom-call | tf_op jit(solution)/shard_map/mlp/pallas_call | solution.py:191
  (60 shorter events, 13.6 us)
Async XLA Ops:
  0.0 113.2 %copy-start = (f32[1,16,24,8]{2,3,1,0:T(8,128)S(1)}, f32[1,16,24,8]{2,3,1,0:T(8,128)}, u32[]{:S(2)}) copy-start(f32[1,16,24,8]{2,3,1,0:T(8,128)} %param.11) | copy-start | bytes 36868
  0.8 1.8 %copy-start.1 = (f32[16,180,256]{2,0,1:T(8,128)S(1)}, f32[16,180,256]{2,0,1:T(8,128)}, u32[]{:S(2)}) copy-start(f32[16,180,256]{2,0,1:T(8,128)} %param.9) | copy-start | bytes 8847364
  6.1 22.4 %all-to-all-start = ((bf16[4,180,4,256]{3,2,1,0:T(4,128)(2,1)}), bf16[4,180,4,256]{3,2,1,0:T(4,128)(2,1)}, u32[]{:S(2)}, u32[]{:S(2)}) async-start(bf16[4,180,4,256]{3,2,1,0:T(4,128)(2,1)} %bitcast.48), calls=%async_computation | async-start | bytes 2949120 | tf_op jit(solution)/shard_map/all_to_all | solution.py:225
  11.7 18.4 %collective-permute-start = (bf16[1,180,256]{2,1,0:T(8,128)(2,1)S(1)}, bf16[1,180,256]{2,1,0:T(8,128)(2,1)S(1)}, u32[]{:S(2)}, u32[]{:S(2)}) collective-permute-start(bf16[1,180,256]{2,1,0:T(8,128)(2,1)S(1)} %get-tuple-element.26), channel_id=1, source_target_pairs={{0,1},{1,2},{2,3},{4,5},{5,6},{6,7},{8,9},{9,10},{10,11},{12,13},{... | collective-permute-start | bytes 276488 | tf_op jit(solution)/shard_map/ppermute | solution.py:28
  14.9 15.2 %collective-permute-start.1 = (bf16[1,180,256]{2,1,0:T(8,128)(2,1)S(1)}, bf16[1,180,256]{2,1,0:T(8,128)(2,1)S(1)}, u32[]{:S(2)}, u32[]{:S(2)}) collective-permute-start(bf16[1,180,256]{2,1,0:T(8,128)(2,1)S(1)} %get-tuple-element.25), channel_id=1, source_target_pairs={{1,0},{2,1},{3,2},{5,4},{6,5},{7,6},{9,8},{10,9},{11,10},{13,12},{... | collective-permute-start | bytes 276488 | tf_op jit(solution)/shard_map/ppermute | solution.py:29
  28.4 1.7 %copy-start.8 = (bf16[512,720]{0,1:T(8,128)(2,1)S(1)}, bf16[512,720]{0,1:T(8,128)(2,1)}, u32[]{:S(2)}) copy-start(bf16[512,720]{0,1:T(8,128)(2,1)} %fusion.8) | copy-start | bytes 2211844
  32.9 29.5 %all-to-all-start.1 = ((bf16[512,4,256]{2,1,0:T(4,128)(2,1)}), bf16[512,4,256]{2,1,0:T(4,128)(2,1)S(1)}, u32[]{:S(2)}, u32[]{:S(2)}) async-start(bf16[512,4,256]{2,1,0:T(4,128)(2,1)} %copy.66), calls=%async_computation.1 | async-start | bytes 2097152 | tf_op jit(solution)/shard_map/all_to_all | solution.py:257
  42.8 2.5 %collective-permute-start.2 = (bf16[18,8,256]{2,1,0:T(8,128)(2,1)S(1)}, bf16[18,8,256]{2,1,0:T(8,128)(2,1)S(1)}, u32[]{:S(2)}, u32[]{:S(2)}) collective-permute-start(bf16[18,8,256]{2,1,0:T(8,128)(2,1)S(1)} %get-tuple-element.24), channel_id=1, source_target_pairs={{0,4},{4,8},{8,12},{12,0},{1,5},{5,9},{9,13},{13,1},{2,6},{6,10},{... | collective-permute-start | bytes 221192 | tf_op jit(solution)/shard_map/ppermute | solution.py:28
  43.3 5.0 %collective-permute-start.3 = (bf16[18,8,256]{2,1,0:T(8,128)(2,1)S(1)}, bf16[18,8,256]{2,1,0:T(8,128)(2,1)S(1)}, u32[]{:S(2)}, u32[]{:S(2)}) collective-permute-start(bf16[18,8,256]{2,1,0:T(8,128)(2,1)S(1)} %get-tuple-element.23), channel_id=1, source_target_pairs={{4,0},{8,4},{12,8},{0,12},{5,1},{9,5},{13,9},{1,13},{6,2},{10,6},{... | collective-permute-start | bytes 221192 | tf_op jit(solution)/shard_map/ppermute | solution.py:29
  45.0 18.5 %copy-start.11 = (f32[1,256,256]{2,1,0:T(8,128)S(1)}, f32[1,256,256]{2,1,0:T(8,128)}, u32[]{:S(2)}) copy-start(f32[1,256,256]{2,1,0:T(8,128)} %param.15) | copy-start | bytes 786436
  62.5 1.6 %copy-start.7 = (bf16[256,16,64,1]{2,1,0,3:T(8,128)(2,1)S(1)}, bf16[256,16,64,1]{2,1,0,3:T(8,128)(2,1)}, u32[]{:S(2)}) copy-start(bf16[256,16,64,1]{2,1,0,3:T(8,128)(2,1)} %get-tuple-element.21) | copy-start | bytes 1572868
  70.2 9.9 %copy-start.10 = (s32[16]{0:T(128)S(1)}, s32[16]{0:T(128)}, u32[]{:S(2)}) copy-start(s32[16]{0:T(128)} %param.13) | copy-start | bytes 196
  70.2 9.9 %copy-start.9 = (s32[16,24]{1,0:T(8,128)S(1)}, s32[16,24]{1,0:T(8,128)}, u32[]{:S(2)}) copy-start(s32[16,24]{1,0:T(8,128)} %param.12) | copy-start | bytes 4612
  73.0 29.8 %all-to-all-start.2 = ((bf16[64,32,256]{2,1,0:T(8,128)(2,1)}), bf16[64,32,256]{2,1,0:T(8,128)(2,1)S(1)}, u32[]{:S(2)}, u32[]{:S(2)}) async-start(bf16[64,32,256]{2,1,0:T(8,128)(2,1)} %bitcast.61), calls=%async_computation.2 | async-start | bytes 2097152 | tf_op jit(solution)/shard_map/all_to_all | solution.py:273
  106.8 25.8 %all-to-all-start.3 = ((bf16[4,180,4,256]{3,2,1,0:T(4,128)(2,1)}), bf16[4,180,4,256]{3,2,1,0:T(4,128)(2,1)S(1)}, u32[]{:S(2)}, u32[]{:S(2)}) async-start(bf16[4,180,4,256]{3,2,1,0:T(4,128)(2,1)} %bitcast.59), calls=%async_computation.3 | async-start | bytes 2949120 | tf_op jit(solution)/shard_map/all_to_all | solution.py:278
  113.6 1.2 copy-start.6
  132.7 5.4 %copy-start.4 = (bf16[1,256,512]{2,1,0:T(8,128)(2,1)S(1)}, bf16[1,256,512]{2,1,0:T(8,128)(2,1)}, u32[]{:S(2)}) copy-start(bf16[1,256,512]{2,1,0:T(8,128)(2,1)} %param.16) | copy-start | bytes 786436
  132.7 5.4 %copy-start.5 = (bf16[1,512,256]{2,1,0:T(8,128)(2,1)S(1)}, bf16[1,512,256]{2,1,0:T(8,128)(2,1)}, u32[]{:S(2)}) copy-start(bf16[1,512,256]{2,1,0:T(8,128)(2,1)} %param.17) | copy-start | bytes 786436
  134.3 3.8 %copy-start.2 = (f32[16,180,256]{2,0,1:T(8,128)S(1)}, f32[16,180,256]{2,0,1:T(8,128)}, u32[]{:S(2)}) copy-start(f32[16,180,256]{2,0,1:T(8,128)} %param.9) | copy-start | bytes 8847364
  138.1 1.4 copy-start.3

commit v5 on v4

--- a/solution.py
+++ b/solution.py
@@ -170,11 +170,12 @@
     )(state, gain)
 
 
-def mlp_body(state_ref, disco_ref, *refs):
-    *spectral_refs, gain_ref, in_ref, out_mat_ref, out_ref = refs
+def mlp_body(state_ref, disco_ref, spectral_ref, gain_ref, in_ref, out_mat_ref, out_ref):
     cells = state_ref.shape[0] * state_ref.shape[1]
     channels = state_ref.shape[2]
-    spectral = jnp.concatenate([ref[...].astype(jnp.float32) for ref in spectral_refs], axis=2)
+    spectral = jnp.concatenate(
+        [spectral_ref[n].astype(jnp.float32) for n in range(spectral_ref.shape[0])], axis=1
+    )
     state = (state_ref[...] + disco_ref[...] + spectral).reshape(cells, channels)
     normed = layer_norm(state, gain_ref[...]).astype(jnp.bfloat16)
     hidden = jax.nn.gelu(jnp.dot(normed, in_ref[...], preferred_element_type=jnp.float32))
@@ -186,19 +187,20 @@
 
 def mlp_update(state, disco, spectral, gain, mat_in, mat_out):
     cols, rows, channels = state.shape
+    lon_parts, share = spectral.shape[0], spectral.shape[2]
     step = max(size for size in range(1, STEP + 1) if cols % size == 0)
     cell = pl.BlockSpec((step, rows, channels), lambda i: (i, 0, 0))
     return pl.pallas_call(
         mlp_body,
         grid=(cols // step,),
         in_specs=[cell, cell]
-        + [pl.BlockSpec((step, rows, part.shape[2]), lambda i: (i, 0, 0)) for part in spectral]
+        + [pl.BlockSpec((lon_parts, step, share, channels), lambda i: (0, i, 0, 0))]
         + [pl.BlockSpec(mat.shape, lambda i: (0, 0)) for mat in (gain, mat_in, mat_out)],
         out_specs=cell,
         out_shape=jax.ShapeDtypeStruct(state.shape, jnp.float32),
         compiler_params=pltpu.CompilerParams(vmem_limit_bytes=48 * 2**20),
         name="mlp",
-    )(state, disco, *spectral, gain, mat_in, mat_out)
+    )(state, disco, spectral, gain, mat_in, mat_out)
 
 
 def local(state, norm_gain, disco_kernel, taps, counts, disco_mix, filter_gain, mlp_in, mlp_out):
@@ -276,8 +278,7 @@
     ).astype(jnp.bfloat16)
     restored = restored.reshape(lon_parts, lon_cols, share, channels)
     spectral = lax.all_to_all(restored, "lon", split_axis=0, concat_axis=0, tiled=True)
-    spectral = jnp.transpose(spectral, (1, 0, 2, 3)).reshape(lon_cols, lat_rows, channels)
-    result = mlp_update(turned, disco, [spectral], norm_gain[0, 1:2], mlp_in[0], mlp_out[0])
+    result = mlp_update(turned, disco, spectral, norm_gain[0, 1:2], mlp_in[0], mlp_out[0])
     return jnp.transpose(result, (1, 0, 2))
 
 

time: 148 us -> 142 us (0.959)
  local copies, waits for them, and re-layouts: 24.9 us -> 18.1 us
    reshape x2 -> x0, local copies, waits for them, and re-layouts: 5.63 us -> none  [the longest x1 3.76 us: local(): jnp.transpose(spectral, (1, 0, 2, 3)).reshape(lon_cols, lat_rows, channels)]
    convert_element_type x0 -> x1, local copies, waits for them, and re-layouts: none -> 1.87 us  [local(): restored = jnp.einsum('mp,imc->pic', waves, returned, preferred_element_t...]
    transpose x1 -> x0, local copies, waits for them, and re-layouts: 1.62 us -> none  [local(): jnp.transpose(spectral, (1, 0, 2, 3)).reshape(lon_cols, lat_rows, channels)]
    unnamed x24 -> x22, local copies, waits for them, and re-layouts: 4.21 us -> 2.85 us
  transfers between devices with their start and end apart: 8 -> 8, of which waited for: 5 -> 5; matrix products, arithmetic and copies ran while one was open for 10% -> 10% of each run, Pallas kernels for 12% -> 13%
where the time goes in v5:
time: 142 us; the launch traced here: 141 us
  waiting for transfers between devices  44.8 us (32%)
  starting transfers between devices  31.7 us (22%)
  Pallas kernels  27.3 us (19%)
  local copies, waits for them, and re-layouts  18.1 us (13%)
  other arithmetic  9.63 us (7%)
  matrix products  9.46 us (7%)
    all_to_all x1, waiting for transfers between devices, local(): lax.all_to_all(filtered, ('lat', 'lon'), split_axis=0, concat_axis=1, til...  22.7 us
    pallas_call x1, Pallas kernels, disco_update(): pl.pallas_call(disco_body, grid=(rows,), in_specs=[ext_spec(0), ext_spec(...  15.4 us
    all_to_all x1, waiting for transfers between devices, local(): lax.all_to_all(spectrum, ('lat', 'lon'), split_axis=0, concat_axis=0, til...  14 us
    pallas_call x1, Pallas kernels, mlp_update(): pl.pallas_call(mlp_body, grid=(cols // step,), in_specs=[cell, cell] + [p...  7.81 us
    all_to_all x1, starting transfers between devices, local(): lax.all_to_all(restored, 'lon', split_axis=0, concat_axis=0, tiled=True)  7.15 us
    all_to_all x1, starting transfers between devices, local(): lax.all_to_all(filtered, ('lat', 'lon'), split_axis=0, concat_axis=1, til...  6.94 us
    convert_element_type x1, other arithmetic, local(): jnp.cos(steps.astype(jnp.float32) * (2.0 * math.pi / lon_total))  6.61 us
    all_to_all x1, starting transfers between devices, local(): lax.all_to_all(spectrum, ('lat', 'lon'), split_axis=0, concat_axis=0, til...  6.58 us
  transfers between devices with their start and end apart: 8, of which 5 were waited for; matrix products, arithmetic and copies ran while one was open for 10% of the time, Pallas kernels for 13%

profile of v5, /device:TPU:19, one launch (start us, length us, event | category | flops | bytes accessed | tf_op | source)
XLA Modules:
  0.0 141.3 jit_solution(3966828284998195861)
XLA Ops:
  0.8 1.8 %copy-done.1 = f32[16,180,256]{2,0,1:T(8,128)S(1)} copy-done((f32[16,180,256]{2,0,1:T(8,128)S(1)}, f32[16,180,256]{2,0,1:T(8,128)}, u32[]{:S(2)}) %copy-start.1) | copy-done | bytes 2949144
  4.4 1.6 %copy.95 = bf16[180,4,4,256]{3,2,0,1:T(4,128)(2,1)} copy(bf16[180,4,4,256]{3,2,1,0:T(4,128)(2,1)S(1)} %reshape.132) | data formatting | bytes 2949120 | tf_op jit(solution)/shard_map/reshape | solution.py:226
  6.1 5.1 %all-to-all-start = ((bf16[4,180,4,256]{3,2,1,0:T(4,128)(2,1)}), bf16[4,180,4,256]{3,2,1,0:T(4,128)(2,1)}, u32[]{:S(2)}, u32[]{:S(2)}) async-start(bf16[4,180,4,256]{3,2,1,0:T(4,128)(2,1)} %bitcast.47), calls=%async_computation | async-start | bytes 2949120 | tf_op jit(solution)/shard_map/all_to_all | solution.py:227
  11.7 3.2 %collective-permute-start = (bf16[1,180,256]{2,1,0:T(8,128)(2,1)S(1)}, bf16[1,180,256]{2,1,0:T(8,128)(2,1)S(1)}, u32[]{:S(2)}, u32[]{:S(2)}) collective-permute-start(bf16[1,180,256]{2,1,0:T(8,128)(2,1)S(1)} %get-tuple-element.26), channel_id=1, source_target_pairs={{0,1},{1,2},{2,3},{4,5},{5,6},{6,7},{8,9},{9,10},{10,11},{12,13},{... | collective-permute-start | bytes 276488 | tf_op jit(solution)/shard_map/ppermute | solution.py:28
  14.9 2.1 %collective-permute-start.1 = (bf16[1,180,256]{2,1,0:T(8,128)(2,1)S(1)}, bf16[1,180,256]{2,1,0:T(8,128)(2,1)S(1)}, u32[]{:S(2)}, u32[]{:S(2)}) collective-permute-start(bf16[1,180,256]{2,1,0:T(8,128)(2,1)S(1)} %get-tuple-element.25), channel_id=1, source_target_pairs={{1,0},{2,1},{3,2},{5,4},{6,5},{7,6},{9,8},{10,9},{11,10},{13,12},{... | collective-permute-start | bytes 276488 | tf_op jit(solution)/shard_map/ppermute | solution.py:29
  17.0 6.6 %fusion.8 = bf16[512,720]{0,1:T(8,128)(2,1)} fusion(s32[512]{0:T(512)S(1)} %fusion.42, s32[512]{0:T(512)S(1)} %fusion.35), kind=kLoop, calls=%fused_computation.16 | loop fusion | flops 4055040 | bytes 741376 | tf_op jit(solution)/shard_map/convert_element_type | solution.py:234
  23.6 4.8 %all-to-all-done = bf16[4,180,4,256]{3,2,1,0:T(4,128)(2,1)} async-done(((bf16[4,180,4,256]{3,2,1,0:T(4,128)(2,1)}), bf16[4,180,4,256]{3,2,1,0:T(4,128)(2,1)}, u32[]{:S(2)}, u32[]{:S(2)}) %all-to-all-start) | async-done | bytes 1474592 | tf_op jit(solution)/shard_map/all_to_all | solution.py:227
  28.4 1.6 %copy.77 = bf16[720,4,256]{2,0,1:T(8,128)(2,1)S(1)} copy(bf16[720,4,256]{2,1,0:T(4,128)(2,1)} %bitcast.4) | data formatting | bytes 2949120 | tf_op jit(solution)/shard_map/reshape | solution.py:228
  31.1 1.8 %copy.63 = bf16[512,4,256]{2,1,0:T(4,128)(2,1)} copy(bf16[512,4,256]{2,0,1:T(8,128)(2,1)S(1)} %convolution_convert_fusion.1) | data formatting | bytes 2097152 | tf_op jit(solution)/shard_map/convert_element_type | solution.py:258
  32.9 6.6 %all-to-all-start.1 = ((bf16[512,4,256]{2,1,0:T(4,128)(2,1)}), bf16[512,4,256]{2,1,0:T(4,128)(2,1)S(1)}, u32[]{:S(2)}, u32[]{:S(2)}) async-start(bf16[512,4,256]{2,1,0:T(4,128)(2,1)} %copy.63), calls=%async_computation.1 | async-start | bytes 2097152 | tf_op jit(solution)/shard_map/all_to_all | solution.py:259
  39.9 2.7 %legendre.1 = f32[256,16,64]{2,1,0:T(8,128)S(1)} custom-call(f32[16,64]{1,0:T(8,128)S(1)} %broadcast_in_dim.30.orders_ref, f32[16,64]{1,0:T(8,128)S(1)} %broadcast_in_dim.31.cosine_ref, f32[16,64]{1,0:T(8,128)S(1)} %add_exponential_fusion.diagonal_ref), custom_call_target="tpu_custom_call" | custom-call | flops 10485760 | bytes 2097152 | tf_op jit(solution)/shard_map/legendre/pallas_call | solution.py:92
  43.4 1.7 %fusion.13 = (bf16[256,16,64,1]{2,1,0,3:T(8,128)(2,1)}, bf16[256,16,64,1]{2,1,0,3:T(8,128)(2,1)}) fusion(f32[256,16,64]{2,1,0:T(8,128)S(1)} %legendre.1, f32[16]{0:T(128)S(1)} %get-tuple-element.29, f32[64]{0:T(128)S(1)} %broadcast_multiply_fusion), kind=kLoop, calls=%fused_computation.24 | loop fusion | flops 1048576 | bytes 2097472 | tf_op jit(solution)/shard_map/convert_element_type | solution.py:242
  45.3 3.1 %collective-permute-done.3 = bf16[18,8,256]{2,1,0:T(8,128)(2,1)S(1)} collective-permute-done((bf16[18,8,256]{2,1,0:T(8,128)(2,1)S(1)}, bf16[18,8,256]{2,1,0:T(8,128)(2,1)S(1)}, u32[]{:S(2)}, u32[]{:S(2)}) %collective-permute-start.3) | collective-permute-done | bytes 73760 | tf_op jit(solution)/shard_map/ppermute | solution.py:29
  48.3 14.0 %all-to-all-done.1 = bf16[512,4,256]{2,1,0:T(4,128)(2,1)S(1)} async-done(((bf16[512,4,256]{2,1,0:T(4,128)(2,1)}), bf16[512,4,256]{2,1,0:T(4,128)(2,1)S(1)}, u32[]{:S(2)}, u32[]{:S(2)}) %all-to-all-start.1) | async-done | bytes 1048608 | tf_op jit(solution)/shard_map/all_to_all | solution.py:259
  64.1 6.1 %fusion.12 = bf16[64,2,16,256]{3,0,1,2:T(8,128)(2,1)} fusion(f32[256,256]{1,0:T(8,128)S(1)} %bitcast.62, bf16[256,16,64,1]{2,1,0,3:T(8,128)(2,1)} %get-tuple-element.22, bf16[256,16,64,1]{2,1,0,3:T(8,128)(2,1)S(1)} %copy-done.6, bf16[16,64,2,256]{3,0,2,1:T(8,128)(2,1)} %bitcast.60), kind=kOutput, calls=%fused_computation.22 | convolution fusion | flops 541589504 | bytes 3407872 | tf_op jit(solution)/shard_map/lmj,mlrc->mjrc/dot_general | solution.py:271
  70.2 2.8 %copy.72 = bf16[64,2,16,256]{3,2,1,0:T(8,128)(2,1)} copy(bf16[64,2,16,256]{3,0,1,2:T(8,128)(2,1)} %fusion.12) | data formatting | bytes 2097152 | tf_op jit(solution)/shard_map/convert_element_type | solution.py:273
  73.0 6.9 %all-to-all-start.2 = ((bf16[64,32,256]{2,1,0:T(8,128)(2,1)}), bf16[64,32,256]{2,1,0:T(8,128)(2,1)S(1)}, u32[]{:S(2)}, u32[]{:S(2)}) async-start(bf16[64,32,256]{2,1,0:T(8,128)(2,1)} %bitcast.58), calls=%async_computation.2 | async-start | bytes 2097152 | tf_op jit(solution)/shard_map/all_to_all | solution.py:275
  80.1 22.7 %all-to-all-done.2 = bf16[64,32,256]{2,1,0:T(8,128)(2,1)S(1)} async-done(((bf16[64,32,256]{2,1,0:T(8,128)(2,1)}), bf16[64,32,256]{2,1,0:T(8,128)(2,1)S(1)}, u32[]{:S(2)}, u32[]{:S(2)}) %all-to-all-start.2) | async-done | bytes 1048608 | tf_op jit(solution)/shard_map/all_to_all | solution.py:275
  102.9 2.0 %convolution_convert_fusion = bf16[720,4,256]{2,0,1:T(8,128)(2,1)S(1)} fusion(bf16[4,512,256]{2,1,0:T(8,128)(2,1)S(1)} %bitcast.61, bf16[512,720]{0,1:T(8,128)(2,1)} %fusion.8), kind=kOutput, calls=%fused_computation.9 | convolution fusion | flops 755712000 | bytes 3260416 | tf_op jit(solution)/shard_map/mp,imc->pic/dot_general | solution.py:276
  105.0 1.9 %copy.74 = bf16[720,4,256]{2,1,0:T(4,128)(2,1)} copy(bf16[720,4,256]{2,0,1:T(8,128)(2,1)S(1)} %convolution_convert_fusion) | data formatting | bytes 2949120 | tf_op jit(solution)/shard_map/convert_element_type | solution.py:278
  106.8 7.1 %all-to-all-start.3 = ((bf16[4,180,4,256]{3,2,1,0:T(4,128)(2,1)}), bf16[4,180,4,256]{3,2,1,0:T(4,128)(2,1)}, u32[]{:S(2)}, u32[]{:S(2)}) async-start(bf16[4,180,4,256]{3,2,1,0:T(4,128)(2,1)} %bitcast.21), calls=%async_computation.3 | async-start | bytes 2949120 | tf_op jit(solution)/shard_map/all_to_all | solution.py:280
  115.6 15.4 %disco.1 = f32[16,180,256]{2,1,0:T(8,128)S(1)} custom-call(bf16[18,208,256]{2,1,0:T(8,128)(2,1)S(1)} %maximum_maximum_fusion.above_ref.here_ref.below_ref, bf16[18,208,256]{2,1,0:T(8,128)(2,1)S(1)} %maximum_maximum_fusion.above_ref.here_ref.below_ref, bf16[18,208,256]{2,1,0:T(8,128)(2,1)S(1)} %maximum_maximum_fusion.above_ref.here_ref.below_ref, ...), custom_call_target="tpu_custom_call" | custom-call | flops 6039797760 | bytes 12582912 | tf_op jit(solution)/shard_map/disco/pallas_call | solution.py:133
  131.0 2.5 %copy.93 = f32[16,180,256]{2,0,1:T(8,128)} copy(f32[16,180,256]{2,1,0:T(8,128)S(1)} %disco.1) | data formatting | bytes 5898240 | tf_op jit(solution)/shard_map/disco/pallas_call | solution.py:133
  133.5 7.8 %mlp.1 = f32[180,16,256]{2,1,0:T(8,128)} custom-call(f32[180,16,256]{2,1,0:T(8,128)S(1)} %bitcast.49, f32[180,16,256]{2,1,0:T(8,128)} %bitcast.56, bf16[4,180,4,256]{3,2,1,0:T(4,128)(2,1)} %all-to-all-done.3.spectral_ref, f32[1,256]{1,0:T(1,128)S(1)} %get-tuple-element.27.gain_ref, bf16[256,512]{1,0:T(8,128)(2,1)S(1)} %bitcast.50, bf16[512,256]{1,0:T(8,128)(2,1)S(1)} %bitcast.51), custom_call_target="tpu_custom_call" | custom-call | tf_op jit(solution)/shard_map/mlp/pallas_call | solution.py:193
  (56 shorter events, 9.0 us)
Async XLA Ops:
  0.0 114.0 %copy-start = (f32[1,16,24,8]{2,3,1,0:T(8,128)S(1)}, f32[1,16,24,8]{2,3,1,0:T(8,128)}, u32[]{:S(2)}) copy-start(f32[1,16,24,8]{2,3,1,0:T(8,128)} %param.11) | copy-start | bytes 36868
  0.8 1.8 %copy-start.1 = (f32[16,180,256]{2,0,1:T(8,128)S(1)}, f32[16,180,256]{2,0,1:T(8,128)}, u32[]{:S(2)}) copy-start(f32[16,180,256]{2,0,1:T(8,128)} %param.9) | copy-start | bytes 8847364
  6.1 22.4 %all-to-all-start = ((bf16[4,180,4,256]{3,2,1,0:T(4,128)(2,1)}), bf16[4,180,4,256]{3,2,1,0:T(4,128)(2,1)}, u32[]{:S(2)}, u32[]{:S(2)}) async-start(bf16[4,180,4,256]{3,2,1,0:T(4,128)(2,1)} %bitcast.47), calls=%async_computation | async-start | bytes 2949120 | tf_op jit(solution)/shard_map/all_to_all | solution.py:227
  11.7 18.4 %collective-permute-start = (bf16[1,180,256]{2,1,0:T(8,128)(2,1)S(1)}, bf16[1,180,256]{2,1,0:T(8,128)(2,1)S(1)}, u32[]{:S(2)}, u32[]{:S(2)}) collective-permute-start(bf16[1,180,256]{2,1,0:T(8,128)(2,1)S(1)} %get-tuple-element.26), channel_id=1, source_target_pairs={{0,1},{1,2},{2,3},{4,5},{5,6},{6,7},{8,9},{9,10},{10,11},{12,13},{... | collective-permute-start | bytes 276488 | tf_op jit(solution)/shard_map/ppermute | solution.py:28
  14.9 15.2 %collective-permute-start.1 = (bf16[1,180,256]{2,1,0:T(8,128)(2,1)S(1)}, bf16[1,180,256]{2,1,0:T(8,128)(2,1)S(1)}, u32[]{:S(2)}, u32[]{:S(2)}) collective-permute-start(bf16[1,180,256]{2,1,0:T(8,128)(2,1)S(1)} %get-tuple-element.25), channel_id=1, source_target_pairs={{1,0},{2,1},{3,2},{5,4},{6,5},{7,6},{9,8},{10,9},{11,10},{13,12},{... | collective-permute-start | bytes 276488 | tf_op jit(solution)/shard_map/ppermute | solution.py:29
  28.4 1.7 %copy-start.7 = (bf16[512,720]{0,1:T(8,128)(2,1)S(1)}, bf16[512,720]{0,1:T(8,128)(2,1)}, u32[]{:S(2)}) copy-start(bf16[512,720]{0,1:T(8,128)(2,1)} %fusion.8) | copy-start | bytes 2211844
  32.9 29.5 %all-to-all-start.1 = ((bf16[512,4,256]{2,1,0:T(4,128)(2,1)}), bf16[512,4,256]{2,1,0:T(4,128)(2,1)S(1)}, u32[]{:S(2)}, u32[]{:S(2)}) async-start(bf16[512,4,256]{2,1,0:T(4,128)(2,1)} %copy.63), calls=%async_computation.1 | async-start | bytes 2097152 | tf_op jit(solution)/shard_map/all_to_all | solution.py:259
  42.8 2.5 %collective-permute-start.2 = (bf16[18,8,256]{2,1,0:T(8,128)(2,1)S(1)}, bf16[18,8,256]{2,1,0:T(8,128)(2,1)S(1)}, u32[]{:S(2)}, u32[]{:S(2)}) collective-permute-start(bf16[18,8,256]{2,1,0:T(8,128)(2,1)S(1)} %get-tuple-element.24), channel_id=1, source_target_pairs={{0,4},{4,8},{8,12},{12,0},{1,5},{5,9},{9,13},{13,1},{2,6},{6,10},{... | collective-permute-start | bytes 221192 | tf_op jit(solution)/shard_map/ppermute | solution.py:28
  43.4 5.0 %collective-permute-start.3 = (bf16[18,8,256]{2,1,0:T(8,128)(2,1)S(1)}, bf16[18,8,256]{2,1,0:T(8,128)(2,1)S(1)}, u32[]{:S(2)}, u32[]{:S(2)}) collective-permute-start(bf16[18,8,256]{2,1,0:T(8,128)(2,1)S(1)} %get-tuple-element.23), channel_id=1, source_target_pairs={{4,0},{8,4},{12,8},{0,12},{5,1},{9,5},{13,9},{1,13},{6,2},{10,6},{... | collective-permute-start | bytes 221192 | tf_op jit(solution)/shard_map/ppermute | solution.py:29
  45.0 18.5 %copy-start.10 = (f32[1,256,256]{2,1,0:T(8,128)S(1)}, f32[1,256,256]{2,1,0:T(8,128)}, u32[]{:S(2)}) copy-start(f32[1,256,256]{2,1,0:T(8,128)} %param.15) | copy-start | bytes 786436
  62.5 1.6 %copy-start.6 = (bf16[256,16,64,1]{2,1,0,3:T(8,128)(2,1)S(1)}, bf16[256,16,64,1]{2,1,0,3:T(8,128)(2,1)}, u32[]{:S(2)}) copy-start(bf16[256,16,64,1]{2,1,0,3:T(8,128)(2,1)} %get-tuple-element.21) | copy-start | bytes 1572868
  70.2 9.9 %copy-start.9 = (s32[16]{0:T(128)S(1)}, s32[16]{0:T(128)}, u32[]{:S(2)}) copy-start(s32[16]{0:T(128)} %param.13) | copy-start | bytes 196
  70.2 9.9 %copy-start.8 = (s32[16,24]{1,0:T(8,128)S(1)}, s32[16,24]{1,0:T(8,128)}, u32[]{:S(2)}) copy-start(s32[16,24]{1,0:T(8,128)} %param.12) | copy-start | bytes 4612
  73.0 29.8 %all-to-all-start.2 = ((bf16[64,32,256]{2,1,0:T(8,128)(2,1)}), bf16[64,32,256]{2,1,0:T(8,128)(2,1)S(1)}, u32[]{:S(2)}, u32[]{:S(2)}) async-start(bf16[64,32,256]{2,1,0:T(8,128)(2,1)} %bitcast.58), calls=%async_computation.2 | async-start | bytes 2097152 | tf_op jit(solution)/shard_map/all_to_all | solution.py:275
  106.8 26.6 %all-to-all-start.3 = ((bf16[4,180,4,256]{3,2,1,0:T(4,128)(2,1)}), bf16[4,180,4,256]{3,2,1,0:T(4,128)(2,1)}, u32[]{:S(2)}, u32[]{:S(2)}) async-start(bf16[4,180,4,256]{3,2,1,0:T(4,128)(2,1)} %bitcast.21), calls=%async_computation.3 | async-start | bytes 2949120 | tf_op jit(solution)/shard_map/all_to_all | solution.py:280
  114.3 1.2 copy-start.5
  130.9 2.5 %copy-start.2 = (f32[16,180,256]{2,0,1:T(8,128)S(1)}, f32[16,180,256]{2,0,1:T(8,128)}, u32[]{:S(2)}) copy-start(f32[16,180,256]{2,0,1:T(8,128)} %param.9) | copy-start | bytes 8847364
  130.9 2.5 %copy-start.3 = (bf16[1,256,512]{2,1,0:T(8,128)(2,1)S(1)}, bf16[1,256,512]{2,1,0:T(8,128)(2,1)}, u32[]{:S(2)}) copy-start(bf16[1,256,512]{2,1,0:T(8,128)(2,1)} %param.16) | copy-start | bytes 786436
  131.0 2.5 %copy-start.4 = (bf16[1,512,256]{2,1,0:T(8,128)(2,1)S(1)}, bf16[1,512,256]{2,1,0:T(8,128)(2,1)}, u32[]{:S(2)}) copy-start(bf16[1,512,256]{2,1,0:T(8,128)(2,1)} %param.17) | copy-start | bytes 786436

commit v6 on v5

--- a/solution.py
+++ b/solution.py
@@ -238,8 +238,8 @@
     factor = jnp.where(own_modes == 0, 1.0, 2.0).astype(jnp.float32)
     legendre = legendre_table(own_modes, lat_total, L)
     weights = math.pi * jnp.sin(colatitudes(lat_total)) / (lat_total * lon_total)
-    weighted = (legendre * weights[None, None, :]).astype(jnp.bfloat16)
-    legendre = (legendre * factor[None, :, None]).astype(jnp.bfloat16)
+    weighted = (legendre * (factor[:, None] * weights[None, :])[None]).astype(jnp.bfloat16)
+    legendre = legendre.astype(jnp.bfloat16)
 
     live = jnp.arange(S, dtype=jnp.int32)[None, :] < counts[:, None]
     lanes = taps // tap_span * REACH + taps % tap_span
@@ -263,9 +263,9 @@
     )
     disco = jnp.transpose(disco_update(extended, base, disco_mix[0], lon_cols), (1, 0, 2))
     owned = owned.reshape(parts, 2, modes_own, share, channels)
-    owned = jnp.transpose(owned, (2, 0, 3, 1, 4)).reshape(modes_own, lat_total, 2, channels)
+    owned = jnp.transpose(owned, (0, 3, 1, 2, 4)).reshape(lat_total, 2, modes_own, channels)
     coefficient = jnp.einsum(
-        "lmj,mjrc->mlrc", weighted, owned, preferred_element_type=jnp.float32
+        "lmj,jrmc->mlrc", weighted, owned, preferred_element_type=jnp.float32
     )
     scaled = (coefficient * filter_gain[0][None, :, None, :]).astype(jnp.bfloat16)
     filtered = jnp.einsum(

time: 142 us -> 141 us (level)
  local copies, waits for them, and re-layouts: 18.1 us -> 16.6 us
    unnamed x22 -> x20, local copies, waits for them, and re-layouts: 2.85 us -> 2.32 us
  transfers between devices with their start and end apart: 8 -> 8, of which waited for: 5 -> 5; matrix products, arithmetic and copies ran while one was open for 10% -> 11% of each run, Pallas kernels for 13% -> 13%
where the time goes in v6:
time: 141 us; the launch traced here: 140 us
  waiting for transfers between devices  44.8 us (32%)
  starting transfers between devices  31.7 us (22%)
  Pallas kernels  27.3 us (19%)
  local copies, waits for them, and re-layouts  16.6 us (12%)
  other arithmetic  9.62 us (7%)
  matrix products  9.48 us (7%)
    all_to_all x1, waiting for transfers between devices, local(): lax.all_to_all(filtered, ('lat', 'lon'), split_axis=0, concat_axis=1, til...  22.7 us
    pallas_call x1, Pallas kernels, disco_update(): pl.pallas_call(disco_body, grid=(rows,), in_specs=[ext_spec(0), ext_spec(...  15.4 us
    all_to_all x1, waiting for transfers between devices, local(): lax.all_to_all(spectrum, ('lat', 'lon'), split_axis=0, concat_axis=0, til...  14 us
    pallas_call x1, Pallas kernels, mlp_update(): pl.pallas_call(mlp_body, grid=(cols // step,), in_specs=[cell, cell] + [p...  7.81 us
    all_to_all x1, starting transfers between devices, local(): lax.all_to_all(restored, 'lon', split_axis=0, concat_axis=0, tiled=True)  7.15 us
    all_to_all x1, starting transfers between devices, local(): lax.all_to_all(filtered, ('lat', 'lon'), split_axis=0, concat_axis=1, til...  6.94 us
    convert_element_type x1, other arithmetic, local(): jnp.cos(steps.astype(jnp.float32) * (2.0 * math.pi / lon_total))  6.61 us
    all_to_all x1, starting transfers between devices, local(): lax.all_to_all(spectrum, ('lat', 'lon'), split_axis=0, concat_axis=0, til...  6.58 us
  transfers between devices with their start and end apart: 8, of which 5 were waited for; matrix products, arithmetic and copies ran while one was open for 11% of the time, Pallas kernels for 13%

profile of v6, /device:TPU:19, one launch (start us, length us, event | category | flops | bytes accessed | tf_op | source)
XLA Modules:
  0.0 139.8 jit_solution(754210480417169158)
XLA Ops:
  0.8 1.8 %copy-done.1 = f32[16,180,256]{2,0,1:T(8,128)S(1)} copy-done((f32[16,180,256]{2,0,1:T(8,128)S(1)}, f32[16,180,256]{2,0,1:T(8,128)}, u32[]{:S(2)}) %copy-start.1) | copy-done | bytes 2949144
  4.4 1.6 %copy.93 = bf16[180,4,4,256]{3,2,0,1:T(4,128)(2,1)} copy(bf16[180,4,4,256]{3,2,1,0:T(4,128)(2,1)S(1)} %reshape.152) | data formatting | bytes 2949120 | tf_op jit(solution)/shard_map/reshape | solution.py:226
  6.1 5.1 %all-to-all-start = ((bf16[4,180,4,256]{3,2,1,0:T(4,128)(2,1)}), bf16[4,180,4,256]{3,2,1,0:T(4,128)(2,1)}, u32[]{:S(2)}, u32[]{:S(2)}) async-start(bf16[4,180,4,256]{3,2,1,0:T(4,128)(2,1)} %bitcast.47), calls=%async_computation | async-start | bytes 2949120 | tf_op jit(solution)/shard_map/all_to_all | solution.py:227
  11.7 3.2 %collective-permute-start = (bf16[1,180,256]{2,1,0:T(8,128)(2,1)S(1)}, bf16[1,180,256]{2,1,0:T(8,128)(2,1)S(1)}, u32[]{:S(2)}, u32[]{:S(2)}) collective-permute-start(bf16[1,180,256]{2,1,0:T(8,128)(2,1)S(1)} %get-tuple-element.26), channel_id=1, source_target_pairs={{0,1},{1,2},{2,3},{4,5},{5,6},{6,7},{8,9},{9,10},{10,11},{12,13},{... | collective-permute-start | bytes 276488 | tf_op jit(solution)/shard_map/ppermute | solution.py:28
  14.9 2.1 %collective-permute-start.1 = (bf16[1,180,256]{2,1,0:T(8,128)(2,1)S(1)}, bf16[1,180,256]{2,1,0:T(8,128)(2,1)S(1)}, u32[]{:S(2)}, u32[]{:S(2)}) collective-permute-start(bf16[1,180,256]{2,1,0:T(8,128)(2,1)S(1)} %get-tuple-element.25), channel_id=1, source_target_pairs={{1,0},{2,1},{3,2},{5,4},{6,5},{7,6},{9,8},{10,9},{11,10},{13,12},{... | collective-permute-start | bytes 276488 | tf_op jit(solution)/shard_map/ppermute | solution.py:29
  17.0 6.6 %fusion.8 = bf16[512,720]{0,1:T(8,128)(2,1)} fusion(s32[512]{0:T(512)S(1)} %fusion.41, s32[512]{0:T(512)S(1)} %fusion.34), kind=kLoop, calls=%fused_computation.15 | loop fusion | flops 4055040 | bytes 741376 | tf_op jit(solution)/shard_map/convert_element_type | solution.py:234
  23.6 4.8 %all-to-all-done = bf16[4,180,4,256]{3,2,1,0:T(4,128)(2,1)} async-done(((bf16[4,180,4,256]{3,2,1,0:T(4,128)(2,1)}), bf16[4,180,4,256]{3,2,1,0:T(4,128)(2,1)}, u32[]{:S(2)}, u32[]{:S(2)}) %all-to-all-start) | async-done | bytes 1474592 | tf_op jit(solution)/shard_map/all_to_all | solution.py:227
  28.4 1.6 %copy.75 = bf16[720,4,256]{2,0,1:T(8,128)(2,1)S(1)} copy(bf16[720,4,256]{2,1,0:T(4,128)(2,1)} %bitcast.4) | data formatting | bytes 2949120 | tf_op jit(solution)/shard_map/reshape | solution.py:228
  31.1 1.8 %copy.63 = bf16[512,4,256]{2,1,0:T(4,128)(2,1)} copy(bf16[512,4,256]{2,0,1:T(8,128)(2,1)S(1)} %convolution_convert_fusion.1) | data formatting | bytes 2097152 | tf_op jit(solution)/shard_map/convert_element_type | solution.py:258
  32.9 6.6 %all-to-all-start.1 = ((bf16[512,4,256]{2,1,0:T(4,128)(2,1)}), bf16[512,4,256]{2,1,0:T(4,128)(2,1)S(1)}, u32[]{:S(2)}, u32[]{:S(2)}) async-start(bf16[512,4,256]{2,1,0:T(4,128)(2,1)} %copy.63), calls=%async_computation.1 | async-start | bytes 2097152 | tf_op jit(solution)/shard_map/all_to_all | solution.py:259
  39.9 2.7 %legendre.1 = f32[256,16,64]{2,1,0:T(8,128)S(1)} custom-call(f32[16,64]{1,0:T(8,128)S(1)} %broadcast_in_dim.30.orders_ref, f32[16,64]{1,0:T(8,128)S(1)} %broadcast_in_dim.31.cosine_ref, f32[16,64]{1,0:T(8,128)S(1)} %add_exponential_fusion.diagonal_ref), custom_call_target="tpu_custom_call" | custom-call | flops 10485760 | bytes 2097152 | tf_op jit(solution)/shard_map/legendre/pallas_call | solution.py:92
  43.4 1.6 %convert_bitcast_fusion = (bf16[256,16,64,1]{2,1,0,3:T(8,128)(2,1)}, bf16[256,16,64,1]{2,1,0,3:T(8,128)(2,1)}) fusion(f32[256,16,64]{2,1,0:T(8,128)S(1)} %legendre.1, f32[16,64]{1,0:T(8,128)S(1)} %broadcast_multiply_fusion), kind=kLoop, calls=%fused_computation.27 | loop fusion | flops 786432 | bytes 2101248 | tf_op jit(solution)/shard_map/convert_element_type | solution.py:242
  45.3 3.1 %collective-permute-done.3 = bf16[18,8,256]{2,1,0:T(8,128)(2,1)S(1)} collective-permute-done((bf16[18,8,256]{2,1,0:T(8,128)(2,1)S(1)}, bf16[18,8,256]{2,1,0:T(8,128)(2,1)S(1)}, u32[]{:S(2)}, u32[]{:S(2)}) %collective-permute-start.3) | collective-permute-done | bytes 73760 | tf_op jit(solution)/shard_map/ppermute | solution.py:29
  48.3 14.0 %all-to-all-done.1 = bf16[512,4,256]{2,1,0:T(4,128)(2,1)S(1)} async-done(((bf16[512,4,256]{2,1,0:T(4,128)(2,1)}), bf16[512,4,256]{2,1,0:T(4,128)(2,1)S(1)}, u32[]{:S(2)}, u32[]{:S(2)}) %all-to-all-start.1) | async-done | bytes 1048608 | tf_op jit(solution)/shard_map/all_to_all | solution.py:259
  62.6 6.1 %fusion.12 = bf16[64,2,16,256]{3,0,1,2:T(8,128)(2,1)} fusion(f32[256,256]{1,0:T(8,128)S(1)} %bitcast.62, bf16[256,16,64,1]{2,1,0,3:T(8,128)(2,1)} %get-tuple-element.22, bf16[256,16,64,1]{2,1,0,3:T(8,128)(2,1)} %get-tuple-element.21, bf16[64,2,16,256]{3,2,1,0:T(8,128)(2,1)S(1)} %bitcast.60), kind=kOutput, calls=%fused_computation.21 | convolution fusion | flops 541589504 | bytes 3407872 | tf_op jit(solution)/shard_map/lmj,mlrc->mjrc/dot_general | solution.py:271
  68.7 2.8 %copy.70 = bf16[64,2,16,256]{3,2,1,0:T(8,128)(2,1)} copy(bf16[64,2,16,256]{3,0,1,2:T(8,128)(2,1)} %fusion.12) | data formatting | bytes 2097152 | tf_op jit(solution)/shard_map/convert_element_type | solution.py:273
  71.5 6.9 %all-to-all-start.2 = ((bf16[64,32,256]{2,1,0:T(8,128)(2,1)}), bf16[64,32,256]{2,1,0:T(8,128)(2,1)S(1)}, u32[]{:S(2)}, u32[]{:S(2)}) async-start(bf16[64,32,256]{2,1,0:T(8,128)(2,1)} %bitcast.58), calls=%async_computation.2 | async-start | bytes 2097152 | tf_op jit(solution)/shard_map/all_to_all | solution.py:275
  78.6 22.7 %all-to-all-done.2 = bf16[64,32,256]{2,1,0:T(8,128)(2,1)S(1)} async-done(((bf16[64,32,256]{2,1,0:T(8,128)(2,1)}), bf16[64,32,256]{2,1,0:T(8,128)(2,1)S(1)}, u32[]{:S(2)}, u32[]{:S(2)}) %all-to-all-start.2) | async-done | bytes 1048608 | tf_op jit(solution)/shard_map/all_to_all | solution.py:275
  101.4 2.0 %convolution_convert_fusion = bf16[720,4,256]{2,0,1:T(8,128)(2,1)S(1)} fusion(bf16[4,512,256]{2,1,0:T(8,128)(2,1)S(1)} %bitcast.61, bf16[512,720]{0,1:T(8,128)(2,1)} %fusion.8), kind=kOutput, calls=%fused_computation.8 | convolution fusion | flops 755712000 | bytes 3260416 | tf_op jit(solution)/shard_map/mp,imc->pic/dot_general | solution.py:276
  103.4 1.9 %copy.72 = bf16[720,4,256]{2,1,0:T(4,128)(2,1)} copy(bf16[720,4,256]{2,0,1:T(8,128)(2,1)S(1)} %convolution_convert_fusion) | data formatting | bytes 2949120 | tf_op jit(solution)/shard_map/convert_element_type | solution.py:278
  105.3 7.2 %all-to-all-start.3 = ((bf16[4,180,4,256]{3,2,1,0:T(4,128)(2,1)}), bf16[4,180,4,256]{3,2,1,0:T(4,128)(2,1)}, u32[]{:S(2)}, u32[]{:S(2)}) async-start(bf16[4,180,4,256]{3,2,1,0:T(4,128)(2,1)} %bitcast.21), calls=%async_computation.3 | async-start | bytes 2949120 | tf_op jit(solution)/shard_map/all_to_all | solution.py:280
  114.0 15.4 %disco.1 = f32[16,180,256]{2,1,0:T(8,128)S(1)} custom-call(bf16[18,208,256]{2,1,0:T(8,128)(2,1)S(1)} %maximum_maximum_fusion.above_ref.here_ref.below_ref, bf16[18,208,256]{2,1,0:T(8,128)(2,1)S(1)} %maximum_maximum_fusion.above_ref.here_ref.below_ref, bf16[18,208,256]{2,1,0:T(8,128)(2,1)S(1)} %maximum_maximum_fusion.above_ref.here_ref.below_ref, ...), custom_call_target="tpu_custom_call" | custom-call | flops 6039797760 | bytes 12582912 | tf_op jit(solution)/shard_map/disco/pallas_call | solution.py:133
  129.5 2.5 %copy.91 = f32[16,180,256]{2,0,1:T(8,128)} copy(f32[16,180,256]{2,1,0:T(8,128)S(1)} %disco.1) | data formatting | bytes 5898240 | tf_op jit(solution)/shard_map/disco/pallas_call | solution.py:133
  132.0 7.8 %mlp.1 = f32[180,16,256]{2,1,0:T(8,128)} custom-call(f32[180,16,256]{2,1,0:T(8,128)S(1)} %bitcast.49, f32[180,16,256]{2,1,0:T(8,128)} %bitcast.56, bf16[4,180,4,256]{3,2,1,0:T(4,128)(2,1)} %all-to-all-done.3.spectral_ref, f32[1,256]{1,0:T(1,128)S(1)} %get-tuple-element.27.gain_ref, bf16[256,512]{1,0:T(8,128)(2,1)S(1)} %bitcast.50, bf16[512,256]{1,0:T(8,128)(2,1)S(1)} %bitcast.51), custom_call_target="tpu_custom_call" | custom-call | tf_op jit(solution)/shard_map/mlp/pallas_call | solution.py:193
  (55 shorter events, 7.6 us)
Async XLA Ops:
  0.0 112.5 %copy-start = (f32[1,16,24,8]{2,3,1,0:T(8,128)S(1)}, f32[1,16,24,8]{2,3,1,0:T(8,128)}, u32[]{:S(2)}) copy-start(f32[1,16,24,8]{2,3,1,0:T(8,128)} %param.11) | copy-start | bytes 36868
  0.8 1.8 %copy-start.1 = (f32[16,180,256]{2,0,1:T(8,128)S(1)}, f32[16,180,256]{2,0,1:T(8,128)}, u32[]{:S(2)}) copy-start(f32[16,180,256]{2,0,1:T(8,128)} %param.9) | copy-start | bytes 8847364
  6.1 22.4 %all-to-all-start = ((bf16[4,180,4,256]{3,2,1,0:T(4,128)(2,1)}), bf16[4,180,4,256]{3,2,1,0:T(4,128)(2,1)}, u32[]{:S(2)}, u32[]{:S(2)}) async-start(bf16[4,180,4,256]{3,2,1,0:T(4,128)(2,1)} %bitcast.47), calls=%async_computation | async-start | bytes 2949120 | tf_op jit(solution)/shard_map/all_to_all | solution.py:227
  11.7 18.4 %collective-permute-start = (bf16[1,180,256]{2,1,0:T(8,128)(2,1)S(1)}, bf16[1,180,256]{2,1,0:T(8,128)(2,1)S(1)}, u32[]{:S(2)}, u32[]{:S(2)}) collective-permute-start(bf16[1,180,256]{2,1,0:T(8,128)(2,1)S(1)} %get-tuple-element.26), channel_id=1, source_target_pairs={{0,1},{1,2},{2,3},{4,5},{5,6},{6,7},{8,9},{9,10},{10,11},{12,13},{... | collective-permute-start | bytes 276488 | tf_op jit(solution)/shard_map/ppermute | solution.py:28
  14.9 15.2 %collective-permute-start.1 = (bf16[1,180,256]{2,1,0:T(8,128)(2,1)S(1)}, bf16[1,180,256]{2,1,0:T(8,128)(2,1)S(1)}, u32[]{:S(2)}, u32[]{:S(2)}) collective-permute-start(bf16[1,180,256]{2,1,0:T(8,128)(2,1)S(1)} %get-tuple-element.25), channel_id=1, source_target_pairs={{1,0},{2,1},{3,2},{5,4},{6,5},{7,6},{9,8},{10,9},{11,10},{13,12},{... | collective-permute-start | bytes 276488 | tf_op jit(solution)/shard_map/ppermute | solution.py:29
  28.4 1.7 %copy-start.6 = (bf16[512,720]{0,1:T(8,128)(2,1)S(1)}, bf16[512,720]{0,1:T(8,128)(2,1)}, u32[]{:S(2)}) copy-start(bf16[512,720]{0,1:T(8,128)(2,1)} %fusion.8) | copy-start | bytes 2211844
  32.9 29.5 %all-to-all-start.1 = ((bf16[512,4,256]{2,1,0:T(4,128)(2,1)}), bf16[512,4,256]{2,1,0:T(4,128)(2,1)S(1)}, u32[]{:S(2)}, u32[]{:S(2)}) async-start(bf16[512,4,256]{2,1,0:T(4,128)(2,1)} %copy.63), calls=%async_computation.1 | async-start | bytes 2097152 | tf_op jit(solution)/shard_map/all_to_all | solution.py:259
  42.9 2.4 %collective-permute-start.2 = (bf16[18,8,256]{2,1,0:T(8,128)(2,1)S(1)}, bf16[18,8,256]{2,1,0:T(8,128)(2,1)S(1)}, u32[]{:S(2)}, u32[]{:S(2)}) collective-permute-start(bf16[18,8,256]{2,1,0:T(8,128)(2,1)S(1)} %get-tuple-element.24), channel_id=1, source_target_pairs={{0,4},{4,8},{8,12},{12,0},{1,5},{5,9},{9,13},{13,1},{2,6},{6,10},{... | collective-permute-start | bytes 221192 | tf_op jit(solution)/shard_map/ppermute | solution.py:28
  43.4 4.9 %collective-permute-start.3 = (bf16[18,8,256]{2,1,0:T(8,128)(2,1)S(1)}, bf16[18,8,256]{2,1,0:T(8,128)(2,1)S(1)}, u32[]{:S(2)}, u32[]{:S(2)}) collective-permute-start(bf16[18,8,256]{2,1,0:T(8,128)(2,1)S(1)} %get-tuple-element.23), channel_id=1, source_target_pairs={{4,0},{8,4},{12,8},{0,12},{5,1},{9,5},{13,9},{1,13},{6,2},{10,6},{... | collective-permute-start | bytes 221192 | tf_op jit(solution)/shard_map/ppermute | solution.py:29
  45.0 17.5 %copy-start.9 = (f32[1,256,256]{2,1,0:T(8,128)S(1)}, f32[1,256,256]{2,1,0:T(8,128)}, u32[]{:S(2)}) copy-start(f32[1,256,256]{2,1,0:T(8,128)} %param.15) | copy-start | bytes 786436
  68.7 9.8 %copy-start.8 = (s32[16]{0:T(128)S(1)}, s32[16]{0:T(128)}, u32[]{:S(2)}) copy-start(s32[16]{0:T(128)} %param.13) | copy-start | bytes 196
  68.7 9.9 %copy-start.7 = (s32[16,24]{1,0:T(8,128)S(1)}, s32[16,24]{1,0:T(8,128)}, u32[]{:S(2)}) copy-start(s32[16,24]{1,0:T(8,128)} %param.12) | copy-start | bytes 4612
  71.5 29.8 %all-to-all-start.2 = ((bf16[64,32,256]{2,1,0:T(8,128)(2,1)}), bf16[64,32,256]{2,1,0:T(8,128)(2,1)S(1)}, u32[]{:S(2)}, u32[]{:S(2)}) async-start(bf16[64,32,256]{2,1,0:T(8,128)(2,1)} %bitcast.58), calls=%async_computation.2 | async-start | bytes 2097152 | tf_op jit(solution)/shard_map/all_to_all | solution.py:275
  105.3 26.6 %all-to-all-start.3 = ((bf16[4,180,4,256]{3,2,1,0:T(4,128)(2,1)}), bf16[4,180,4,256]{3,2,1,0:T(4,128)(2,1)}, u32[]{:S(2)}, u32[]{:S(2)}) async-start(bf16[4,180,4,256]{3,2,1,0:T(4,128)(2,1)} %bitcast.21), calls=%async_computation.3 | async-start | bytes 2949120 | tf_op jit(solution)/shard_map/all_to_all | solution.py:280
  112.8 1.2 copy-start.5
  129.4 2.5 %copy-start.2 = (f32[16,180,256]{2,0,1:T(8,128)S(1)}, f32[16,180,256]{2,0,1:T(8,128)}, u32[]{:S(2)}) copy-start(f32[16,180,256]{2,0,1:T(8,128)} %param.9) | copy-start | bytes 8847364
  129.4 2.5 %copy-start.3 = (bf16[1,256,512]{2,1,0:T(8,128)(2,1)S(1)}, bf16[1,256,512]{2,1,0:T(8,128)(2,1)}, u32[]{:S(2)}) copy-start(bf16[1,256,512]{2,1,0:T(8,128)(2,1)} %param.16) | copy-start | bytes 786436
  129.5 2.5 %copy-start.4 = (bf16[1,512,256]{2,1,0:T(8,128)(2,1)S(1)}, bf16[1,512,256]{2,1,0:T(8,128)(2,1)}, u32[]{:S(2)}) copy-start(bf16[1,512,256]{2,1,0:T(8,128)(2,1)} %param.17) | copy-start | bytes 786436

commit v7 on v6

--- a/solution.py
+++ b/solution.py
@@ -15,7 +15,7 @@
 WIDTH = 64
 REACH = WIDTH + 2 * R
 LANES = 256
-STEP = 30
+STEP = 60
 
 exact_prec = lax.Precision.HIGHEST
 

time: 141 us -> 139 us (0.986)
  Pallas kernels: 27.3 us -> 25.7 us
where the time goes in v7:
time: 139 us; the launch traced here: 138 us
  waiting for transfers between devices  44.8 us (32%)
  starting transfers between devices  31.6 us (23%)
  Pallas kernels  25.7 us (18%)
  local copies, waits for them, and re-layouts  16.6 us (12%)
  other arithmetic  9.62 us (7%)
  matrix products  9.49 us (7%)
    all_to_all x1, waiting for transfers between devices, local(): lax.all_to_all(filtered, ('lat', 'lon'), split_axis=0, concat_axis=1, til...  22.7 us
    pallas_call x1, Pallas kernels, disco_update(): pl.pallas_call(disco_body, grid=(rows,), in_specs=[ext_spec(0), ext_spec(...  15.4 us
    all_to_all x1, waiting for transfers between devices, local(): lax.all_to_all(spectrum, ('lat', 'lon'), split_axis=0, concat_axis=0, til...  14 us
    all_to_all x1, starting transfers between devices, local(): lax.all_to_all(restored, 'lon', split_axis=0, concat_axis=0, tiled=True)  7.15 us
    all_to_all x1, starting transfers between devices, local(): lax.all_to_all(filtered, ('lat', 'lon'), split_axis=0, concat_axis=1, til...  6.9 us
    convert_element_type x1, other arithmetic, local(): jnp.cos(steps.astype(jnp.float32) * (2.0 * math.pi / lon_total))  6.61 us
    all_to_all x1, starting transfers between devices, local(): lax.all_to_all(spectrum, ('lat', 'lon'), split_axis=0, concat_axis=0, til...  6.58 us
    pallas_call x1, Pallas kernels, mlp_update(): pl.pallas_call(mlp_body, grid=(cols // step,), in_specs=[cell, cell] + [p...  6.52 us
  transfers between devices with their start and end apart: 8, of which 5 were waited for; matrix products, arithmetic and copies ran while one was open for 11% of the time, Pallas kernels for 13%

profile of v7, /device:TPU:19, one launch (start us, length us, event | category | flops | bytes accessed | tf_op | source)
XLA Modules:
  0.0 138.1 jit_solution(15694066938398584252)
XLA Ops:
  0.8 1.8 %copy-done.1 = f32[16,180,256]{2,0,1:T(8,128)S(1)} copy-done((f32[16,180,256]{2,0,1:T(8,128)S(1)}, f32[16,180,256]{2,0,1:T(8,128)}, u32[]{:S(2)}) %copy-start.1) | copy-done | bytes 2949144
  4.1 1.6 %copy.93 = bf16[180,4,4,256]{3,2,0,1:T(4,128)(2,1)} copy(bf16[180,4,4,256]{3,2,1,0:T(4,128)(2,1)S(1)} %reshape.152) | data formatting | bytes 2949120 | tf_op jit(solution)/shard_map/reshape | solution.py:226
  5.7 5.1 %all-to-all-start = ((bf16[4,180,4,256]{3,2,1,0:T(4,128)(2,1)}), bf16[4,180,4,256]{3,2,1,0:T(4,128)(2,1)}, u32[]{:S(2)}, u32[]{:S(2)}) async-start(bf16[4,180,4,256]{3,2,1,0:T(4,128)(2,1)} %bitcast.47), calls=%async_computation | async-start | bytes 2949120 | tf_op jit(solution)/shard_map/all_to_all | solution.py:227
  11.3 3.2 %collective-permute-start = (bf16[1,180,256]{2,1,0:T(8,128)(2,1)S(1)}, bf16[1,180,256]{2,1,0:T(8,128)(2,1)S(1)}, u32[]{:S(2)}, u32[]{:S(2)}) collective-permute-start(bf16[1,180,256]{2,1,0:T(8,128)(2,1)S(1)} %get-tuple-element.26), channel_id=1, source_target_pairs={{0,1},{1,2},{2,3},{4,5},{5,6},{6,7},{8,9},{9,10},{10,11},{12,13},{... | collective-permute-start | bytes 276488 | tf_op jit(solution)/shard_map/ppermute | solution.py:28
  14.6 2.1 %collective-permute-start.1 = (bf16[1,180,256]{2,1,0:T(8,128)(2,1)S(1)}, bf16[1,180,256]{2,1,0:T(8,128)(2,1)S(1)}, u32[]{:S(2)}, u32[]{:S(2)}) collective-permute-start(bf16[1,180,256]{2,1,0:T(8,128)(2,1)S(1)} %get-tuple-element.25), channel_id=1, source_target_pairs={{1,0},{2,1},{3,2},{5,4},{6,5},{7,6},{9,8},{10,9},{11,10},{13,12},{... | collective-permute-start | bytes 276488 | tf_op jit(solution)/shard_map/ppermute | solution.py:29
  16.7 6.6 %fusion.8 = bf16[512,720]{0,1:T(8,128)(2,1)} fusion(s32[512]{0:T(512)S(1)} %fusion.41, s32[512]{0:T(512)S(1)} %fusion.34), kind=kLoop, calls=%fused_computation.15 | loop fusion | flops 4055040 | bytes 741376 | tf_op jit(solution)/shard_map/convert_element_type | solution.py:234
  23.3 4.8 %all-to-all-done = bf16[4,180,4,256]{3,2,1,0:T(4,128)(2,1)} async-done(((bf16[4,180,4,256]{3,2,1,0:T(4,128)(2,1)}), bf16[4,180,4,256]{3,2,1,0:T(4,128)(2,1)}, u32[]{:S(2)}, u32[]{:S(2)}) %all-to-all-start) | async-done | bytes 1474592 | tf_op jit(solution)/shard_map/all_to_all | solution.py:227
  28.1 1.6 %copy.75 = bf16[720,4,256]{2,0,1:T(8,128)(2,1)S(1)} copy(bf16[720,4,256]{2,1,0:T(4,128)(2,1)} %bitcast.4) | data formatting | bytes 2949120 | tf_op jit(solution)/shard_map/reshape | solution.py:228
  30.7 1.8 %copy.63 = bf16[512,4,256]{2,1,0:T(4,128)(2,1)} copy(bf16[512,4,256]{2,0,1:T(8,128)(2,1)S(1)} %convolution_convert_fusion.1) | data formatting | bytes 2097152 | tf_op jit(solution)/shard_map/convert_element_type | solution.py:258
  32.5 6.6 %all-to-all-start.1 = ((bf16[512,4,256]{2,1,0:T(4,128)(2,1)}), bf16[512,4,256]{2,1,0:T(4,128)(2,1)S(1)}, u32[]{:S(2)}, u32[]{:S(2)}) async-start(bf16[512,4,256]{2,1,0:T(4,128)(2,1)} %copy.63), calls=%async_computation.1 | async-start | bytes 2097152 | tf_op jit(solution)/shard_map/all_to_all | solution.py:259
  39.6 2.7 %legendre.1 = f32[256,16,64]{2,1,0:T(8,128)S(1)} custom-call(f32[16,64]{1,0:T(8,128)S(1)} %broadcast_in_dim.30.orders_ref, f32[16,64]{1,0:T(8,128)S(1)} %broadcast_in_dim.31.cosine_ref, f32[16,64]{1,0:T(8,128)S(1)} %add_exponential_fusion.diagonal_ref), custom_call_target="tpu_custom_call" | custom-call | flops 10485760 | bytes 2097152 | tf_op jit(solution)/shard_map/legendre/pallas_call | solution.py:92
  43.1 1.6 %convert_bitcast_fusion = (bf16[256,16,64,1]{2,1,0,3:T(8,128)(2,1)}, bf16[256,16,64,1]{2,1,0,3:T(8,128)(2,1)}) fusion(f32[256,16,64]{2,1,0:T(8,128)S(1)} %legendre.1, f32[16,64]{1,0:T(8,128)S(1)} %broadcast_multiply_fusion), kind=kLoop, calls=%fused_computation.27 | loop fusion | flops 786432 | bytes 2101248 | tf_op jit(solution)/shard_map/convert_element_type | solution.py:242
  44.9 3.1 %collective-permute-done.3 = bf16[18,8,256]{2,1,0:T(8,128)(2,1)S(1)} collective-permute-done((bf16[18,8,256]{2,1,0:T(8,128)(2,1)S(1)}, bf16[18,8,256]{2,1,0:T(8,128)(2,1)S(1)}, u32[]{:S(2)}, u32[]{:S(2)}) %collective-permute-start.3) | collective-permute-done | bytes 73760 | tf_op jit(solution)/shard_map/ppermute | solution.py:29
  48.0 14.0 %all-to-all-done.1 = bf16[512,4,256]{2,1,0:T(4,128)(2,1)S(1)} async-done(((bf16[512,4,256]{2,1,0:T(4,128)(2,1)}), bf16[512,4,256]{2,1,0:T(4,128)(2,1)S(1)}, u32[]{:S(2)}, u32[]{:S(2)}) %all-to-all-start.1) | async-done | bytes 1048608 | tf_op jit(solution)/shard_map/all_to_all | solution.py:259
  62.2 6.1 %fusion.12 = bf16[64,2,16,256]{3,0,1,2:T(8,128)(2,1)} fusion(f32[256,256]{1,0:T(8,128)S(1)} %bitcast.62, bf16[256,16,64,1]{2,1,0,3:T(8,128)(2,1)} %get-tuple-element.22, bf16[256,16,64,1]{2,1,0,3:T(8,128)(2,1)} %get-tuple-element.21, bf16[64,2,16,256]{3,2,1,0:T(8,128)(2,1)S(1)} %bitcast.60), kind=kOutput, calls=%fused_computation.21 | convolution fusion | flops 541589504 | bytes 3407872 | tf_op jit(solution)/shard_map/lmj,mlrc->mjrc/dot_general | solution.py:271
  68.3 2.8 %copy.70 = bf16[64,2,16,256]{3,2,1,0:T(8,128)(2,1)} copy(bf16[64,2,16,256]{3,0,1,2:T(8,128)(2,1)} %fusion.12) | data formatting | bytes 2097152 | tf_op jit(solution)/shard_map/convert_element_type | solution.py:273
  71.1 6.9 %all-to-all-start.2 = ((bf16[64,32,256]{2,1,0:T(8,128)(2,1)}), bf16[64,32,256]{2,1,0:T(8,128)(2,1)S(1)}, u32[]{:S(2)}, u32[]{:S(2)}) async-start(bf16[64,32,256]{2,1,0:T(8,128)(2,1)} %bitcast.58), calls=%async_computation.2 | async-start | bytes 2097152 | tf_op jit(solution)/shard_map/all_to_all | solution.py:275
  78.2 22.7 %all-to-all-done.2 = bf16[64,32,256]{2,1,0:T(8,128)(2,1)S(1)} async-done(((bf16[64,32,256]{2,1,0:T(8,128)(2,1)}), bf16[64,32,256]{2,1,0:T(8,128)(2,1)S(1)}, u32[]{:S(2)}, u32[]{:S(2)}) %all-to-all-start.2) | async-done | bytes 1048608 | tf_op jit(solution)/shard_map/all_to_all | solution.py:275
  101.0 2.0 %convolution_convert_fusion = bf16[720,4,256]{2,0,1:T(8,128)(2,1)S(1)} fusion(bf16[4,512,256]{2,1,0:T(8,128)(2,1)S(1)} %bitcast.61, bf16[512,720]{0,1:T(8,128)(2,1)} %fusion.8), kind=kOutput, calls=%fused_computation.8 | convolution fusion | flops 755712000 | bytes 3260416 | tf_op jit(solution)/shard_map/mp,imc->pic/dot_general | solution.py:276
  103.1 1.9 %copy.72 = bf16[720,4,256]{2,1,0:T(4,128)(2,1)} copy(bf16[720,4,256]{2,0,1:T(8,128)(2,1)S(1)} %convolution_convert_fusion) | data formatting | bytes 2949120 | tf_op jit(solution)/shard_map/convert_element_type | solution.py:278
  104.9 7.1 %all-to-all-start.3 = ((bf16[4,180,4,256]{3,2,1,0:T(4,128)(2,1)}), bf16[4,180,4,256]{3,2,1,0:T(4,128)(2,1)}, u32[]{:S(2)}, u32[]{:S(2)}) async-start(bf16[4,180,4,256]{3,2,1,0:T(4,128)(2,1)} %bitcast.21), calls=%async_computation.3 | async-start | bytes 2949120 | tf_op jit(solution)/shard_map/all_to_all | solution.py:280
  113.7 15.4 %disco.1 = f32[16,180,256]{2,1,0:T(8,128)S(1)} custom-call(bf16[18,208,256]{2,1,0:T(8,128)(2,1)S(1)} %maximum_maximum_fusion.above_ref.here_ref.below_ref, bf16[18,208,256]{2,1,0:T(8,128)(2,1)S(1)} %maximum_maximum_fusion.above_ref.here_ref.below_ref, bf16[18,208,256]{2,1,0:T(8,128)(2,1)S(1)} %maximum_maximum_fusion.above_ref.here_ref.below_ref, ...), custom_call_target="tpu_custom_call" | custom-call | flops 6039797760 | bytes 12582912 | tf_op jit(solution)/shard_map/disco/pallas_call | solution.py:133
  129.1 2.5 %copy.91 = f32[16,180,256]{2,0,1:T(8,128)} copy(f32[16,180,256]{2,1,0:T(8,128)S(1)} %disco.1) | data formatting | bytes 5898240 | tf_op jit(solution)/shard_map/disco/pallas_call | solution.py:133
  131.6 6.5 %mlp.1 = f32[180,16,256]{2,1,0:T(8,128)} custom-call(f32[180,16,256]{2,1,0:T(8,128)S(1)} %bitcast.49, f32[180,16,256]{2,1,0:T(8,128)} %bitcast.56, bf16[4,180,4,256]{3,2,1,0:T(4,128)(2,1)} %all-to-all-done.3.spectral_ref, f32[1,256]{1,0:T(1,128)S(1)} %get-tuple-element.27.gain_ref, bf16[256,512]{1,0:T(8,128)(2,1)S(1)} %bitcast.50, bf16[512,256]{1,0:T(8,128)(2,1)S(1)} %bitcast.51), custom_call_target="tpu_custom_call" | custom-call | tf_op jit(solution)/shard_map/mlp/pallas_call | solution.py:193
  (55 shorter events, 7.2 us)
Async XLA Ops:
  0.0 112.1 %copy-start = (f32[1,16,24,8]{2,3,1,0:T(8,128)S(1)}, f32[1,16,24,8]{2,3,1,0:T(8,128)}, u32[]{:S(2)}) copy-start(f32[1,16,24,8]{2,3,1,0:T(8,128)} %param.11) | copy-start | bytes 36868
  0.8 1.8 %copy-start.1 = (f32[16,180,256]{2,0,1:T(8,128)S(1)}, f32[16,180,256]{2,0,1:T(8,128)}, u32[]{:S(2)}) copy-start(f32[16,180,256]{2,0,1:T(8,128)} %param.9) | copy-start | bytes 8847364
  5.7 22.4 %all-to-all-start = ((bf16[4,180,4,256]{3,2,1,0:T(4,128)(2,1)}), bf16[4,180,4,256]{3,2,1,0:T(4,128)(2,1)}, u32[]{:S(2)}, u32[]{:S(2)}) async-start(bf16[4,180,4,256]{3,2,1,0:T(4,128)(2,1)} %bitcast.47), calls=%async_computation | async-start | bytes 2949120 | tf_op jit(solution)/shard_map/all_to_all | solution.py:227
  11.3 18.4 %collective-permute-start = (bf16[1,180,256]{2,1,0:T(8,128)(2,1)S(1)}, bf16[1,180,256]{2,1,0:T(8,128)(2,1)S(1)}, u32[]{:S(2)}, u32[]{:S(2)}) collective-permute-start(bf16[1,180,256]{2,1,0:T(8,128)(2,1)S(1)} %get-tuple-element.26), channel_id=1, source_target_pairs={{0,1},{1,2},{2,3},{4,5},{5,6},{6,7},{8,9},{9,10},{10,11},{12,13},{... | collective-permute-start | bytes 276488 | tf_op jit(solution)/shard_map/ppermute | solution.py:28
  14.6 15.2 %collective-permute-start.1 = (bf16[1,180,256]{2,1,0:T(8,128)(2,1)S(1)}, bf16[1,180,256]{2,1,0:T(8,128)(2,1)S(1)}, u32[]{:S(2)}, u32[]{:S(2)}) collective-permute-start(bf16[1,180,256]{2,1,0:T(8,128)(2,1)S(1)} %get-tuple-element.25), channel_id=1, source_target_pairs={{1,0},{2,1},{3,2},{5,4},{6,5},{7,6},{9,8},{10,9},{11,10},{13,12},{... | collective-permute-start | bytes 276488 | tf_op jit(solution)/shard_map/ppermute | solution.py:29
  28.1 1.7 %copy-start.6 = (bf16[512,720]{0,1:T(8,128)(2,1)S(1)}, bf16[512,720]{0,1:T(8,128)(2,1)}, u32[]{:S(2)}) copy-start(bf16[512,720]{0,1:T(8,128)(2,1)} %fusion.8) | copy-start | bytes 2211844
  32.5 29.5 %all-to-all-start.1 = ((bf16[512,4,256]{2,1,0:T(4,128)(2,1)}), bf16[512,4,256]{2,1,0:T(4,128)(2,1)S(1)}, u32[]{:S(2)}, u32[]{:S(2)}) async-start(bf16[512,4,256]{2,1,0:T(4,128)(2,1)} %copy.63), calls=%async_computation.1 | async-start | bytes 2097152 | tf_op jit(solution)/shard_map/all_to_all | solution.py:259
  42.5 2.4 %collective-permute-start.2 = (bf16[18,8,256]{2,1,0:T(8,128)(2,1)S(1)}, bf16[18,8,256]{2,1,0:T(8,128)(2,1)S(1)}, u32[]{:S(2)}, u32[]{:S(2)}) collective-permute-start(bf16[18,8,256]{2,1,0:T(8,128)(2,1)S(1)} %get-tuple-element.24), channel_id=1, source_target_pairs={{0,4},{4,8},{8,12},{12,0},{1,5},{5,9},{9,13},{13,1},{2,6},{6,10},{... | collective-permute-start | bytes 221192 | tf_op jit(solution)/shard_map/ppermute | solution.py:28
  43.1 4.9 %collective-permute-start.3 = (bf16[18,8,256]{2,1,0:T(8,128)(2,1)S(1)}, bf16[18,8,256]{2,1,0:T(8,128)(2,1)S(1)}, u32[]{:S(2)}, u32[]{:S(2)}) collective-permute-start(bf16[18,8,256]{2,1,0:T(8,128)(2,1)S(1)} %get-tuple-element.23), channel_id=1, source_target_pairs={{4,0},{8,4},{12,8},{0,12},{5,1},{9,5},{13,9},{1,13},{6,2},{10,6},{... | collective-permute-start | bytes 221192 | tf_op jit(solution)/shard_map/ppermute | solution.py:29
  44.7 17.5 %copy-start.9 = (f32[1,256,256]{2,1,0:T(8,128)S(1)}, f32[1,256,256]{2,1,0:T(8,128)}, u32[]{:S(2)}) copy-start(f32[1,256,256]{2,1,0:T(8,128)} %param.15) | copy-start | bytes 786436
  68.3 9.8 %copy-start.8 = (s32[16]{0:T(128)S(1)}, s32[16]{0:T(128)}, u32[]{:S(2)}) copy-start(s32[16]{0:T(128)} %param.13) | copy-start | bytes 196
  68.3 9.9 %copy-start.7 = (s32[16,24]{1,0:T(8,128)S(1)}, s32[16,24]{1,0:T(8,128)}, u32[]{:S(2)}) copy-start(s32[16,24]{1,0:T(8,128)} %param.12) | copy-start | bytes 4612
  71.1 29.8 %all-to-all-start.2 = ((bf16[64,32,256]{2,1,0:T(8,128)(2,1)}), bf16[64,32,256]{2,1,0:T(8,128)(2,1)S(1)}, u32[]{:S(2)}, u32[]{:S(2)}) async-start(bf16[64,32,256]{2,1,0:T(8,128)(2,1)} %bitcast.58), calls=%async_computation.2 | async-start | bytes 2097152 | tf_op jit(solution)/shard_map/all_to_all | solution.py:275
  104.9 26.6 %all-to-all-start.3 = ((bf16[4,180,4,256]{3,2,1,0:T(4,128)(2,1)}), bf16[4,180,4,256]{3,2,1,0:T(4,128)(2,1)}, u32[]{:S(2)}, u32[]{:S(2)}) async-start(bf16[4,180,4,256]{3,2,1,0:T(4,128)(2,1)} %bitcast.21), calls=%async_computation.3 | async-start | bytes 2949120 | tf_op jit(solution)/shard_map/all_to_all | solution.py:280
  112.4 1.2 copy-start.5
  129.0 2.5 %copy-start.2 = (f32[16,180,256]{2,0,1:T(8,128)S(1)}, f32[16,180,256]{2,0,1:T(8,128)}, u32[]{:S(2)}) copy-start(f32[16,180,256]{2,0,1:T(8,128)} %param.9) | copy-start | bytes 8847364
  129.0 2.5 %copy-start.3 = (bf16[1,256,512]{2,1,0:T(8,128)(2,1)S(1)}, bf16[1,256,512]{2,1,0:T(8,128)(2,1)}, u32[]{:S(2)}) copy-start(bf16[1,256,512]{2,1,0:T(8,128)(2,1)} %param.16) | copy-start | bytes 786436
  129.1 2.5 %copy-start.4 = (bf16[1,512,256]{2,1,0:T(8,128)(2,1)S(1)}, bf16[1,512,256]{2,1,0:T(8,128)(2,1)}, u32[]{:S(2)}) copy-start(bf16[1,512,256]{2,1,0:T(8,128)(2,1)} %param.17) | copy-start | bytes 786436
